TPU v7x, 32 devices: a whole 2x2x4 slice. The times are simulated.
32 devices in a mesh: groups: 2 (over y), row: 8 (over z, x), col: 2 (over core).
Axes of the slice: x: 2, y: 2, z: 4, core: 2. Of those that a mesh axis runs over, the one named last changes fastest.
Arguments:
- points: bfloat16 [64, 6144], P(None, ('groups', 'row', 'col')), parts along dimension 1, may hold values from -8.5 to 8.5
- direction: float32 [32, 6144], P(None, ('groups', 'row', 'col')), parts along dimension 1, may hold values from -80 to 80
- residual: float32 [32, 6144], P(None, ('groups', 'row', 'col')), parts along dimension 1, may hold values from -80 to 80
- solution: float32 [32, 6144], P(None, ('groups', 'row', 'col')), parts along dimension 1, may hold values from -6 to 6
Outputs:
- solution_next: float32 [32, 6144], P(None, ('groups', 'row', 'col')), parts along dimension 1
- residual_next: float32 [32, 6144], P(None, ('groups', 'row', 'col')), parts along dimension 1
- direction_next: float32 [32, 6144], P(None, ('groups', 'row', 'col')), parts along dimension 1
There are 2 independent parts, one for each index of `groups`. A program takes and returns all parts, laid end to end along the dimension named above; each array names one. Nothing has to cross between parts.
All inputs are finite; a program needn't handle non-finite values.
Results may differ from a plain program's by a relative error of at most 0.0027.
Values may be sent and summed in bfloat16 or wider, within the bound.
No kernel may reach another device: no remote copies, remote signals or barrier semaphores. Data moves between devices by JAX's collectives and lax.ppermute only.
A program may use at most 64 MiB of HBM per device.

v0:
```python
import math

import jax
import jax.numpy as jnp
from jax import lax
from jax.sharding import PartitionSpec as P

amplitude = 1.0
length_square = 32.0
noise_level = 0.5


def squares(points):
    widened = points.astype(jnp.float32)
    return jnp.sum(widened * widened, axis=0)


def kernel_tile(row_points, row_square, col_points, col_square):
    products = lax.dot_general(
        row_points, col_points, (((0,), (0,)), ((), ())), preferred_element_type=jnp.float32
    )
    distance = row_square[:, None] + col_square[None, :] - 2.0 * products
    return (amplitude * jnp.exp(-distance / (2.0 * length_square))).astype(jnp.bfloat16)


def fold_columns(row_points, running_sum, pieces):
    row_square = squares(row_points)
    col_points, col_probes = pieces
    column_count = col_points.shape[1]
    block_size = math.gcd(column_count, 2048)

    def one_block(block_index, running):
        offset = block_index * block_size
        part_points = lax.dynamic_slice_in_dim(col_points, offset, block_size, 1)
        part_probes = lax.dynamic_slice_in_dim(col_probes, offset, block_size, 1)
        kernel = kernel_tile(row_points, row_square, part_points, squares(part_points))
        return running + lax.dot_general(
            part_probes, kernel, (((1,), (1,)), ((), ())), preferred_element_type=jnp.float32
        )

    return lax.fori_loop(0, column_count // block_size, one_block, running_sum)


def body(points, direction, residual, solution):
    probes = direction.astype(jnp.bfloat16)
    initial = jnp.zeros((probes.shape[0], points.shape[1]), jnp.float32)
    applied = fold_columns(
        points,
        initial,
        (
            lax.all_gather(points, ("row", "col"), axis=1, tiled=True),
            lax.all_gather(probes, ("row", "col"), axis=1, tiled=True),
        ),
    )
    image = applied + noise_level * direction
    old_norm, curvature = lax.psum(
        (jnp.sum(residual * residual, axis=1), jnp.sum(direction * image, axis=1)), ("row", "col")
    )
    step_size = old_norm / curvature
    solution_next = solution + step_size[:, None] * direction
    residual_next = residual - step_size[:, None] * image
    new_norm = lax.psum(jnp.sum(residual_next * residual_next, axis=1), ("row", "col"))
    direction_next = residual_next + (new_norm / (old_norm + 1e-06))[:, None] * direction
    return (solution_next, residual_next, direction_next)


def solution(mesh):
    placed = (
        P(None, ("groups", "row", "col")),
        P(None, ("groups", "row", "col")),
        P(None, ("groups", "row", "col")),
        P(None, ("groups", "row", "col")),
    )
    return jax.shard_map(
        body,
        mesh=mesh,
        in_specs=placed,
        out_specs=(
            P(None, ("groups", "row", "col")),
            P(None, ("groups", "row", "col")),
            P(None, ("groups", "row", "col")),
        ),
        check_vma=False,
    )
```

profile of v0, /device:TPU:0, one launch (start us, length us, event | category | flops | bytes accessed | tf_op | source)
XLA Modules:
  0.0 109.8 jit_solution(630193757113701278)
XLA Ops:
  0.6 24.8 %all-gather.1 = bf16[16,192,64]{1,2,0:T(8,128)(2,1)S(1)} all-gather(bf16[1,192,64]{1,2,0:T(8,128)(2,1)} %bitcast.36), channel_id=1, replica_groups=mesh['groups'=2,'row'=8,'col'=2] {'row','col'}, dimensions={0}, use_global_device_ids=true | all-gather | bytes 417792 | tf_op jit(solution)/shard_map/all_gather | solution.py:51
  25.4 0.3 copy.10
  25.7 0.0 copy-start
  25.7 0.5 reshape.13
  26.3 0.2 copy-done
  26.5 18.1 %all-gather = bf16[16,192,32]{1,2,0:T(8,128)(2,1)S(1)} all-gather(bf16[1,192,32]{1,2,0:T(8,128)(2,1)S(1)} %convert_bitcast_fusion), channel_id=1, replica_groups=mesh['groups'=2,'row'=8,'col'=2] {'row','col'}, dimensions={0}, use_global_device_ids=true | all-gather | bytes 208896 | tf_op jit(solution)/shard_map/all_gather | solution.py:52
  44.6 0.1 copy.9
  44.8 0.0 copy-start.1
  44.8 0.3 reshape.11
  45.1 0.5 copy-done.1
  45.6 0.0 copy-start.2
  45.6 2.0 %while.14 = (s32[]{:T(128)}, f32[32,192]{1,0:T(8,128)S(1)}, bf16[32,3072]{1,0:T(8,128)(2,1)S(1)}, f32[192]{0:T(256)S(1)}, bf16[64,3072]{1,0:T(8,128)(2,1)S(1)}, ...) while((s32[]{:T(128)}, f32[32,192]{1,0:T(8,128)S(1)}, ...), condition=%wide.region_5.0_spmd.clone, body=%wide.region_3.5_spmd.clone.sunk | while | flops 39136264 | bytes 428704 | solution.py:41
  45.6 0.6 fusion.28
  46.3 0.6 fusion.28
  46.9 0.6 fusion.28
  47.5 0.0 copy-done.2
  47.5 0.0 copy-start.4
  47.6 0.1 multiply_reduce_fusion.3
  47.7 31.1 %all-reduce = (f32[32]{0:T(128)S(1)}, f32[32]{0:T(128)S(1)}) all-reduce(f32[32]{0:T(128)S(1)} %get-tuple-element.152, f32[32]{0:T(128)S(1)} %get-tuple-element.151), channel_id=1, replica_groups=mesh['groups'=2,'row'=8,'col'=2] {'row','col'}, use_global_device_ids=true, to_apply=%region_1.2 | all-reduce | flops 64 | bytes 512 | tf_op jit(solution)/shard_map/psum | solution.py:56
  78.8 0.0 copy-done.4
  78.8 0.8 multiply_reduce_fusion.2
  79.6 0.0 copy-start.3
  79.6 29.5 %psum.23 = f32[32]{0:T(128)S(1)} all-reduce(f32[32]{0:T(128)S(1)} %get-tuple-element.148), channel_id=1, replica_groups=mesh['groups'=2,'row'=8,'col'=2] {'row','col'}, use_global_device_ids=true, to_apply=%region_9.0 | all-reduce | flops 32 | bytes 256 | tf_op jit(solution)/shard_map/psum | solution.py:62
  109.1 0.7 multiply_add_fusion
  109.8 0.0 copy-done.3
  (8 shorter events, 0.2 us)
Async XLA Ops:
  25.7 0.8 copy-start
  44.8 0.8 copy-start.1
  45.6 2.0 %copy-start.2 = (f32[32,192]{1,0:T(8,128)S(1)}, f32[32,192]{1,0:T(8,128)}, u32[]{:S(2)}) copy-start(f32[32,192]{1,0:T(8,128)} %param.8) | copy-start | bytes 73732
  47.5 31.2 %copy-start.4 = (f32[32,192]{1,0:T(8,128)S(1)}, f32[32,192]{1,0:T(8,128)}, u32[]{:S(2)}) copy-start(f32[32,192]{1,0:T(8,128)} %param.9) | copy-start | bytes 73732
  79.6 30.2 %copy-start.3 = (f32[32,192]{1,0:T(8,128)}, f32[32,192]{1,0:T(8,128)S(1)}, u32[]{:S(2)}) copy-start(f32[32,192]{1,0:T(8,128)S(1)} %get-tuple-element.149) | copy-start | bytes 73732
where the time goes:
time: 110 us
  blocking collectives  104 us (95%)
  local copies, waits for them, and re-layouts  1.94 us (2%)
  other arithmetic  1.8 us (2%)
  matrix products  1.71 us (2%)
    psum x1, blocking collectives, body(): lax.psum((jnp.sum(residual * residual, axis=1), jnp.sum(direction * image...  31.1 us
    psum x1, blocking collectives, body(): lax.psum(jnp.sum(residual_next * residual_next, axis=1), ('row', 'col'))  29.5 us
    all_gather x1, blocking collectives, body(): lax.all_gather(points, ('row', 'col'), axis=1, tiled=True)  24.8 us
    all_gather x1, blocking collectives, body(): lax.all_gather(probes, ('row', 'col'), axis=1, tiled=True)  18.1 us

commit v1 on v0

v1 whole, which is shorter than its diff:
```python
import math

import jax
import jax.numpy as jnp
from jax import lax
from jax.sharding import PartitionSpec as P

amplitude = 1.0
length_square = 32.0
noise_level = 0.5

AXES = ("row", "col")


def squares(points):
    widened = points.astype(jnp.float32)
    return jnp.sum(widened * widened, axis=0)


def kernel_tile(row_points, row_square, col_points, col_square):
    products = lax.dot_general(
        row_points, col_points, (((0,), (0,)), ((), ())), preferred_element_type=jnp.float32
    )
    distance = row_square[:, None] + col_square[None, :] - 2.0 * products
    return (amplitude * jnp.exp(-distance / (2.0 * length_square))).astype(jnp.bfloat16)


def fold_columns(row_points, running_sum, pieces):
    row_square = squares(row_points)
    col_points, col_probes = pieces
    column_count = col_points.shape[1]
    block_size = math.gcd(column_count, 2048)

    def one_block(block_index, running):
        offset = block_index * block_size
        part_points = lax.dynamic_slice_in_dim(col_points, offset, block_size, 1)
        part_probes = lax.dynamic_slice_in_dim(col_probes, offset, block_size, 1)
        kernel = kernel_tile(row_points, row_square, part_points, squares(part_points))
        return running + lax.dot_general(
            part_probes, kernel, (((1,), (1,)), ((), ())), preferred_element_type=jnp.float32
        )

    return lax.fori_loop(0, column_count // block_size, one_block, running_sum)


def strides(count):
    found = []
    while count > 1:
        assert count % 2 == 0
        count //= 2
        found.append(count)
    return found


def swapped(array, count, stride):
    return lax.ppermute(array, AXES, [(i, i ^ stride) for i in range(count)])


def make_body(count):
    def total(values):
        for stride in reversed(strides(count)):
            values = values + swapped(values, count, stride)
        return values

    def body(points, direction, residual, solution):
        probes = direction.astype(jnp.bfloat16)
        held = jnp.concatenate([points, probes], axis=0)[None]
        for stride in strides(count):
            held = jnp.concatenate([held, swapped(held, count, stride)], axis=0)
        held = jnp.transpose(held, (1, 0, 2)).reshape(held.shape[1], -1)
        initial = jnp.zeros((probes.shape[0], points.shape[1]), jnp.float32)
        applied = fold_columns(points, initial, (held[: points.shape[0]], held[points.shape[0] :]))
        image = applied + noise_level * direction
        sums = total(
            jnp.stack(
                [
                    jnp.sum(residual * residual, axis=1),
                    jnp.sum(direction * image, axis=1),
                    jnp.sum(residual * image, axis=1),
                    jnp.sum(image * image, axis=1),
                ]
            )
        )
        old_norm, curvature, cross, image_norm = sums[0], sums[1], sums[2], sums[3]
        step_size = old_norm / curvature
        solution_next = solution + step_size[:, None] * direction
        residual_next = residual - step_size[:, None] * image
        new_norm = old_norm + step_size * (step_size * image_norm - 2.0 * cross)
        direction_next = residual_next + (new_norm / (old_norm + 1e-06))[:, None] * direction
        return (solution_next, residual_next, direction_next)

    return body


def solution(mesh):
    placed = P(None, ("groups", "row", "col"))
    return jax.shard_map(
        make_body(mesh.shape["row"] * mesh.shape["col"]),
        mesh=mesh,
        in_specs=(placed,) * 4,
        out_specs=(placed,) * 3,
        check_vma=False,
    )
```

time: 110 us -> 38 us (0.35)
  blocking collectives: 104 us -> 0 us
  waiting for transfers between devices: 0 us -> 18.6 us
  starting transfers between devices: 0 us -> 13.2 us
    psum x2 -> x0, blocking collectives: 60.6 us -> none  [the longest x1 31.1 us: body(): lax.psum((jnp.sum(residual * residual, axis=1), jnp.sum(direction * image...]
    all_gather x2 -> x0, blocking collectives: 42.9 us -> none  [the longest x1 24.8 us: body(): lax.all_gather(points, ('row', 'col'), axis=1, tiled=True)]
    ppermute x0 -> x8, waiting for transfers between devices: none -> 18.6 us  [swapped(): return lax.ppermute(array, AXES, [(i, i ^ stride) for i in range(count)])]
    ppermute x0 -> x8, starting transfers between devices: none -> 13.2 us  [swapped(): return lax.ppermute(array, AXES, [(i, i ^ stride) for i in range(count)])]
    unnamed x12 -> x11, local copies, waits for them, and re-layouts: 1.5 us -> 0.05 us
    slice x0 -> x6, local copies, waits for them, and re-layouts: none -> 1.29 us  [the longest x3 0.87 us: body(): held[:points.shape[0]]]
  transfers between devices with their start and end apart: 0 -> 8, of which waited for: 0 -> 8; matrix products, arithmetic and copies ran while one was open for 0% -> 0% of each run, Pallas kernels for 0% -> 0%
where the time goes in v1:
time: 38 us; the launch traced here: 37.8 us
  waiting for transfers between devices  18.6 us (49%)
  starting transfers between devices  13.2 us (35%)
  other arithmetic  2.01 us (5%)
  matrix products  1.71 us (4%)
  local copies, waits for them, and re-layouts  1.37 us (4%)
  between operations  0.81 us (2%)
    ppermute x8, waiting for transfers between devices, swapped(): return lax.ppermute(array, AXES, [(i, i ^ stride) for i in range(count)])  18.6 us
    ppermute x8, starting transfers between devices, swapped(): return lax.ppermute(array, AXES, [(i, i ^ stride) for i in range(count)])  13.2 us
    dot_general x3, matrix products, one_block(): lax.dot_general(part_probes, kernel, (((1,), (1,)), ((), ())), preferred_...  1.71 us
    slice x3, local copies, waits for them, and re-layouts, body(): held[:points.shape[0]]  0.87 us
    convert_element_type x1, other arithmetic, body(): probes = direction.astype(jnp.bfloat16)  0.77 us
  transfers between devices with their start and end apart: 8, of which 8 were waited for; matrix products, arithmetic and copies ran while one was open for 0% of the time, Pallas kernels for 0%

profile of v1, /device:TPU:0, one launch (start us, length us, event | category | flops | bytes accessed | tf_op | source)
XLA Modules:
  0.0 37.8 jit_solution(8319133283347036270)
XLA Ops:
  0.6 0.0 copy-start
  0.6 0.8 %convert_element_type.20 = bf16[32,192]{1,0:T(8,128)(2,1)S(1)} convert(f32[32,192]{1,0:T(8,128)} %param.7) | non-fusion elementwise | flops 6144 | bytes 36864 | tf_op jit(solution)/shard_map/convert_element_type | solution.py:66
  1.4 4.1 %collective-permute-start = (bf16[1,96,192]{2,1,0:T(8,128)(2,1)S(1)}, bf16[1,96,192]{2,1,0:T(8,128)(2,1)S(1)}, u32[]{:S(2)}, u32[]{:S(2)}) collective-permute-start(bf16[1,96,192]{2,1,0:T(8,128)(2,1)S(1)} %maximum_bitcast_fusion), channel_id=1, source_target_pairs={{0,8},{1,9},{2,10},{3,11},{4,12},{5,13},{6,14},{7,15},{8,0},{9,1},... | collective-permute-start | bytes 110600 | tf_op jit(solution)/shard_map/ppermute | solution.py:56
  5.5 2.6 %collective-permute-done = bf16[1,96,192]{2,1,0:T(8,128)(2,1)S(1)} collective-permute-done((bf16[1,96,192]{2,1,0:T(8,128)(2,1)S(1)}, bf16[1,96,192]{2,1,0:T(8,128)(2,1)S(1)}, u32[]{:S(2)}, u32[]{:S(2)}) %collective-permute-start) | collective-permute-done | bytes 36896 | tf_op jit(solution)/shard_map/ppermute | solution.py:56
  8.1 1.4 %collective-permute-start.1 = (bf16[2,96,192]{2,1,0:T(8,128)(2,1)S(1)}, bf16[2,96,192]{2,1,0:T(8,128)(2,1)S(1)}, u32[]{:S(2)}, u32[]{:S(2)}) collective-permute-start(bf16[2,96,192]{2,1,0:T(8,128)(2,1)S(1)} %pad_maximum_fusion.2), channel_id=1, source_target_pairs={{0,4},{1,5},{2,6},{3,7},{4,0},{5,1},{6,2},{7,3},{8,12},{9,13},{10,... | collective-permute-start | bytes 221192 | tf_op jit(solution)/shard_map/ppermute | solution.py:56
  9.6 3.2 %collective-permute-done.1 = bf16[2,96,192]{2,1,0:T(8,128)(2,1)S(1)} collective-permute-done((bf16[2,96,192]{2,1,0:T(8,128)(2,1)S(1)}, bf16[2,96,192]{2,1,0:T(8,128)(2,1)S(1)}, u32[]{:S(2)}, u32[]{:S(2)}) %collective-permute-start.1) | collective-permute-done | bytes 73760 | tf_op jit(solution)/shard_map/ppermute | solution.py:56
  12.9 1.8 %collective-permute-start.2 = (bf16[4,96,192]{2,1,0:T(8,128)(2,1)S(1)}, bf16[4,96,192]{2,1,0:T(8,128)(2,1)S(1)}, u32[]{:S(2)}, u32[]{:S(2)}) collective-permute-start(bf16[4,96,192]{2,1,0:T(8,128)(2,1)S(1)} %pad_maximum_fusion.1), channel_id=1, source_target_pairs={{0,2},{1,3},{2,0},{3,1},{4,6},{5,7},{6,4},{7,5},{8,10},{9,11},{10,... | collective-permute-start | bytes 442376 | tf_op jit(solution)/shard_map/ppermute | solution.py:56
  14.7 3.9 %collective-permute-done.2 = bf16[4,96,192]{2,1,0:T(8,128)(2,1)S(1)} collective-permute-done((bf16[4,96,192]{2,1,0:T(8,128)(2,1)S(1)}, bf16[4,96,192]{2,1,0:T(8,128)(2,1)S(1)}, u32[]{:S(2)}, u32[]{:S(2)}) %collective-permute-start.2) | collective-permute-done | bytes 147488 | tf_op jit(solution)/shard_map/ppermute | solution.py:56
  18.6 0.1 pad_maximum_fusion
  18.7 0.1 collective-permute-start.3
  18.8 1.7 %collective-permute-done.3 = bf16[8,96,192]{2,1,0:T(8,128)(2,1)S(1)} collective-permute-done((bf16[8,96,192]{2,1,0:T(8,128)(2,1)S(1)}, bf16[8,96,192]{2,1,0:T(8,128)(2,1)S(1)}, u32[]{:S(2)}, u32[]{:S(2)}) %collective-permute-start.3) | collective-permute-done | bytes 294944 | tf_op jit(solution)/shard_map/ppermute | solution.py:56
  20.6 0.2 copy.7
  20.7 0.3 slice.25
  21.0 0.3 copy.8
  21.3 0.5 %slice.27 = bf16[64,3072]{1,0:T(8,128)(2,1)S(1)} reshape(bf16[64,16,192]{2,1,0:T(8,128)(2,1)S(1)} %copy.8) | data formatting | bytes 786432 | tf_op jit(solution)/shard_map/slice | solution.py:72
  21.8 0.0 copy-start.1
  21.9 0.0 copy-start.2
  21.9 2.0 %while.14 = (s32[]{:T(128)}, f32[32,192]{1,0:T(8,128)S(1)}, bf16[32,3072]{1,0:T(8,128)(2,1)S(1)}, f32[192]{0:T(256)S(1)}, bf16[64,3072]{1,0:T(8,128)(2,1)S(1)}, ...) while((s32[]{:T(128)}, f32[32,192]{1,0:T(8,128)S(1)}, ...), condition=%wide.region_4.0_spmd.clone, body=%wide.region_2.4_spmd.clone.sunk | while | flops 39136264 | bytes 428712 | solution.py:43
  21.9 0.6 %fusion.33 = f32[32,192]{1,0:T(8,128)S(1)} fusion(bf16[64,192]{1,0:T(8,128)(2,1)S(1)} %get-tuple-element.217, f32[1024]{0:T(1024)S(1)} %multiply_reduce_fusion.7, f32[192]{0:T(256)S(1)} %get-tuple-element.215, bf16[64,3072]{1,0:T(8,128)(2,1)S(1)} %get-tuple-element.216, s32[]{:T(128)S(6)} %select_n.10, bf16[32,3072]{1,0:T(8,128)(2,1)S(1)} %get-tuple-element.214, ...), kind=kOutput, calls=%fused_computation.8.clone.1 | convolution fusion | flops 38940672 | bytes 293376 | tf_op jit(solution)/shard_map/while/body/eval_jaxpr/dot_general | solution.py:39
  22.6 0.6 %fusion.33 = f32[32,192]{1,0:T(8,128)S(1)} fusion(bf16[64,192]{1,0:T(8,128)(2,1)S(1)} %get-tuple-element.217, f32[1024]{0:T(1024)S(1)} %multiply_reduce_fusion.7, f32[192]{0:T(256)S(1)} %get-tuple-element.215, bf16[64,3072]{1,0:T(8,128)(2,1)S(1)} %get-tuple-element.216, s32[]{:T(128)S(6)} %select_n.10, bf16[32,3072]{1,0:T(8,128)(2,1)S(1)} %get-tuple-element.214, ...), kind=kOutput, calls=%fused_computation.8.clone.1 | convolution fusion | flops 38940672 | bytes 293376 | tf_op jit(solution)/shard_map/while/body/eval_jaxpr/dot_general | solution.py:39
  23.2 0.6 %fusion.33 = f32[32,192]{1,0:T(8,128)S(1)} fusion(bf16[64,192]{1,0:T(8,128)(2,1)S(1)} %get-tuple-element.217, f32[1024]{0:T(1024)S(1)} %multiply_reduce_fusion.7, f32[192]{0:T(256)S(1)} %get-tuple-element.215, bf16[64,3072]{1,0:T(8,128)(2,1)S(1)} %get-tuple-element.216, s32[]{:T(128)S(6)} %select_n.10, bf16[32,3072]{1,0:T(8,128)(2,1)S(1)} %get-tuple-element.214, ...), kind=kOutput, calls=%fused_computation.8.clone.1 | convolution fusion | flops 38940672 | bytes 293376 | tf_op jit(solution)/shard_map/while/body/eval_jaxpr/dot_general | solution.py:39
  23.9 0.1 multiply_reduce_fusion.4
  24.0 0.0 copy-start.3
  24.0 0.2 collective-permute-start.4
  24.2 1.0 %collective-permute-done.4 = f32[4,32]{1,0:T(4,128)S(1)} collective-permute-done((f32[4,32]{1,0:T(4,128)S(1)}, f32[4,32]{1,0:T(4,128)S(1)}, u32[]{:S(2)}, u32[]{:S(2)}) %collective-permute-start.4) | collective-permute-done | bytes 544 | tf_op jit(solution)/shard_map/ppermute | solution.py:56
  25.3 1.8 %collective-permute-start.5 = (f32[4,32]{1,0:T(4,128)S(1)}, f32[4,32]{1,0:T(4,128)S(1)}, u32[]{:S(2)}, u32[]{:S(2)}) collective-permute-start(f32[4,32]{1,0:T(4,128)S(1)} %fusion.23), channel_id=1, source_target_pairs={{0,2},{1,3},{2,0},{3,1},{4,6},{5,7},{6,4},{7,5},{8,10},{9,11},{10,... | collective-permute-start | bytes 1544 | tf_op jit(solution)/shard_map/ppermute | solution.py:56
  27.0 1.9 %collective-permute-done.5 = f32[4,32]{1,0:T(4,128)S(1)} collective-permute-done((f32[4,32]{1,0:T(4,128)S(1)}, f32[4,32]{1,0:T(4,128)S(1)}, u32[]{:S(2)}, u32[]{:S(2)}) %collective-permute-start.5) | collective-permute-done | bytes 544 | tf_op jit(solution)/shard_map/ppermute | solution.py:56
  28.9 1.4 %collective-permute-start.6 = (f32[4,32]{1,0:T(4,128)S(1)}, f32[4,32]{1,0:T(4,128)S(1)}, u32[]{:S(2)}, u32[]{:S(2)}) collective-permute-start(f32[4,32]{1,0:T(4,128)S(1)} %fusion.25), channel_id=1, source_target_pairs={{0,4},{1,5},{2,6},{3,7},{4,0},{5,1},{6,2},{7,3},{8,12},{9,13},{10,... | collective-permute-start | bytes 1544 | tf_op jit(solution)/shard_map/ppermute | solution.py:56
  30.4 2.2 %collective-permute-done.6 = f32[4,32]{1,0:T(4,128)S(1)} collective-permute-done((f32[4,32]{1,0:T(4,128)S(1)}, f32[4,32]{1,0:T(4,128)S(1)}, u32[]{:S(2)}, u32[]{:S(2)}) %collective-permute-start.6) | collective-permute-done | bytes 544 | tf_op jit(solution)/shard_map/ppermute | solution.py:56
  32.6 2.4 %collective-permute-start.7 = (f32[4,32]{1,0:T(4,128)S(1)}, f32[4,32]{1,0:T(4,128)S(1)}, u32[]{:S(2)}, u32[]{:S(2)}) collective-permute-start(f32[4,32]{1,0:T(4,128)S(1)} %add.105), channel_id=1, source_target_pairs={{0,8},{1,9},{2,10},{3,11},{4,12},{5,13},{6,14},{7,15},{8,0},{9,1},... | collective-permute-start | bytes 1544 | tf_op jit(solution)/shard_map/ppermute | solution.py:56
  35.0 2.0 %collective-permute-done.7 = f32[4,32]{1,0:T(4,128)S(1)} collective-permute-done((f32[4,32]{1,0:T(4,128)S(1)}, f32[4,32]{1,0:T(4,128)S(1)}, u32[]{:S(2)}, u32[]{:S(2)}) %collective-permute-start.7) | collective-permute-done | bytes 544 | tf_op jit(solution)/shard_map/ppermute | solution.py:56
  37.1 0.7 %multiply_add_fusion = (f32[32,192]{1,0:T(8,128)}, f32[32,192]{1,0:T(8,128)}, f32[32,192]{1,0:T(8,128)}) fusion(f32[32,192]{1,0:T(8,128)S(1)} %copy-done.1, f32[32]{0:T(128)S(1)} %get-tuple-element.152, f32[32,192]{1,0:T(8,128)S(1)} %copy-done.2, f32[32,192]{1,0:T(8,128)S(1)} %get-tuple-element.112, f32[32]{0:T(128)S(1)} %get-tuple-element.153, ...), kind=kLoop, calls=%fused_computation.25 | loop fusion | flops 49152 | bytes 172288 | tf_op jit(solution)/shard_map/add | solution.py:89
  (25 shorter events, 0.4 us)
Async XLA Ops:
  0.6 0.8 %copy-start = (bf16[64,192]{1,0:T(8,128)(2,1)S(1)}, bf16[64,192]{1,0:T(8,128)(2,1)}, u32[]{:S(2)}) copy-start(bf16[64,192]{1,0:T(8,128)(2,1)} %param.6) | copy-start | bytes 73732
  1.4 6.7 %collective-permute-start = (bf16[1,96,192]{2,1,0:T(8,128)(2,1)S(1)}, bf16[1,96,192]{2,1,0:T(8,128)(2,1)S(1)}, u32[]{:S(2)}, u32[]{:S(2)}) collective-permute-start(bf16[1,96,192]{2,1,0:T(8,128)(2,1)S(1)} %maximum_bitcast_fusion), channel_id=1, source_target_pairs={{0,8},{1,9},{2,10},{3,11},{4,12},{5,13},{6,14},{7,15},{8,0},{9,1},... | collective-permute-start | bytes 110600 | tf_op jit(solution)/shard_map/ppermute | solution.py:56
  8.1 4.7 %collective-permute-start.1 = (bf16[2,96,192]{2,1,0:T(8,128)(2,1)S(1)}, bf16[2,96,192]{2,1,0:T(8,128)(2,1)S(1)}, u32[]{:S(2)}, u32[]{:S(2)}) collective-permute-start(bf16[2,96,192]{2,1,0:T(8,128)(2,1)S(1)} %pad_maximum_fusion.2), channel_id=1, source_target_pairs={{0,4},{1,5},{2,6},{3,7},{4,0},{5,1},{6,2},{7,3},{8,12},{9,13},{10,... | collective-permute-start | bytes 221192 | tf_op jit(solution)/shard_map/ppermute | solution.py:56
  12.9 5.7 %collective-permute-start.2 = (bf16[4,96,192]{2,1,0:T(8,128)(2,1)S(1)}, bf16[4,96,192]{2,1,0:T(8,128)(2,1)S(1)}, u32[]{:S(2)}, u32[]{:S(2)}) collective-permute-start(bf16[4,96,192]{2,1,0:T(8,128)(2,1)S(1)} %pad_maximum_fusion.1), channel_id=1, source_target_pairs={{0,2},{1,3},{2,0},{3,1},{4,6},{5,7},{6,4},{7,5},{8,10},{9,11},{10,... | collective-permute-start | bytes 442376 | tf_op jit(solution)/shard_map/ppermute | solution.py:56
  18.7 1.8 %collective-permute-start.3 = (bf16[8,96,192]{2,1,0:T(8,128)(2,1)S(1)}, bf16[8,96,192]{2,1,0:T(8,128)(2,1)S(1)}, u32[]{:S(2)}, u32[]{:S(2)}) collective-permute-start(bf16[8,96,192]{2,1,0:T(8,128)(2,1)S(1)} %pad_maximum_fusion), channel_id=1, source_target_pairs={{0,1},{1,0},{2,3},{3,2},{4,5},{5,4},{6,7},{7,6},{8,9},{9,8},{10,11... | collective-permute-start | bytes 884744 | tf_op jit(solution)/shard_map/ppermute | solution.py:56
  21.8 2.0 %copy-start.1 = (f32[32,192]{1,0:T(8,128)S(1)}, f32[32,192]{1,0:T(8,128)}, u32[]{:S(2)}) copy-start(f32[32,192]{1,0:T(8,128)} %param.7) | copy-start | bytes 73732
  21.9 2.0 %copy-start.2 = (f32[32,192]{1,0:T(8,128)S(1)}, f32[32,192]{1,0:T(8,128)}, u32[]{:S(2)}) copy-start(f32[32,192]{1,0:T(8,128)} %param.8) | copy-start | bytes 73732
  24.0 13.1 %copy-start.3 = (f32[32,192]{1,0:T(8,128)S(1)}, f32[32,192]{1,0:T(8,128)}, u32[]{:S(2)}) copy-start(f32[32,192]{1,0:T(8,128)} %param.9) | copy-start | bytes 73732
  24.0 1.2 %collective-permute-start.4 = (f32[4,32]{1,0:T(4,128)S(1)}, f32[4,32]{1,0:T(4,128)S(1)}, u32[]{:S(2)}, u32[]{:S(2)}) collective-permute-start(f32[4,32]{1,0:T(4,128)S(1)} %pad_maximum_fusion.3), channel_id=1, source_target_pairs={{0,1},{1,0},{2,3},{3,2},{4,5},{5,4},{6,7},{7,6},{8,9},{9,8},{10,11... | collective-permute-start | bytes 1544 | tf_op jit(solution)/shard_map/ppermute | solution.py:56
  25.3 3.7 %collective-permute-start.5 = (f32[4,32]{1,0:T(4,128)S(1)}, f32[4,32]{1,0:T(4,128)S(1)}, u32[]{:S(2)}, u32[]{:S(2)}) collective-permute-start(f32[4,32]{1,0:T(4,128)S(1)} %fusion.23), channel_id=1, source_target_pairs={{0,2},{1,3},{2,0},{3,1},{4,6},{5,7},{6,4},{7,5},{8,10},{9,11},{10,... | collective-permute-start | bytes 1544 | tf_op jit(solution)/shard_map/ppermute | solution.py:56
  28.9 3.7 %collective-permute-start.6 = (f32[4,32]{1,0:T(4,128)S(1)}, f32[4,32]{1,0:T(4,128)S(1)}, u32[]{:S(2)}, u32[]{:S(2)}) collective-permute-start(f32[4,32]{1,0:T(4,128)S(1)} %fusion.25), channel_id=1, source_target_pairs={{0,4},{1,5},{2,6},{3,7},{4,0},{5,1},{6,2},{7,3},{8,12},{9,13},{10,... | collective-permute-start | bytes 1544 | tf_op jit(solution)/shard_map/ppermute | solution.py:56
  32.6 4.5 %collective-permute-start.7 = (f32[4,32]{1,0:T(4,128)S(1)}, f32[4,32]{1,0:T(4,128)S(1)}, u32[]{:S(2)}, u32[]{:S(2)}) collective-permute-start(f32[4,32]{1,0:T(4,128)S(1)} %add.105), channel_id=1, source_target_pairs={{0,8},{1,9},{2,10},{3,11},{4,12},{5,13},{6,14},{7,15},{8,0},{9,1},... | collective-permute-start | bytes 1544 | tf_op jit(solution)/shard_map/ppermute | solution.py:56

commit v2 on v1

v2 whole, which is shorter than its diff:
```python
import functools
import math

import jax
import jax.numpy as jnp
from jax import lax
from jax.experimental import pallas as pl
from jax.experimental.pallas import tpu as pltpu
from jax.sharding import PartitionSpec as P

amplitude = 1.0
length_square = 32.0
noise_level = 0.5

AXES = ("row", "col")
LANES = 128
VMEM_BYTES = 32 << 20
RATE = math.log2(math.e) / length_square
SHIFT = math.log2(amplitude)


def in_vmem():
    return pl.BlockSpec(memory_space=pltpu.VMEM)


def halves(values):
    high = values.astype(jnp.bfloat16)
    return high, (values - high.astype(jnp.float32)).astype(jnp.bfloat16)


def pack_kernel(points_ref, direction_ref, residual_ref, out_ref):
    direction_high, direction_low = halves(direction_ref[...])
    residual_high, residual_low = halves(residual_ref[...])
    fields = jnp.concatenate(
        [points_ref[...], direction_high, residual_high, residual_low, direction_low], axis=0
    )
    height = fields.shape[0]
    out_ref[:height] = fields[:, :LANES]
    out_ref[height:] = jnp.concatenate(
        [fields[: height // 2, LANES:], fields[height // 2 :, LANES:]], axis=1
    )


def unpack_kernel(dim, first_ref, second_ref, held_ref, residual_ref, direction_ref):
    packs = [first_ref[0], first_ref[1], second_ref[0], second_ref[1]]
    side = LANES // 2
    height = packs[0].shape[0] * 2 // 3
    middle = height // 2
    probes = middle - dim
    upper, lower = [], []
    for pack in packs:
        upper.append(pack[:middle])
        lower.append(pack[middle:height])
    for left, right in ((packs[0], packs[1]), (packs[2], packs[3])):
        left, right = left[height:], right[height:]
        upper.append(jnp.concatenate([left[:, :side], right[:, :side]], axis=1))
        lower.append(jnp.concatenate([left[:, side:], right[:, side:]], axis=1))
    for index in range(len(upper)):
        span = slice(index * LANES, (index + 1) * LANES)
        held_ref[:, span] = upper[index]
        low = lower[index].astype(jnp.float32)
        residual_ref[:, span] = low[:probes] + low[probes : 2 * probes]
        direction_ref[:, span] = upper[index][dim:].astype(jnp.float32) + low[2 * probes :]


def widened(points, own):
    values = points.astype(jnp.float32)
    half = -0.5 * jnp.sum(values * values, axis=0, keepdims=True)
    high = half.astype(jnp.bfloat16).astype(jnp.float32)
    middle = (half - high).astype(jnp.bfloat16).astype(jnp.float32)
    low = half - high - middle
    row = lax.broadcasted_iota(jnp.int32, (16, points.shape[1]), 0)
    base = 0 if own else 3
    extra = jnp.where(row < 6, 1.0, 0.0)
    extra = jnp.where(row == base, high, extra)
    extra = jnp.where(row == base + 1, middle, extra)
    extra = jnp.where(row == base + 2, low, extra)
    return jnp.concatenate([points, extra.astype(jnp.bfloat16)], axis=0)


def fold(own, pieces, applied, dim):
    own_points = widened(own[:dim], True)
    for piece in pieces:
        half = lax.dot_general(
            widened(piece[:dim], False),
            own_points,
            (((0,), (0,)), ((), ())),
            preferred_element_type=jnp.float32,
        )
        kernel = jnp.exp2(half * RATE + SHIFT).astype(jnp.bfloat16)
        part = lax.dot_general(
            piece[dim:], kernel, (((1,), (0,)), ((), ())), preferred_element_type=jnp.float32
        )
        applied = part if applied is None else applied + part
    return applied


def first_fold_kernel(dim, own_ref, applied_ref):
    own = own_ref[...]
    applied_ref[...] = fold(own, [own], None, dim)


def fold_kernel(dim, own_ref, pieces_ref, before_ref, applied_ref):
    pieces = [pieces_ref[index] for index in range(pieces_ref.shape[0])]
    applied_ref[...] = fold(own_ref[...], pieces, before_ref[...], dim)


def long_fold_kernel(dim, own_ref, piece_ref, before_ref, applied_ref):
    @pl.when(pl.program_id(0) == 0)
    def _():
        applied_ref[...] = before_ref[...]

    applied_ref[...] = fold(own_ref[...], [piece_ref[0]], applied_ref[...], dim)


def sums_kernel(applied_ref, residual_ref, direction_ref, sums_ref):
    residual, direction = residual_ref[...], direction_ref[...]
    image = applied_ref[...] + noise_level * direction
    lane = lax.broadcasted_iota(jnp.int32, (image.shape[0], LANES), 1)
    table = jnp.zeros((image.shape[0], LANES), jnp.float32)
    products = (residual * residual, direction * image, residual * image, image * image)
    for index, product in enumerate(products):
        table = jnp.where(lane == index, jnp.sum(product, axis=1, keepdims=True), table)
    sums_ref[...] = table.T[:8]


def last_kernel(dim, own_ref, pieces_ref, before_ref, residual_ref, direction_ref, applied_ref, sums_ref):
    fold_kernel(dim, own_ref, pieces_ref, before_ref, applied_ref)
    sums_kernel(applied_ref, residual_ref, direction_ref, sums_ref)


def call(kernel, outs, args, pieces=0):
    columns, dim = 768, 80
    cost = None
    if pieces:
        count = pieces * columns * columns
        cost = pl.CostEstimate(
            flops=2 * count * (dim + 32), bytes_accessed=count, transcendentals=count
        )
    return pl.pallas_call(
        kernel,
        out_shape=outs,
        in_specs=[in_vmem()] * len(args),
        out_specs=jax.tree.map(lambda _: in_vmem(), outs),
        compiler_params=pltpu.CompilerParams(vmem_limit_bytes=VMEM_BYTES),
        cost_estimate=cost,
    )(*args)


def long_fold(own, pieces, before, dim):
    whole = lambda index: (0, 0)
    return pl.pallas_call(
        functools.partial(long_fold_kernel, dim),
        grid=(pieces.shape[0],),
        out_shape=jax.ShapeDtypeStruct(before.shape, before.dtype),
        in_specs=[
            pl.BlockSpec(own.shape, whole),
            pl.BlockSpec((1, *pieces.shape[1:]), lambda index: (index, 0, 0)),
            pl.BlockSpec(before.shape, whole),
        ],
        out_specs=pl.BlockSpec(before.shape, whole),
        compiler_params=pltpu.CompilerParams(vmem_limit_bytes=VMEM_BYTES),
    )(own, pieces, before)


def strides(count):
    found = []
    while count > 1:
        assert count % 2 == 0
        count //= 2
        found.append(count)
    return found


def swapped(array, count, stride):
    return lax.ppermute(array, AXES, [(i, i ^ stride) for i in range(count)])


def make_body(count):
    far, middle, *near = strides(count)

    def body(points, direction, residual, solution):
        dim, width = points.shape
        probes = direction.shape[0]
        columns = 4 * width
        height = dim + 4 * probes
        full = jax.ShapeDtypeStruct((probes, columns), jnp.float32)
        table = jax.ShapeDtypeStruct((8, probes), jnp.float32)
        packed = call(
            pack_kernel,
            jax.ShapeDtypeStruct((height * 3 // 2, LANES), jnp.bfloat16),
            (points, direction, residual),
        )[None]
        pair = jnp.concatenate([packed, swapped(packed, count, far)], axis=0)
        other = swapped(pair, count, middle)
        own, all_residual, all_direction = call(
            functools.partial(unpack_kernel, dim),
            (jax.ShapeDtypeStruct((dim + probes, columns), jnp.bfloat16), full, full),
            (pair, other),
        )
        held = own[None]
        applied = None
        pieces = None
        for stride in near:
            arriving = swapped(held, count, stride)
            if applied is None:
                applied = call(functools.partial(first_fold_kernel, dim), full, (own,), 1)
            elif pieces.shape[0] <= 2:
                applied = call(
                    functools.partial(fold_kernel, dim), full, (own, pieces, applied), pieces.shape[0]
                )
            else:
                applied = long_fold(own, pieces, applied, dim)
            held = jnp.concatenate([held, arriving], axis=0)
            pieces = arriving
        if pieces.shape[0] <= 2:
            applied, sums = call(
                functools.partial(last_kernel, dim),
                (full, table),
                (own, pieces, applied, all_residual, all_direction),
                pieces.shape[0],
            )
        else:
            applied = long_fold(own, pieces, applied, dim)
            sums = call(sums_kernel, table, (applied, all_residual, all_direction))
        for stride in reversed(near):
            sums = sums + swapped(sums, count, stride)
        start = 4 * LANES
        applied = jnp.concatenate([applied[:, :LANES], applied[:, start : start + width - LANES]], axis=1)
        image = applied + noise_level * direction
        old_norm, curvature, cross, image_norm = sums[0], sums[1], sums[2], sums[3]
        step_size = old_norm / curvature
        solution_next = solution + step_size[:, None] * direction
        residual_next = residual - step_size[:, None] * image
        new_norm = old_norm + step_size * (step_size * image_norm - 2.0 * cross)
        direction_next = residual_next + (new_norm / (old_norm + 1e-06))[:, None] * direction
        return (solution_next, residual_next, direction_next)

    return body


def solution(mesh):
    placed = P(None, ("groups", "row", "col"))
    return jax.shard_map(
        make_body(mesh.shape["row"] * mesh.shape["col"]),
        mesh=mesh,
        in_specs=(placed,) * 4,
        out_specs=(placed,) * 3,
        check_vma=False,
    )
```

time: 38 us -> 30.5 us (0.80)
  starting transfers between devices: 13.2 us -> 8.65 us
  waiting for transfers between devices: 18.6 us -> 14.8 us
  Pallas kernels: 0 us -> 2.97 us
  matrix products: 1.71 us -> 0 us
  other arithmetic: 2.01 us -> 0.78 us
  local copies, waits for them, and re-layouts: 1.37 us -> 2.28 us
    ppermute x8 -> x6, starting transfers between devices: 13.2 us -> 8.65 us  [swapped(): return lax.ppermute(array, AXES, [(i, i ^ stride) for i in range(count)])]
    ppermute x8 -> x6, waiting for transfers between devices: 18.6 us -> 14.8 us  [swapped(): return lax.ppermute(array, AXES, [(i, i ^ stride) for i in range(count)])]
    pallas_call x0 -> x5, Pallas kernels: none -> 2.97 us  [call(): pl.pallas_call(kernel, out_shape=outs, in_specs=[in_vmem()] * len(args),...]
    unnamed x11 -> x12, local copies, waits for them, and re-layouts: 0.05 us -> 2.28 us
    dot_general x3 -> x0, matrix products: 1.71 us -> none  [one_block(): lax.dot_general(part_probes, kernel, (((1,), (1,)), ((), ())), preferred_...]
    slice x6 -> x2, local copies, waits for them, and re-layouts: 1.29 us -> 0.01 us  [the longest x1 0.01 us: body(): applied[:, start:start + width - LANES]]
    convert_element_type x1 -> x0, other arithmetic: 0.77 us -> none  [body(): probes = direction.astype(jnp.bfloat16)]
  transfers between devices with their start and end apart: 8 -> 6, of which waited for: 8 -> 6; matrix products, arithmetic and copies ran while one was open for 0% -> 0% of each run, Pallas kernels for 0% -> 4%
where the time goes in v2:
time: 30.5 us; the launch traced here: 30.2 us
  waiting for transfers between devices  14.8 us (49%)
  starting transfers between devices  8.65 us (28%)
  Pallas kernels  2.97 us (10%)
  local copies, waits for them, and re-layouts  2.28 us (7%)
  other arithmetic  0.78 us (3%)
  between operations  0.69 us (2%)
    ppermute x6, waiting for transfers between devices, swapped(): return lax.ppermute(array, AXES, [(i, i ^ stride) for i in range(count)])  14.8 us
    ppermute x6, starting transfers between devices, swapped(): return lax.ppermute(array, AXES, [(i, i ^ stride) for i in range(count)])  8.65 us
    pallas_call x5, Pallas kernels, call(): pl.pallas_call(kernel, out_shape=outs, in_specs=[in_vmem()] * len(args),...  2.97 us
    unnamed x12, local copies, waits for them, and re-layouts  2.28 us
    add x1, other arithmetic, body(): residual_next + (new_norm / (old_norm + 1e-06))[:, None] * direction  0.71 us
  transfers between devices with their start and end apart: 6, of which 6 were waited for; matrix products, arithmetic and copies ran while one was open for 0% of the time, Pallas kernels for 4%

profile of v2, /device:TPU:0, one launch (start us, length us, event | category | flops | bytes accessed | tf_op | source)
XLA Modules:
  0.0 30.2 jit_solution(14143107638797211702)
XLA Ops:
  0.6 0.0 copy-start
  0.6 0.7 %copy-done = f32[32,192]{1,0:T(8,128)S(1)} copy-done((f32[32,192]{1,0:T(8,128)S(1)}, f32[32,192]{1,0:T(8,128)}, u32[]{:S(2)}) %copy-start) | copy-done | bytes 24600
  1.4 0.0 copy-start.2
  1.4 0.8 %copy-done.2 = f32[32,192]{1,0:T(8,128)S(1)} copy-done((f32[32,192]{1,0:T(8,128)S(1)}, f32[32,192]{1,0:T(8,128)}, u32[]{:S(2)}) %copy-start.2) | copy-done | bytes 24600
  2.1 0.0 copy-start.4
  2.2 0.8 %copy-done.4 = bf16[64,192]{1,0:T(8,128)(2,1)S(1)} copy-done((bf16[64,192]{1,0:T(8,128)(2,1)S(1)}, bf16[64,192]{1,0:T(8,128)(2,1)}, u32[]{:S(2)}) %copy-start.4) | copy-done | bytes 24600
  2.9 0.1 shard_map.67
  3.0 4.1 %collective-permute-start = (bf16[1,288,128]{2,1,0:T(8,128)(2,1)S(1)}, bf16[1,288,128]{2,1,0:T(8,128)(2,1)S(1)}, u32[]{:S(2)}, u32[]{:S(2)}) collective-permute-start(bf16[1,288,128]{2,1,0:T(8,128)(2,1)S(1)} %bitcast.24), channel_id=1, source_target_pairs={{0,8},{1,9},{2,10},{3,11},{4,12},{5,13},{6,14},{7,15},{8,0},{9,1},... | collective-permute-start | bytes 221192 | tf_op jit(solution)/shard_map/ppermute | solution.py:176
  7.1 3.9 %collective-permute-done = bf16[1,288,128]{2,1,0:T(8,128)(2,1)S(1)} collective-permute-done((bf16[1,288,128]{2,1,0:T(8,128)(2,1)S(1)}, bf16[1,288,128]{2,1,0:T(8,128)(2,1)S(1)}, u32[]{:S(2)}, u32[]{:S(2)}) %collective-permute-start) | collective-permute-done | bytes 73760 | tf_op jit(solution)/shard_map/ppermute | solution.py:176
  11.0 0.7 %collective-permute-start.1 = (bf16[2,288,128]{2,1,0:T(8,128)(2,1)S(1)}, bf16[2,288,128]{2,1,0:T(8,128)(2,1)S(1)}, u32[]{:S(2)}, u32[]{:S(2)}) collective-permute-start(bf16[2,288,128]{2,1,0:T(8,128)(2,1)S(1)} %pad_maximum_fusion.1.first_ref), channel_id=1, source_target_pairs={{0,4},{1,5},{2,6},{3,7},{4,0},{5,1},{6,2},{7,3},{8,12},{9,13},{10,... | collective-permute-start | bytes 442376 | tf_op jit(solution)/shard_map/ppermute | solution.py:176
  11.7 4.5 %collective-permute-done.1.second_ref = bf16[2,288,128]{2,1,0:T(8,128)(2,1)S(1)} collective-permute-done((bf16[2,288,128]{2,1,0:T(8,128)(2,1)S(1)}, bf16[2,288,128]{2,1,0:T(8,128)(2,1)S(1)}, u32[]{:S(2)}, u32[]{:S(2)}) %collective-permute-start.1) | collective-permute-done | bytes 147488 | tf_op jit(solution)/shard_map/ppermute | solution.py:176
  16.2 0.1 shard_map.68
  16.3 1.8 %collective-permute-start.2 = (bf16[1,96,768]{2,1,0:T(8,128)(2,1)S(1)}, bf16[1,96,768]{2,1,0:T(8,128)(2,1)S(1)}, u32[]{:S(2)}, u32[]{:S(2)}) collective-permute-start(bf16[1,96,768]{2,1,0:T(8,128)(2,1)S(1)} %bitcast.26), channel_id=1, source_target_pairs={{0,2},{1,3},{2,0},{3,1},{4,6},{5,7},{6,4},{7,5},{8,10},{9,11},{10,... | collective-permute-start | bytes 442376 | tf_op jit(solution)/shard_map/ppermute | solution.py:176
  18.1 3.4 %collective-permute-done.2.pieces_ref = bf16[1,96,768]{2,1,0:T(8,128)(2,1)S(1)} collective-permute-done((bf16[1,96,768]{2,1,0:T(8,128)(2,1)S(1)}, bf16[1,96,768]{2,1,0:T(8,128)(2,1)S(1)}, u32[]{:S(2)}, u32[]{:S(2)}) %collective-permute-start.2) | collective-permute-done | bytes 147488 | tf_op jit(solution)/shard_map/ppermute | solution.py:176
  21.5 0.1 collective-permute-start.3
  21.6 0.7 %shard_map.69.before_ref = f32[32,768]{1,0:T(8,128)S(1)} custom-call(bf16[96,768]{1,0:T(8,128)(2,1)S(1)} %get-tuple-element.8.own_ref), custom_call_target="tpu_custom_call" | custom-call | flops 132120576 | bytes 589824 | tf_op jit(solution)/shard_map/pallas_call | solution.py:140
  22.3 0.7 %shard_map.70.before_ref = f32[32,768]{1,0:T(8,128)S(1)} custom-call(bf16[96,768]{1,0:T(8,128)(2,1)S(1)} %get-tuple-element.8.own_ref, bf16[1,96,768]{2,1,0:T(8,128)(2,1)S(1)} %collective-permute-done.2.pieces_ref, f32[32,768]{1,0:T(8,128)S(1)} %shard_map.69.before_ref), custom_call_target="tpu_custom_call" | custom-call | flops 132120576 | bytes 589824 | tf_op jit(solution)/shard_map/pallas_call | solution.py:140
  23.0 0.2 collective-permute-done.3.pieces_ref
  23.2 0.0 copy-start.5
  23.2 1.4 %shard_map.71 = (f32[32,768]{1,0:T(8,128)S(1)}, f32[8,32]{1,0:T(8,128)S(1)}) custom-call(bf16[96,768]{1,0:T(8,128)(2,1)S(1)} %get-tuple-element.8.own_ref, bf16[2,96,768]{2,1,0:T(8,128)(2,1)S(1)} %collective-permute-done.3.pieces_ref, f32[32,768]{1,0:T(8,128)S(1)} %shard_map.70.before_ref, f32[32,768]{1,0:T(8,128)S(1)} %get-tuple-element.9.residual_ref, ...), custom_call_target="tpu_custom_call" | custom-call | flops 264241152 | bytes 1179648 | tf_op jit(solution)/shard_map/pallas_call | solution.py:140
  24.6 0.3 %collective-permute-start.4 = (f32[8,32]{1,0:T(8,128)S(1)}, f32[8,32]{1,0:T(8,128)S(1)}, u32[]{:S(2)}, u32[]{:S(2)}) collective-permute-start(f32[8,32]{1,0:T(8,128)S(1)} %get-tuple-element.11), channel_id=1, source_target_pairs={{0,1},{1,0},{2,3},{3,2},{4,5},{5,4},{6,7},{7,6},{8,9},{9,8},{10,11... | collective-permute-start | bytes 3080 | tf_op jit(solution)/shard_map/ppermute | solution.py:176
  25.0 0.9 %collective-permute-done.4 = f32[8,32]{1,0:T(8,128)S(1)} collective-permute-done((f32[8,32]{1,0:T(8,128)S(1)}, f32[8,32]{1,0:T(8,128)S(1)}, u32[]{:S(2)}, u32[]{:S(2)}) %collective-permute-start.4) | collective-permute-done | bytes 1056 | tf_op jit(solution)/shard_map/ppermute | solution.py:176
  25.8 1.7 %collective-permute-start.5 = (f32[8,32]{1,0:T(8,128)S(1)}, f32[8,32]{1,0:T(8,128)S(1)}, u32[]{:S(2)}, u32[]{:S(2)}) collective-permute-start(f32[8,32]{1,0:T(8,128)S(1)} %add.32), channel_id=1, source_target_pairs={{0,2},{1,3},{2,0},{3,1},{4,6},{5,7},{6,4},{7,5},{8,10},{9,11},{10,... | collective-permute-start | bytes 3080 | tf_op jit(solution)/shard_map/ppermute | solution.py:176
  27.5 0.0 copy-start.3
  27.5 0.0 copy-start.1
  27.5 1.9 %collective-permute-done.5 = f32[8,32]{1,0:T(8,128)S(1)} collective-permute-done((f32[8,32]{1,0:T(8,128)S(1)}, f32[8,32]{1,0:T(8,128)S(1)}, u32[]{:S(2)}, u32[]{:S(2)}) %collective-permute-start.5) | collective-permute-done | bytes 1056 | tf_op jit(solution)/shard_map/ppermute | solution.py:176
  29.4 0.0 copy-done.5
  29.4 0.0 copy-done.3
  29.5 0.0 copy-done.1
  29.5 0.7 %multiply_add_fusion = (f32[32,192]{1,0:T(8,128)}, f32[32,192]{1,0:T(8,128)}, f32[32,192]{1,0:T(8,128)}) fusion(f32[32,192]{1,0:T(8,128)S(1)} %copy-done.1, f32[32]{0:T(128)S(1)} %get-tuple-element.15, f32[32,192]{1,0:T(8,128)S(1)} %copy-done.3, f32[32,64]{1,0:T(8,128)S(1)} %slice.21, f32[32,128]{1,0:T(8,128)S(1)} %slice.20, f32[32]{0:T(128)S(1)} %get-tuple-element.16, ...), kind=kLoop, calls=%fused_computation.5 | loop fusion | flops 55296 | bytes 172288 | tf_op jit(solution)/shard_map/add | solution.py:236
  (7 shorter events, 0.1 us)
Async XLA Ops:
  0.6 0.8 %copy-start = (f32[32,192]{1,0:T(8,128)S(1)}, f32[32,192]{1,0:T(8,128)}, u32[]{:S(2)}) copy-start(f32[32,192]{1,0:T(8,128)} %direction_ref.1) | copy-start | bytes 73732
  1.4 0.8 %copy-start.2 = (f32[32,192]{1,0:T(8,128)S(1)}, f32[32,192]{1,0:T(8,128)}, u32[]{:S(2)}) copy-start(f32[32,192]{1,0:T(8,128)} %residual_ref.1) | copy-start | bytes 73732
  2.1 0.8 %copy-start.4 = (bf16[64,192]{1,0:T(8,128)(2,1)S(1)}, bf16[64,192]{1,0:T(8,128)(2,1)}, u32[]{:S(2)}) copy-start(bf16[64,192]{1,0:T(8,128)(2,1)} %points_ref.1) | copy-start | bytes 73732
  3.0 8.0 %collective-permute-start = (bf16[1,288,128]{2,1,0:T(8,128)(2,1)S(1)}, bf16[1,288,128]{2,1,0:T(8,128)(2,1)S(1)}, u32[]{:S(2)}, u32[]{:S(2)}) collective-permute-start(bf16[1,288,128]{2,1,0:T(8,128)(2,1)S(1)} %bitcast.24), channel_id=1, source_target_pairs={{0,8},{1,9},{2,10},{3,11},{4,12},{5,13},{6,14},{7,15},{8,0},{9,1},... | collective-permute-start | bytes 221192 | tf_op jit(solution)/shard_map/ppermute | solution.py:176
  11.0 5.2 %collective-permute-start.1 = (bf16[2,288,128]{2,1,0:T(8,128)(2,1)S(1)}, bf16[2,288,128]{2,1,0:T(8,128)(2,1)S(1)}, u32[]{:S(2)}, u32[]{:S(2)}) collective-permute-start(bf16[2,288,128]{2,1,0:T(8,128)(2,1)S(1)} %pad_maximum_fusion.1.first_ref), channel_id=1, source_target_pairs={{0,4},{1,5},{2,6},{3,7},{4,0},{5,1},{6,2},{7,3},{8,12},{9,13},{10,... | collective-permute-start | bytes 442376 | tf_op jit(solution)/shard_map/ppermute | solution.py:176
  16.3 5.2 %collective-permute-start.2 = (bf16[1,96,768]{2,1,0:T(8,128)(2,1)S(1)}, bf16[1,96,768]{2,1,0:T(8,128)(2,1)S(1)}, u32[]{:S(2)}, u32[]{:S(2)}) collective-permute-start(bf16[1,96,768]{2,1,0:T(8,128)(2,1)S(1)} %bitcast.26), channel_id=1, source_target_pairs={{0,2},{1,3},{2,0},{3,1},{4,6},{5,7},{6,4},{7,5},{8,10},{9,11},{10,... | collective-permute-start | bytes 442376 | tf_op jit(solution)/shard_map/ppermute | solution.py:176
  21.5 1.6 %collective-permute-start.3 = (bf16[2,96,768]{2,1,0:T(8,128)(2,1)S(1)}, bf16[2,96,768]{2,1,0:T(8,128)(2,1)S(1)}, u32[]{:S(2)}, u32[]{:S(2)}) collective-permute-start(bf16[2,96,768]{2,1,0:T(8,128)(2,1)S(1)} %pad_maximum_fusion), channel_id=1, source_target_pairs={{0,1},{1,0},{2,3},{3,2},{4,5},{5,4},{6,7},{7,6},{8,9},{9,8},{10,11... | collective-permute-start | bytes 884744 | tf_op jit(solution)/shard_map/ppermute | solution.py:176
  23.2 6.2 %copy-start.5 = (f32[32,192]{1,0:T(8,128)S(1)}, f32[32,192]{1,0:T(8,128)}, u32[]{:S(2)}) copy-start(f32[32,192]{1,0:T(8,128)} %param.7) | copy-start | bytes 73732
  24.6 1.2 %collective-permute-start.4 = (f32[8,32]{1,0:T(8,128)S(1)}, f32[8,32]{1,0:T(8,128)S(1)}, u32[]{:S(2)}, u32[]{:S(2)}) collective-permute-start(f32[8,32]{1,0:T(8,128)S(1)} %get-tuple-element.11), channel_id=1, source_target_pairs={{0,1},{1,0},{2,3},{3,2},{4,5},{5,4},{6,7},{7,6},{8,9},{9,8},{10,11... | collective-permute-start | bytes 3080 | tf_op jit(solution)/shard_map/ppermute | solution.py:176
  25.8 3.6 %collective-permute-start.5 = (f32[8,32]{1,0:T(8,128)S(1)}, f32[8,32]{1,0:T(8,128)S(1)}, u32[]{:S(2)}, u32[]{:S(2)}) collective-permute-start(f32[8,32]{1,0:T(8,128)S(1)} %add.32), channel_id=1, source_target_pairs={{0,2},{1,3},{2,0},{3,1},{4,6},{5,7},{6,4},{7,5},{8,10},{9,11},{10,... | collective-permute-start | bytes 3080 | tf_op jit(solution)/shard_map/ppermute | solution.py:176
  27.5 1.9 %copy-start.3 = (f32[32,192]{1,0:T(8,128)S(1)}, f32[32,192]{1,0:T(8,128)}, u32[]{:S(2)}) copy-start(f32[32,192]{1,0:T(8,128)} %residual_ref.1) | copy-start | bytes 73732
  27.5 1.9 %copy-start.1 = (f32[32,192]{1,0:T(8,128)S(1)}, f32[32,192]{1,0:T(8,128)}, u32[]{:S(2)}) copy-start(f32[32,192]{1,0:T(8,128)} %direction_ref.1) | copy-start | bytes 73732

commit v3 on v2

v3 whole, which is shorter than its diff:
```python
import functools
import math

import jax
import jax.numpy as jnp
from jax import lax
from jax.experimental import pallas as pl
from jax.experimental.pallas import tpu as pltpu
from jax.sharding import PartitionSpec as P

amplitude = 1.0
length_square = 32.0
noise_level = 0.5

AXES = ("row", "col")
LANES = 128
VMEM_BYTES = 32 << 20
PACK_VMEM_BYTES = 63 << 20
RATE = math.log2(math.e) / length_square
SHIFT = math.log2(amplitude)


def in_vmem():
    return pl.BlockSpec(memory_space=pltpu.VMEM)


def halves(values):
    high = values.astype(jnp.bfloat16)
    return high, (values - high.astype(jnp.float32)).astype(jnp.bfloat16)


def narrow(fields, out_ref):
    height = fields.shape[0]
    out_ref[0, :height] = fields[:, :LANES]
    out_ref[0, height:] = jnp.concatenate(
        [fields[: height // 2, LANES:], fields[height // 2 :, LANES:]], axis=1
    )


def pack_kernel(
    points_hbm, direction_hbm, residual_hbm, main_ref, rest_ref, points_ref, direction_ref, residual_ref, arrived
):
    copies = [
        pltpu.make_async_copy(source, target, arrived.at[index])
        for index, (source, target) in enumerate(
            (
                (points_hbm, points_ref),
                (direction_hbm, direction_ref),
                (residual_hbm, residual_ref),
            )
        )
    ]
    for copy in copies:
        copy.start()
    for copy in copies:
        copy.wait()
    direction_high, direction_low = halves(direction_ref[...])
    residual_high, residual_low = halves(residual_ref[...])
    narrow(jnp.concatenate([points_ref[...], direction_high], axis=0), main_ref)
    narrow(jnp.concatenate([residual_high, residual_low, direction_low], axis=0), rest_ref)


def wide(packs):
    height = packs[0].shape[0] * 2 // 3
    side = LANES // 2
    tails = [
        jnp.concatenate([pack[height:, :side], pack[height:, side:]], axis=0) for pack in packs
    ]
    return jnp.concatenate(
        [pack[:height] for pack in packs]
        + [jnp.concatenate(tails[index : index + 2], axis=1) for index in (0, 2)],
        axis=1,
    )


def read(*refs):
    return wide([ref[index] for ref in refs for index in range(ref.shape[0])])


def widened(points, own):
    values = points.astype(jnp.float32)
    half = -0.5 * jnp.sum(values * values, axis=0, keepdims=True)
    high = half.astype(jnp.bfloat16).astype(jnp.float32)
    middle = (half - high).astype(jnp.bfloat16).astype(jnp.float32)
    low = half - high - middle
    row = lax.broadcasted_iota(jnp.int32, (16, points.shape[1]), 0)
    base = 0 if own else 3
    extra = jnp.where(row < 6, 1.0, 0.0)
    extra = jnp.where(row == base, high, extra)
    extra = jnp.where(row == base + 1, middle, extra)
    extra = jnp.where(row == base + 2, low, extra)
    return jnp.concatenate([points, extra.astype(jnp.bfloat16)], axis=0)


def fold(own, piece, applied, dim):
    half = lax.dot_general(
        widened(piece[:dim], False),
        widened(own[:dim], True),
        (((0,), (0,)), ((), ())),
        preferred_element_type=jnp.float32,
    )
    kernel = jnp.exp2(half * RATE + SHIFT).astype(jnp.bfloat16)
    part = lax.dot_general(
        piece[dim:], kernel, (((1,), (0,)), ((), ())), preferred_element_type=jnp.float32
    )
    return part if applied is None else applied + part


def first_fold_kernel(dim, own_ref, beside_ref, rest_ref, applied_ref):
    del beside_ref, rest_ref
    own = read(own_ref)
    applied_ref[...] = fold(own, own, None, dim)


def fold_kernel(dim, own_ref, piece_ref, before_ref, applied_ref):
    applied_ref[...] = fold(read(own_ref), read(piece_ref), before_ref[...], dim)


def join_kernel(first_ref, second_ref, after_ref, joined_ref):
    del after_ref
    count = first_ref.shape[0]
    joined_ref[:count] = first_ref[...]
    joined_ref[count:] = second_ref[...]


def long_fold_kernel(dim, own_ref, piece_ref, before_ref, applied_ref):
    @pl.when(pl.program_id(0) == 0)
    def _():
        applied_ref[...] = before_ref[...]

    applied_ref[...] = fold(read(own_ref), read(piece_ref), applied_ref[...], dim)


def sums_kernel(dim, own_ref, rest_ref, other_rest_ref, applied_ref, sums_ref):
    rest = read(rest_ref, other_rest_ref).astype(jnp.float32)
    probes = rest.shape[0] // 3
    residual = rest[:probes] + rest[probes : 2 * probes]
    direction = read(own_ref)[dim:].astype(jnp.float32) + rest[2 * probes :]
    image = applied_ref[...] + noise_level * direction
    lane = lax.broadcasted_iota(jnp.int32, (image.shape[0], LANES), 1)
    table = jnp.zeros((image.shape[0], LANES), jnp.float32)
    products = (residual * residual, direction * image, residual * image, image * image)
    for index, product in enumerate(products):
        table = jnp.where(lane == index, jnp.sum(product, axis=1, keepdims=True), table)
    sums_ref[...] = table.T[:8]


def last_kernel(dim, own_ref, piece_ref, before_ref, rest_ref, other_rest_ref, applied_ref, sums_ref):
    fold_kernel(dim, own_ref, piece_ref, before_ref, applied_ref)
    sums_kernel(dim, own_ref, rest_ref, other_rest_ref, applied_ref, sums_ref)


def call(kernel, outs, args, folds=0):
    columns, dim, probes = 768, 80, 32
    cost = None
    if folds:
        count = folds * columns * columns
        cost = pl.CostEstimate(
            flops=2 * count * (dim + probes), bytes_accessed=count, transcendentals=count
        )
    return pl.pallas_call(
        kernel,
        out_shape=outs,
        in_specs=[in_vmem()] * len(args),
        out_specs=jax.tree.map(lambda _: in_vmem(), outs),
        compiler_params=pltpu.CompilerParams(vmem_limit_bytes=VMEM_BYTES),
        cost_estimate=cost,
    )(*args)


def pack(points, direction, residual):
    rows = points.shape[0] + direction.shape[0]
    shape = jax.ShapeDtypeStruct((1, rows * 3 // 2, LANES), jnp.bfloat16)
    args = (points, direction, residual)
    return pl.pallas_call(
        pack_kernel,
        out_shape=(shape, shape),
        in_specs=[pl.BlockSpec(memory_space=pltpu.HBM)] * 3,
        out_specs=(in_vmem(), in_vmem()),
        scratch_shapes=[pltpu.VMEM(a.shape, a.dtype) for a in args] + [pltpu.SemaphoreType.DMA((3,))],
        compiler_params=pltpu.CompilerParams(vmem_limit_bytes=PACK_VMEM_BYTES),
    )(*args)


def add_fold(own, piece, before, dim):
    if piece.shape[0] == 4:
        full = jax.ShapeDtypeStruct(before.shape, before.dtype)
        return call(functools.partial(fold_kernel, dim), full, (own, piece, before), 1)
    whole = lambda index: (0, 0)
    return pl.pallas_call(
        functools.partial(long_fold_kernel, dim),
        grid=(piece.shape[0] // 4,),
        out_shape=jax.ShapeDtypeStruct(before.shape, before.dtype),
        in_specs=[
            pl.BlockSpec(own.shape, lambda index: (0, 0, 0)),
            pl.BlockSpec((4, *piece.shape[1:]), lambda index: (index, 0, 0)),
            pl.BlockSpec(before.shape, whole),
        ],
        out_specs=pl.BlockSpec(before.shape, whole),
        compiler_params=pltpu.CompilerParams(vmem_limit_bytes=VMEM_BYTES),
    )(own, piece, before)


def strides(count):
    found = []
    while count > 1:
        assert count % 2 == 0
        count //= 2
        found.append(count)
    return found


def swapped(array, count, stride):
    return lax.ppermute(array, AXES, [(i, i ^ stride) for i in range(count)])


def make_body(count):
    far, middle, near, *others, cores = strides(count)

    def body(points, direction, residual, solution):
        dim, width = points.shape
        probes = direction.shape[0]
        full = jax.ShapeDtypeStruct((probes, 4 * width), jnp.float32)
        table = jax.ShapeDtypeStruct((8, probes), jnp.float32)
        main, rest = pack(points, direction, residual)
        pair = jnp.concatenate([main, swapped(main, count, far)], axis=0)
        rest = jnp.concatenate([rest, swapped(rest, count, far)], axis=0)
        other = swapped(pair, count, middle)
        beside = swapped(pair, count, near)
        other_rest = swapped(rest, count, middle)
        own = jnp.concatenate([pair, other], axis=0)
        other_beside = swapped(other, count, near)
        crossed = swapped(own, count, cores)
        applied = call(functools.partial(first_fold_kernel, dim), full, (own, beside, rest), 1)
        applied = add_fold(own, crossed, applied, dim)
        beside = call(
            join_kernel,
            jax.ShapeDtypeStruct(own.shape, own.dtype),
            (beside, other_beside, applied),
        )
        blocks = [own, beside]
        for stride in others:
            blocks.append(swapped(jnp.concatenate(blocks, axis=0), count, stride))
        for block in blocks[1:]:
            crossed = swapped(block, count, cores)
            applied = add_fold(own, block, applied, dim)
            if block is not blocks[-1]:
                applied = add_fold(own, crossed, applied, dim)
        if crossed.shape[0] == 4:
            applied, sums = call(
                functools.partial(last_kernel, dim),
                (full, table),
                (own, crossed, applied, rest, other_rest),
                1,
            )
        else:
            applied = add_fold(own, crossed, applied, dim)
            sums = call(
                functools.partial(sums_kernel, dim), table, (own, rest, other_rest, applied)
            )
        for stride in (cores, *reversed(others), near):
            sums = sums + swapped(sums, count, stride)
        start = 4 * LANES
        applied = jnp.concatenate([applied[:, :LANES], applied[:, start : start + width - LANES]], axis=1)
        image = applied + noise_level * direction
        old_norm, curvature, cross, image_norm = sums[0], sums[1], sums[2], sums[3]
        step_size = old_norm / curvature
        solution_next = solution + step_size[:, None] * direction
        residual_next = residual - step_size[:, None] * image
        new_norm = old_norm + step_size * (step_size * image_norm - 2.0 * cross)
        direction_next = residual_next + (new_norm / (old_norm + 1e-06))[:, None] * direction
        return (solution_next, residual_next, direction_next)

    return body


def solution(mesh):
    placed = P(None, ("groups", "row", "col"))
    return jax.shard_map(
        make_body(mesh.shape["row"] * mesh.shape["col"]),
        mesh=mesh,
        in_specs=(placed,) * 4,
        out_specs=(placed,) * 3,
        check_vma=False,
    )
```

time: 30.5 us -> 31.9 us (1.046)
  starting transfers between devices: 8.65 us -> 14.2 us
  waiting for transfers between devices: 14.8 us -> 10.2 us
  Pallas kernels: 2.97 us -> 4.88 us
  local copies, waits for them, and re-layouts: 2.28 us -> 0.87 us
    ppermute x6 -> x10, starting transfers between devices: 8.65 us -> 14.2 us  [swapped(): return lax.ppermute(array, AXES, [(i, i ^ stride) for i in range(count)])]
    ppermute x6 -> x10, waiting for transfers between devices: 14.8 us -> 10.2 us  [swapped(): return lax.ppermute(array, AXES, [(i, i ^ stride) for i in range(count)])]
    pallas_call x0 -> x1, Pallas kernels: none -> 1.52 us  [pack(): pl.pallas_call(pack_kernel, out_shape=(shape, shape), in_specs=[pl.BlockS...]
    unnamed x12 -> x10, local copies, waits for them, and re-layouts: 2.28 us -> 0.83 us
    pallas_call x5, Pallas kernels: 2.97 us -> 3.36 us  [call(): pl.pallas_call(kernel, out_shape=outs, in_specs=[in_vmem()] * len(args),...]
  transfers between devices with their start and end apart: 6 -> 10, of which waited for: 6 -> 6; matrix products, arithmetic and copies ran while one was open for 0% -> 3% of each run, Pallas kernels for 4% -> 8%
where the time goes in v3:
time: 31.9 us; the launch traced here: 31.6 us
  starting transfers between devices  14.2 us (45%)
  waiting for transfers between devices  10.2 us (32%)
  Pallas kernels  4.88 us (15%)
  local copies, waits for them, and re-layouts  0.87 us (3%)
  other arithmetic  0.73 us (2%)
  between operations  0.73 us (2%)
    ppermute x10, starting transfers between devices, swapped(): return lax.ppermute(array, AXES, [(i, i ^ stride) for i in range(count)])  14.2 us
    ppermute x10, waiting for transfers between devices, swapped(): return lax.ppermute(array, AXES, [(i, i ^ stride) for i in range(count)])  10.2 us
    pallas_call x5, Pallas kernels, call(): pl.pallas_call(kernel, out_shape=outs, in_specs=[in_vmem()] * len(args),...  3.36 us
    pallas_call x1, Pallas kernels, pack(): pl.pallas_call(pack_kernel, out_shape=(shape, shape), in_specs=[pl.BlockS...  1.52 us
    unnamed x10, local copies, waits for them, and re-layouts  0.83 us
    add x1, other arithmetic, body(): residual_next + (new_norm / (old_norm + 1e-06))[:, None] * direction  0.71 us
  transfers between devices with their start and end apart: 10, of which 6 were waited for; matrix products, arithmetic and copies ran while one was open for 3% of the time, Pallas kernels for 8%

profile of v3, /device:TPU:0, one launch (start us, length us, event | category | flops | bytes accessed | tf_op | source)
XLA Modules:
  0.0 31.6 jit_solution(7598060504855875701)
XLA Ops:
  0.6 1.5 %shard_map.67 = (bf16[1,144,128]{2,1,0:T(8,128)(2,1)}, bf16[1,144,128]{2,1,0:T(8,128)(2,1)}) custom-call(bf16[64,192]{1,0:T(8,128)(2,1)} %points_hbm.1, f32[32,192]{1,0:T(8,128)} %direction_hbm.1, f32[32,192]{1,0:T(8,128)} %residual_hbm.1), custom_call_target="tpu_custom_call" | custom-call | tf_op jit(solution)/shard_map/pallas_call | solution.py:175
  2.2 4.1 %collective-permute-start = (bf16[1,144,128]{2,1,0:T(8,128)(2,1)}, bf16[1,144,128]{2,1,0:T(8,128)(2,1)S(1)}, u32[]{:S(2)}, u32[]{:S(2)}) collective-permute-start(bf16[1,144,128]{2,1,0:T(8,128)(2,1)} %get-tuple-element.7), channel_id=1, source_target_pairs={{0,8},{1,9},{2,10},{3,11},{4,12},{5,13},{6,14},{7,15},{8,0},{9,1},... | collective-permute-start | bytes 110600 | tf_op jit(solution)/shard_map/ppermute | solution.py:214
  6.3 0.8 %constant_dynamic-update-slice_fusion.1 = (bf16[2,144,128]{2,1,0:T(8,128)(2,1)S(1)}, bf16[4,144,128]{2,1,0:T(8,128)(2,1)S(1)}) fusion(bf16[1,144,128]{2,1,0:T(8,128)(2,1)} %get-tuple-element.7), kind=kLoop, calls=%fused_computation.6 | loop fusion | bytes 110592
  7.1 1.7 %collective-permute-done = bf16[1,144,128]{2,1,0:T(8,128)(2,1)S(1)} collective-permute-done((bf16[1,144,128]{2,1,0:T(8,128)(2,1)}, bf16[1,144,128]{2,1,0:T(8,128)(2,1)S(1)}, u32[]{:S(2)}, u32[]{:S(2)}) %collective-permute-start) | collective-permute-done | bytes 36896 | tf_op jit(solution)/shard_map/ppermute | solution.py:214
  8.8 1.6 %collective-permute-start.1 = (bf16[2,144,128]{2,1,0:T(8,128)(2,1)S(1)}, bf16[2,144,128]{2,1,0:T(8,128)(2,1)S(1)}, u32[]{:S(2)}, u32[]{:S(2)}) collective-permute-start(bf16[2,144,128]{2,1,0:T(8,128)(2,1)S(1)} %get-tuple-element.15), channel_id=1, source_target_pairs={{0,4},{1,5},{2,6},{3,7},{4,0},{5,1},{6,2},{7,3},{8,12},{9,13},{10,... | collective-permute-start | bytes 221192 | tf_op jit(solution)/shard_map/ppermute | solution.py:214
  10.4 0.0 copy-done.2
  10.4 2.9 %collective-permute-start.5 = (bf16[1,144,128]{2,1,0:T(8,128)(2,1)S(1)}, bf16[1,144,128]{2,1,0:T(8,128)(2,1)S(1)}, u32[]{:S(2)}, u32[]{:S(2)}) collective-permute-start(bf16[1,144,128]{2,1,0:T(8,128)(2,1)S(1)} %copy-done.2), channel_id=1, source_target_pairs={{0,8},{1,9},{2,10},{3,11},{4,12},{5,13},{6,14},{7,15},{8,0},{9,1},... | collective-permute-start | bytes 110600 | tf_op jit(solution)/shard_map/ppermute | solution.py:214
  13.3 0.4 %collective-permute-done.1 = bf16[2,144,128]{2,1,0:T(8,128)(2,1)S(1)} collective-permute-done((bf16[2,144,128]{2,1,0:T(8,128)(2,1)S(1)}, bf16[2,144,128]{2,1,0:T(8,128)(2,1)S(1)}, u32[]{:S(2)}, u32[]{:S(2)}) %collective-permute-start.1) | collective-permute-done | bytes 73760 | tf_op jit(solution)/shard_map/ppermute | solution.py:214
  13.6 0.1 collective-permute-start.4
  13.7 1.6 %collective-permute-start.2 = (bf16[2,144,128]{2,1,0:T(8,128)(2,1)S(1)}, bf16[2,144,128]{2,1,0:T(8,128)(2,1)S(1)}, u32[]{:S(2)}, u32[]{:S(2)}) collective-permute-start(bf16[2,144,128]{2,1,0:T(8,128)(2,1)S(1)} %get-tuple-element.15), channel_id=1, source_target_pairs={{0,2},{1,3},{2,0},{3,1},{4,6},{5,7},{6,4},{7,5},{8,10},{9,11},{10,... | collective-permute-start | bytes 221192 | tf_op jit(solution)/shard_map/ppermute | solution.py:214
  15.4 0.5 %collective-permute-start.3 = (bf16[2,144,128]{2,1,0:T(8,128)(2,1)S(1)}, bf16[2,144,128]{2,1,0:T(8,128)(2,1)S(1)}, u32[]{:S(2)}, u32[]{:S(2)}) collective-permute-start(bf16[2,144,128]{2,1,0:T(8,128)(2,1)S(1)} %collective-permute-done.1), channel_id=1, source_target_pairs={{0,2},{1,3},{2,0},{3,1},{4,6},{5,7},{6,4},{7,5},{8,10},{9,11},{10,... | collective-permute-start | bytes 221192 | tf_op jit(solution)/shard_map/ppermute | solution.py:214
  15.8 0.0 collective-permute-done.5
  15.8 2.9 %collective-permute-done.2.beside_ref.first_ref = bf16[2,144,128]{2,1,0:T(8,128)(2,1)S(1)} collective-permute-done((bf16[2,144,128]{2,1,0:T(8,128)(2,1)S(1)}, bf16[2,144,128]{2,1,0:T(8,128)(2,1)S(1)}, u32[]{:S(2)}, u32[]{:S(2)}) %collective-permute-start.2) | collective-permute-done | bytes 73760 | tf_op jit(solution)/shard_map/ppermute | solution.py:214
  18.7 0.8 %shard_map.68.before_ref = f32[32,768]{1,0:T(8,128)S(1)} custom-call(bf16[4,144,128]{2,1,0:T(8,128)(2,1)S(1)} %constant_dynamic-update-slice_fusion.2.own_ref, bf16[2,144,128]{2,1,0:T(8,128)(2,1)S(1)} %collective-permute-done.2.beside_ref.first_ref, bf16[2,144,128]{2,1,0:T(8,128)(2,1)S(1)} %constant_dynamic-update-slice_fusion.5.rest_ref), custom_call_target="tpu_custom_call" | custom-call | flops 132120576 | bytes 589824 | tf_op jit(solution)/shard_map/pallas_call | solution.py:161
  19.5 0.0 collective-permute-done.4.piece_ref
  19.5 0.8 %shard_map.69.after_ref.before_ref = f32[32,768]{1,0:T(8,128)S(1)} custom-call(bf16[4,144,128]{2,1,0:T(8,128)(2,1)S(1)} %constant_dynamic-update-slice_fusion.2.own_ref, bf16[4,144,128]{2,1,0:T(8,128)(2,1)S(1)} %collective-permute-done.4.piece_ref, f32[32,768]{1,0:T(8,128)S(1)} %shard_map.68.before_ref), custom_call_target="tpu_custom_call" | custom-call | flops 132120576 | bytes 589824 | tf_op jit(solution)/shard_map/pallas_call | solution.py:161
  20.3 0.0 collective-permute-done.3.second_ref
  20.3 0.1 collective-permute-start.6
  20.4 1.7 %collective-permute-start.7 = (bf16[2,144,128]{2,1,0:T(8,128)(2,1)S(1)}, bf16[2,144,128]{2,1,0:T(8,128)(2,1)S(1)}, u32[]{:S(2)}, u32[]{:S(2)}) collective-permute-start(bf16[2,144,128]{2,1,0:T(8,128)(2,1)S(1)} %constant_dynamic-update-slice_fusion.5.rest_ref), channel_id=1, source_target_pairs={{0,4},{1,5},{2,6},{3,7},{4,0},{5,1},{6,2},{7,3},{8,12},{9,13},{10,... | collective-permute-start | bytes 221192 | tf_op jit(solution)/shard_map/ppermute | solution.py:214
  22.1 0.8 %shard_map.71.before_ref = f32[32,768]{1,0:T(8,128)S(1)} custom-call(bf16[4,144,128]{2,1,0:T(8,128)(2,1)S(1)} %constant_dynamic-update-slice_fusion.2.own_ref, bf16[4,144,128]{2,1,0:T(8,128)(2,1)S(1)} %shard_map.70.piece_ref, f32[32,768]{1,0:T(8,128)S(1)} %shard_map.69.after_ref.before_ref), custom_call_target="tpu_custom_call" | custom-call | flops 132120576 | bytes 589824 | tf_op jit(solution)/shard_map/pallas_call | solution.py:161
  22.9 2.2 %collective-permute-done.7.other_rest_ref = bf16[2,144,128]{2,1,0:T(8,128)(2,1)S(1)} collective-permute-done((bf16[2,144,128]{2,1,0:T(8,128)(2,1)S(1)}, bf16[2,144,128]{2,1,0:T(8,128)(2,1)S(1)}, u32[]{:S(2)}, u32[]{:S(2)}) %collective-permute-start.7) | collective-permute-done | bytes 73760 | tf_op jit(solution)/shard_map/ppermute | solution.py:214
  25.1 0.0 collective-permute-done.6.piece_ref
  25.1 0.0 copy-start.3
  25.1 1.0 %shard_map.72 = (f32[32,768]{1,0:T(8,128)S(1)}, f32[8,32]{1,0:T(8,128)S(1)}) custom-call(bf16[4,144,128]{2,1,0:T(8,128)(2,1)S(1)} %constant_dynamic-update-slice_fusion.2.own_ref, bf16[4,144,128]{2,1,0:T(8,128)(2,1)S(1)} %collective-permute-done.6.piece_ref, f32[32,768]{1,0:T(8,128)S(1)} %shard_map.71.before_ref, ...), custom_call_target="tpu_custom_call" | custom-call | flops 132120576 | bytes 589824 | tf_op jit(solution)/shard_map/pallas_call | solution.py:161
  26.1 0.0 collective-permute-start.8
  26.1 1.2 %collective-permute-done.8 = f32[8,32]{1,0:T(8,128)S(1)} collective-permute-done((f32[8,32]{1,0:T(8,128)S(1)}, f32[8,32]{1,0:T(8,128)S(1)}, u32[]{:S(2)}, u32[]{:S(2)}) %collective-permute-start.8) | collective-permute-done | bytes 1056 | tf_op jit(solution)/shard_map/ppermute | solution.py:214
  27.3 1.7 %collective-permute-start.9 = (f32[8,32]{1,0:T(8,128)S(1)}, f32[8,32]{1,0:T(8,128)S(1)}, u32[]{:S(2)}, u32[]{:S(2)}) collective-permute-start(f32[8,32]{1,0:T(8,128)S(1)} %add.32), channel_id=1, source_target_pairs={{0,2},{1,3},{2,0},{3,1},{4,6},{5,7},{6,4},{7,5},{8,10},{9,11},{10,... | collective-permute-start | bytes 3080 | tf_op jit(solution)/shard_map/ppermute | solution.py:214
  29.0 1.9 %collective-permute-done.9 = f32[8,32]{1,0:T(8,128)S(1)} collective-permute-done((f32[8,32]{1,0:T(8,128)S(1)}, f32[8,32]{1,0:T(8,128)S(1)}, u32[]{:S(2)}, u32[]{:S(2)}) %collective-permute-start.9) | collective-permute-done | bytes 1056 | tf_op jit(solution)/shard_map/ppermute | solution.py:214
  30.9 0.0 copy-done.3
  30.9 0.0 copy-done.1
  30.9 0.0 copy-done
  30.9 0.7 %multiply_add_fusion = (f32[32,192]{1,0:T(8,128)}, f32[32,192]{1,0:T(8,128)}, f32[32,192]{1,0:T(8,128)}) fusion(f32[32,192]{1,0:T(8,128)S(1)} %copy-done, f32[32]{0:T(128)S(1)} %get-tuple-element.13, f32[32,192]{1,0:T(8,128)S(1)} %copy-done.1, f32[32,64]{1,0:T(8,128)S(1)} %slice.21, f32[32,128]{1,0:T(8,128)S(1)} %slice.20, f32[32]{0:T(128)S(1)} %get-tuple-element.14, ...), kind=kLoop, calls=%fused_computation.3 | loop fusion | flops 55296 | bytes 172288 | tf_op jit(solution)/shard_map/add | solution.py:271
  (13 shorter events, 0.1 us)
Async XLA Ops:
  2.2 6.6 %collective-permute-start = (bf16[1,144,128]{2,1,0:T(8,128)(2,1)}, bf16[1,144,128]{2,1,0:T(8,128)(2,1)S(1)}, u32[]{:S(2)}, u32[]{:S(2)}) collective-permute-start(bf16[1,144,128]{2,1,0:T(8,128)(2,1)} %get-tuple-element.7), channel_id=1, source_target_pairs={{0,8},{1,9},{2,10},{3,11},{4,12},{5,13},{6,14},{7,15},{8,0},{9,1},... | collective-permute-start | bytes 110600 | tf_op jit(solution)/shard_map/ppermute | solution.py:214
  8.8 1.6 %copy-start.2 = (bf16[1,144,128]{2,1,0:T(8,128)(2,1)S(1)}, bf16[1,144,128]{2,1,0:T(8,128)(2,1)}, u32[]{:S(2)}) copy-start(bf16[1,144,128]{2,1,0:T(8,128)(2,1)} %get-tuple-element.8) | copy-start | bytes 110596
  8.8 4.8 %collective-permute-start.1 = (bf16[2,144,128]{2,1,0:T(8,128)(2,1)S(1)}, bf16[2,144,128]{2,1,0:T(8,128)(2,1)S(1)}, u32[]{:S(2)}, u32[]{:S(2)}) collective-permute-start(bf16[2,144,128]{2,1,0:T(8,128)(2,1)S(1)} %get-tuple-element.15), channel_id=1, source_target_pairs={{0,4},{1,5},{2,6},{3,7},{4,0},{5,1},{6,2},{7,3},{8,12},{9,13},{10,... | collective-permute-start | bytes 221192 | tf_op jit(solution)/shard_map/ppermute | solution.py:214
  10.4 5.4 %collective-permute-start.5 = (bf16[1,144,128]{2,1,0:T(8,128)(2,1)S(1)}, bf16[1,144,128]{2,1,0:T(8,128)(2,1)S(1)}, u32[]{:S(2)}, u32[]{:S(2)}) collective-permute-start(bf16[1,144,128]{2,1,0:T(8,128)(2,1)S(1)} %copy-done.2), channel_id=1, source_target_pairs={{0,8},{1,9},{2,10},{3,11},{4,12},{5,13},{6,14},{7,15},{8,0},{9,1},... | collective-permute-start | bytes 110600 | tf_op jit(solution)/shard_map/ppermute | solution.py:214
  13.6 5.9 %collective-permute-start.4 = (bf16[4,144,128]{2,1,0:T(8,128)(2,1)S(1)}, bf16[4,144,128]{2,1,0:T(8,128)(2,1)S(1)}, u32[]{:S(2)}, u32[]{:S(2)}) collective-permute-start(bf16[4,144,128]{2,1,0:T(8,128)(2,1)S(1)} %constant_dynamic-update-slice_fusion.2.own_ref), channel_id=1, source_target_pairs={{0,1},{1,0},{2,3},{3,2},{4,5},{5,4},{6,7},{7,6},{8,9},{9,8},{10,11... | collective-permute-start | bytes 442376 | tf_op jit(solution)/shard_map/ppermute | solution.py:214
  13.7 5.0 %collective-permute-start.2 = (bf16[2,144,128]{2,1,0:T(8,128)(2,1)S(1)}, bf16[2,144,128]{2,1,0:T(8,128)(2,1)S(1)}, u32[]{:S(2)}, u32[]{:S(2)}) collective-permute-start(bf16[2,144,128]{2,1,0:T(8,128)(2,1)S(1)} %get-tuple-element.15), channel_id=1, source_target_pairs={{0,2},{1,3},{2,0},{3,1},{4,6},{5,7},{6,4},{7,5},{8,10},{9,11},{10,... | collective-permute-start | bytes 221192 | tf_op jit(solution)/shard_map/ppermute | solution.py:214
  15.4 4.9 %collective-permute-start.3 = (bf16[2,144,128]{2,1,0:T(8,128)(2,1)S(1)}, bf16[2,144,128]{2,1,0:T(8,128)(2,1)S(1)}, u32[]{:S(2)}, u32[]{:S(2)}) collective-permute-start(bf16[2,144,128]{2,1,0:T(8,128)(2,1)S(1)} %collective-permute-done.1), channel_id=1, source_target_pairs={{0,2},{1,3},{2,0},{3,1},{4,6},{5,7},{6,4},{7,5},{8,10},{9,11},{10,... | collective-permute-start | bytes 221192 | tf_op jit(solution)/shard_map/ppermute | solution.py:214
  20.3 4.8 %collective-permute-start.6 = (bf16[4,144,128]{2,1,0:T(8,128)(2,1)S(1)}, bf16[4,144,128]{2,1,0:T(8,128)(2,1)S(1)}, u32[]{:S(2)}, u32[]{:S(2)}) collective-permute-start(bf16[4,144,128]{2,1,0:T(8,128)(2,1)S(1)} %shard_map.70.piece_ref), channel_id=1, source_target_pairs={{0,1},{1,0},{2,3},{3,2},{4,5},{5,4},{6,7},{7,6},{8,9},{9,8},{10,11... | collective-permute-start | bytes 442376 | tf_op jit(solution)/shard_map/ppermute | solution.py:214
  20.4 4.7 %collective-permute-start.7 = (bf16[2,144,128]{2,1,0:T(8,128)(2,1)S(1)}, bf16[2,144,128]{2,1,0:T(8,128)(2,1)S(1)}, u32[]{:S(2)}, u32[]{:S(2)}) collective-permute-start(bf16[2,144,128]{2,1,0:T(8,128)(2,1)S(1)} %constant_dynamic-update-slice_fusion.5.rest_ref), channel_id=1, source_target_pairs={{0,4},{1,5},{2,6},{3,7},{4,0},{5,1},{6,2},{7,3},{8,12},{9,13},{10,... | collective-permute-start | bytes 221192 | tf_op jit(solution)/shard_map/ppermute | solution.py:214
  25.1 5.8 %copy-start.3 = (f32[32,192]{1,0:T(8,128)S(1)}, f32[32,192]{1,0:T(8,128)}, u32[]{:S(2)}) copy-start(f32[32,192]{1,0:T(8,128)} %param.7) | copy-start | bytes 73732
  26.1 1.2 %collective-permute-start.8 = (f32[8,32]{1,0:T(8,128)S(1)}, f32[8,32]{1,0:T(8,128)S(1)}, u32[]{:S(2)}, u32[]{:S(2)}) collective-permute-start(f32[8,32]{1,0:T(8,128)S(1)} %get-tuple-element.9), channel_id=1, source_target_pairs={{0,1},{1,0},{2,3},{3,2},{4,5},{5,4},{6,7},{7,6},{8,9},{9,8},{10,11... | collective-permute-start | bytes 3080 | tf_op jit(solution)/shard_map/ppermute | solution.py:214
  27.3 3.6 %collective-permute-start.9 = (f32[8,32]{1,0:T(8,128)S(1)}, f32[8,32]{1,0:T(8,128)S(1)}, u32[]{:S(2)}, u32[]{:S(2)}) collective-permute-start(f32[8,32]{1,0:T(8,128)S(1)} %add.32), channel_id=1, source_target_pairs={{0,2},{1,3},{2,0},{3,1},{4,6},{5,7},{6,4},{7,5},{8,10},{9,11},{10,... | collective-permute-start | bytes 3080 | tf_op jit(solution)/shard_map/ppermute | solution.py:214
  29.0 1.9 %copy-start.1 = (f32[32,192]{1,0:T(8,128)S(1)}, f32[32,192]{1,0:T(8,128)}, u32[]{:S(2)}) copy-start(f32[32,192]{1,0:T(8,128)} %residual_hbm.1) | copy-start | bytes 73732
  29.0 1.9 %copy-start = (f32[32,192]{1,0:T(8,128)S(1)}, f32[32,192]{1,0:T(8,128)}, u32[]{:S(2)}) copy-start(f32[32,192]{1,0:T(8,128)} %direction_hbm.1) | copy-start | bytes 73732

commit v4 on v3

--- a/solution.py
+++ b/solution.py
@@ -15,7 +15,6 @@
 AXES = ("row", "col")
 LANES = 128
 VMEM_BYTES = 32 << 20
-PACK_VMEM_BYTES = 63 << 20
 RATE = math.log2(math.e) / length_square
 SHIFT = math.log2(amplitude)
 
@@ -24,21 +23,8 @@
     return pl.BlockSpec(memory_space=pltpu.VMEM)
 
 
-def halves(values):
-    high = values.astype(jnp.bfloat16)
-    return high, (values - high.astype(jnp.float32)).astype(jnp.bfloat16)
-
-
-def narrow(fields, out_ref):
-    height = fields.shape[0]
-    out_ref[0, :height] = fields[:, :LANES]
-    out_ref[0, height:] = jnp.concatenate(
-        [fields[: height // 2, LANES:], fields[height // 2 :, LANES:]], axis=1
-    )
-
-
 def pack_kernel(
-    points_hbm, direction_hbm, residual_hbm, main_ref, rest_ref, points_ref, direction_ref, residual_ref, arrived
+    points_hbm, direction_hbm, residual_hbm, packed_ref, points_ref, direction_ref, residual_ref, arrived
 ):
     copies = [
         pltpu.make_async_copy(source, target, arrived.at[index])
@@ -54,27 +40,41 @@
         copy.start()
     for copy in copies:
         copy.wait()
-    direction_high, direction_low = halves(direction_ref[...])
-    residual_high, residual_low = halves(residual_ref[...])
-    narrow(jnp.concatenate([points_ref[...], direction_high], axis=0), main_ref)
-    narrow(jnp.concatenate([residual_high, residual_low, direction_low], axis=0), rest_ref)
-
-
-def wide(packs):
-    height = packs[0].shape[0] * 2 // 3
+    fields = jnp.concatenate(
+        [
+            points_ref[...],
+            direction_ref[...].astype(jnp.bfloat16),
+            residual_ref[...].astype(jnp.bfloat16),
+        ],
+        axis=0,
+    )
+    height = fields.shape[0]
+    packed_ref[0, :height] = fields[:, :LANES]
+    packed_ref[0, height:] = jnp.concatenate(
+        [fields[: height // 2, LANES:], fields[height // 2 :, LANES:]], axis=1
+    )
+
+
+def unpack_kernel(packs_ref, held_ref, residual_ref):
+    height = packs_ref.shape[1] * 2 // 3
     side = LANES // 2
-    tails = [
-        jnp.concatenate([pack[height:, :side], pack[height:, side:]], axis=0) for pack in packs
-    ]
-    return jnp.concatenate(
-        [pack[:height] for pack in packs]
-        + [jnp.concatenate(tails[index : index + 2], axis=1) for index in (0, 2)],
-        axis=1,
-    )
-
-
-def read(*refs):
-    return wide([ref[index] for ref in refs for index in range(ref.shape[0])])
+    first, second = packs_ref[0, height:], packs_ref[1, height:]
+    tails = jnp.concatenate(
+        [
+            jnp.concatenate([first[:, :side], second[:, :side]], axis=1),
+            jnp.concatenate([first[:, side:], second[:, side:]], axis=1),
+        ],
+        axis=0,
+    )
+    rows = held_ref.shape[1]
+    for index, part in enumerate((packs_ref[0, :height], packs_ref[1, :height], tails)):
+        span = slice(index * LANES, (index + 1) * LANES)
+        held_ref[0, :, span] = part[:rows]
+        residual_ref[:, span] = part[rows:].astype(jnp.float32)
+
+
+def read(ref):
+    return jnp.concatenate([ref[index] for index in range(ref.shape[0])], axis=1)
 
 
 def widened(points, own):
@@ -106,8 +106,7 @@
     return part if applied is None else applied + part
 
 
-def first_fold_kernel(dim, own_ref, beside_ref, rest_ref, applied_ref):
-    del beside_ref, rest_ref
+def first_fold_kernel(dim, own_ref, applied_ref):
     own = read(own_ref)
     applied_ref[...] = fold(own, own, None, dim)
 
@@ -116,11 +115,9 @@
     applied_ref[...] = fold(read(own_ref), read(piece_ref), before_ref[...], dim)
 
 
-def join_kernel(first_ref, second_ref, after_ref, joined_ref):
+def join_kernel(first_ref, after_ref, joined_ref):
     del after_ref
-    count = first_ref.shape[0]
-    joined_ref[:count] = first_ref[...]
-    joined_ref[count:] = second_ref[...]
+    joined_ref[...] = first_ref[...]
 
 
 def long_fold_kernel(dim, own_ref, piece_ref, before_ref, applied_ref):
@@ -131,11 +128,9 @@
     applied_ref[...] = fold(read(own_ref), read(piece_ref), applied_ref[...], dim)
 
 
-def sums_kernel(dim, own_ref, rest_ref, other_rest_ref, applied_ref, sums_ref):
-    rest = read(rest_ref, other_rest_ref).astype(jnp.float32)
-    probes = rest.shape[0] // 3
-    residual = rest[:probes] + rest[probes : 2 * probes]
-    direction = read(own_ref)[dim:].astype(jnp.float32) + rest[2 * probes :]
+def sums_kernel(dim, own_ref, residual_ref, other_residual_ref, applied_ref, sums_ref):
+    residual = jnp.concatenate([residual_ref[...], other_residual_ref[...]], axis=1)
+    direction = read(own_ref)[dim:].astype(jnp.float32)
     image = applied_ref[...] + noise_level * direction
     lane = lax.broadcasted_iota(jnp.int32, (image.shape[0], LANES), 1)
     table = jnp.zeros((image.shape[0], LANES), jnp.float32)
@@ -145,9 +140,9 @@
     sums_ref[...] = table.T[:8]
 
 
-def last_kernel(dim, own_ref, piece_ref, before_ref, rest_ref, other_rest_ref, applied_ref, sums_ref):
+def last_kernel(dim, own_ref, piece_ref, before_ref, residual_ref, other_residual_ref, applied_ref, sums_ref):
     fold_kernel(dim, own_ref, piece_ref, before_ref, applied_ref)
-    sums_kernel(dim, own_ref, rest_ref, other_rest_ref, applied_ref, sums_ref)
+    sums_kernel(dim, own_ref, residual_ref, other_residual_ref, applied_ref, sums_ref)
 
 
 def call(kernel, outs, args, folds=0):
@@ -169,31 +164,40 @@
 
 
 def pack(points, direction, residual):
-    rows = points.shape[0] + direction.shape[0]
-    shape = jax.ShapeDtypeStruct((1, rows * 3 // 2, LANES), jnp.bfloat16)
-    args = (points, direction, residual)
+    rows = points.shape[0] + direction.shape[0] + residual.shape[0]
+    shape = pltpu.VMEM((1, rows * 3 // 2, LANES), jnp.bfloat16)
+    args = [pltpu.with_memory_space_constraint(a, pltpu.HBM) for a in (points, direction, residual)]
     return pl.pallas_call(
         pack_kernel,
-        out_shape=(shape, shape),
+        out_shape=shape,
         in_specs=[pl.BlockSpec(memory_space=pltpu.HBM)] * 3,
-        out_specs=(in_vmem(), in_vmem()),
+        out_specs=in_vmem(),
         scratch_shapes=[pltpu.VMEM(a.shape, a.dtype) for a in args] + [pltpu.SemaphoreType.DMA((3,))],
-        compiler_params=pltpu.CompilerParams(vmem_limit_bytes=PACK_VMEM_BYTES),
+        compiler_params=pltpu.CompilerParams(vmem_limit_bytes=VMEM_BYTES),
     )(*args)
 
 
+def unpack(packs, dim, probes):
+    columns = 3 * LANES
+    outs = (
+        jax.ShapeDtypeStruct((1, dim + probes, columns), packs.dtype),
+        jax.ShapeDtypeStruct((probes, columns), jnp.float32),
+    )
+    return call(unpack_kernel, outs, (packs,))
+
+
 def add_fold(own, piece, before, dim):
-    if piece.shape[0] == 4:
+    if piece.shape[0] == 2:
         full = jax.ShapeDtypeStruct(before.shape, before.dtype)
         return call(functools.partial(fold_kernel, dim), full, (own, piece, before), 1)
     whole = lambda index: (0, 0)
     return pl.pallas_call(
         functools.partial(long_fold_kernel, dim),
-        grid=(piece.shape[0] // 4,),
+        grid=(piece.shape[0] // 2,),
         out_shape=jax.ShapeDtypeStruct(before.shape, before.dtype),
         in_specs=[
             pl.BlockSpec(own.shape, lambda index: (0, 0, 0)),
-            pl.BlockSpec((4, *piece.shape[1:]), lambda index: (index, 0, 0)),
+            pl.BlockSpec((2, *piece.shape[1:]), lambda index: (index, 0, 0)),
             pl.BlockSpec(before.shape, whole),
         ],
         out_specs=pl.BlockSpec(before.shape, whole),
@@ -222,21 +226,21 @@
         probes = direction.shape[0]
         full = jax.ShapeDtypeStruct((probes, 4 * width), jnp.float32)
         table = jax.ShapeDtypeStruct((8, probes), jnp.float32)
-        main, rest = pack(points, direction, residual)
-        pair = jnp.concatenate([main, swapped(main, count, far)], axis=0)
-        rest = jnp.concatenate([rest, swapped(rest, count, far)], axis=0)
+        packed = pack(points, direction, residual)
+        pair = jnp.concatenate([packed, swapped(packed, count, far)], axis=0)
         other = swapped(pair, count, middle)
-        beside = swapped(pair, count, near)
-        other_rest = swapped(rest, count, middle)
-        own = jnp.concatenate([pair, other], axis=0)
-        other_beside = swapped(other, count, near)
+        half, rest = unpack(pair, dim, probes)
+        other_half, other_rest = unpack(other, dim, probes)
+        own = jnp.concatenate([half, other_half], axis=0)
+        beside = swapped(half, count, near)
+        other_beside = swapped(other_half, count, near)
         crossed = swapped(own, count, cores)
-        applied = call(functools.partial(first_fold_kernel, dim), full, (own, beside, rest), 1)
+        applied = call(functools.partial(first_fold_kernel, dim), full, (own,), 1)
         applied = add_fold(own, crossed, applied, dim)
         beside = call(
             join_kernel,
             jax.ShapeDtypeStruct(own.shape, own.dtype),
-            (beside, other_beside, applied),
+            (jnp.concatenate([beside, other_beside], axis=0), applied),
         )
         blocks = [own, beside]
         for stride in others:
@@ -246,7 +250,7 @@
             applied = add_fold(own, block, applied, dim)
             if block is not blocks[-1]:
                 applied = add_fold(own, crossed, applied, dim)
-        if crossed.shape[0] == 4:
+        if crossed.shape[0] == 2:
             applied, sums = call(
                 functools.partial(last_kernel, dim),
                 (full, table),
@@ -260,7 +264,7 @@
             )
         for stride in (cores, *reversed(others), near):
             sums = sums + swapped(sums, count, stride)
-        start = 4 * LANES
+        start = 2 * LANES
         applied = jnp.concatenate([applied[:, :LANES], applied[:, start : start + width - LANES]], axis=1)
         image = applied + noise_level * direction
         old_norm, curvature, cross, image_norm = sums[0], sums[1], sums[2], sums[3]

time: 31.9 us -> 26.1 us (0.82)
  starting transfers between devices: 14.2 us -> 10.8 us
  Pallas kernels: 4.88 us -> 3.94 us
  local copies, waits for them, and re-layouts: 0.87 us -> 0.04 us
  waiting for transfers between devices: 10.2 us -> 9.7 us
    ppermute x10 -> x8, starting transfers between devices: 14.2 us -> 10.8 us  [swapped(): return lax.ppermute(array, AXES, [(i, i ^ stride) for i in range(count)])]
    unnamed x10 -> x7, local copies, waits for them, and re-layouts: 0.83 us -> 0.02 us
    pallas_call x1, Pallas kernels: 1.52 us -> 0.89 us  [pack(): pl.pallas_call(pack_kernel, out_shape=shape, in_specs=[pl.BlockSpec(memor...]
    ppermute x10 -> x8, waiting for transfers between devices: 10.2 us -> 9.7 us  [swapped(): return lax.ppermute(array, AXES, [(i, i ^ stride) for i in range(count)])]
    pallas_call x5 -> x7, Pallas kernels: 3.36 us -> 3.05 us  [call(): pl.pallas_call(kernel, out_shape=outs, in_specs=[in_vmem()] * len(args),...]
  transfers between devices with their start and end apart: 10 -> 8, of which waited for: 6 -> 6; matrix products, arithmetic and copies ran while one was open for 3% -> 0% of each run, Pallas kernels for 8% -> 6%
where the time goes in v4:
time: 26.1 us; the launch traced here: 25.9 us
  starting transfers between devices  10.8 us (41%)
  waiting for transfers between devices  9.7 us (37%)
  Pallas kernels  3.94 us (15%)
  other arithmetic  0.77 us (3%)
  between operations  0.72 us (3%)
    ppermute x8, starting transfers between devices, swapped(): return lax.ppermute(array, AXES, [(i, i ^ stride) for i in range(count)])  10.8 us
    ppermute x8, waiting for transfers between devices, swapped(): return lax.ppermute(array, AXES, [(i, i ^ stride) for i in range(count)])  9.7 us
    pallas_call x7, Pallas kernels, call(): pl.pallas_call(kernel, out_shape=outs, in_specs=[in_vmem()] * len(args),...  3.05 us
    pallas_call x1, Pallas kernels, pack(): pl.pallas_call(pack_kernel, out_shape=shape, in_specs=[pl.BlockSpec(memor...  0.89 us
    add x1, other arithmetic, body(): residual_next + (new_norm / (old_norm + 1e-06))[:, None] * direction  0.71 us
  transfers between devices with their start and end apart: 8, of which 6 were waited for; matrix products, arithmetic and copies ran while one was open for 0% of the time, Pallas kernels for 6%

profile of v4, /device:TPU:0, one launch (start us, length us, event | category | flops | bytes accessed | tf_op | source)
XLA Modules:
  0.0 25.9 jit_solution(14999395708055028966)
XLA Ops:
  0.6 0.9 %shard_map.67 = bf16[1,192,128]{2,1,0:T(8,128)(2,1)S(1)} custom-call(bf16[64,192]{1,0:T(8,128)(2,1)} %points_hbm.1, f32[32,192]{1,0:T(8,128)} %direction_hbm.1, f32[32,192]{1,0:T(8,128)} %residual_hbm.1), custom_call_target="tpu_custom_call" | custom-call | tf_op jit(solution)/shard_map/pallas_call | solution.py:170
  1.5 4.1 %collective-permute-start = (bf16[1,192,128]{2,1,0:T(8,128)(2,1)S(1)}, bf16[1,192,128]{2,1,0:T(8,128)(2,1)S(1)}, u32[]{:S(2)}, u32[]{:S(2)}) collective-permute-start(bf16[1,192,128]{2,1,0:T(8,128)(2,1)S(1)} %shard_map.67), channel_id=1, source_target_pairs={{0,8},{1,9},{2,10},{3,11},{4,12},{5,13},{6,14},{7,15},{8,0},{9,1},... | collective-permute-start | bytes 147464 | tf_op jit(solution)/shard_map/ppermute | solution.py:218
  5.6 2.6 %collective-permute-done = bf16[1,192,128]{2,1,0:T(8,128)(2,1)S(1)} collective-permute-done((bf16[1,192,128]{2,1,0:T(8,128)(2,1)S(1)}, bf16[1,192,128]{2,1,0:T(8,128)(2,1)S(1)}, u32[]{:S(2)}, u32[]{:S(2)}) %collective-permute-start) | collective-permute-done | bytes 49184 | tf_op jit(solution)/shard_map/ppermute | solution.py:218
  8.2 1.4 %collective-permute-start.1 = (bf16[2,192,128]{2,1,0:T(8,128)(2,1)S(1)}, bf16[2,192,128]{2,1,0:T(8,128)(2,1)S(1)}, u32[]{:S(2)}, u32[]{:S(2)}) collective-permute-start(bf16[2,192,128]{2,1,0:T(8,128)(2,1)S(1)} %pad_maximum_fusion.1.packs_ref), channel_id=1, source_target_pairs={{0,4},{1,5},{2,6},{3,7},{4,0},{5,1},{6,2},{7,3},{8,12},{9,13},{10,... | collective-permute-start | bytes 294920 | tf_op jit(solution)/shard_map/ppermute | solution.py:218
  9.7 0.1 shard_map.68
  9.8 1.5 %collective-permute-start.2 = (bf16[1,96,384]{2,1,0:T(8,128)(2,1)S(1)}, bf16[1,96,384]{2,1,0:T(8,128)(2,1)S(1)}, u32[]{:S(2)}, u32[]{:S(2)}) collective-permute-start(bf16[1,96,384]{2,1,0:T(8,128)(2,1)S(1)} %get-tuple-element.9), channel_id=1, source_target_pairs={{0,2},{1,3},{2,0},{3,1},{4,6},{5,7},{6,4},{7,5},{8,10},{9,11},{10,... | collective-permute-start | bytes 221192 | tf_op jit(solution)/shard_map/ppermute | solution.py:218
  11.3 1.6 %collective-permute-done.1.packs_ref = bf16[2,192,128]{2,1,0:T(8,128)(2,1)S(1)} collective-permute-done((bf16[2,192,128]{2,1,0:T(8,128)(2,1)S(1)}, bf16[2,192,128]{2,1,0:T(8,128)(2,1)S(1)}, u32[]{:S(2)}, u32[]{:S(2)}) %collective-permute-start.1) | collective-permute-done | bytes 98336 | tf_op jit(solution)/shard_map/ppermute | solution.py:218
  12.9 0.1 shard_map.69
  13.0 1.7 %collective-permute-start.3 = (bf16[1,96,384]{2,1,0:T(8,128)(2,1)S(1)}, bf16[1,96,384]{2,1,0:T(8,128)(2,1)S(1)}, u32[]{:S(2)}, u32[]{:S(2)}) collective-permute-start(bf16[1,96,384]{2,1,0:T(8,128)(2,1)S(1)} %get-tuple-element.10), channel_id=1, source_target_pairs={{0,2},{1,3},{2,0},{3,1},{4,6},{5,7},{6,4},{7,5},{8,10},{9,11},{10,... | collective-permute-start | bytes 221192 | tf_op jit(solution)/shard_map/ppermute | solution.py:218
  14.7 0.1 collective-permute-start.4
  14.8 0.7 %shard_map.70.before_ref = f32[32,768]{1,0:T(8,128)S(1)} custom-call(bf16[2,96,384]{2,1,0:T(8,128)(2,1)S(1)} %constant_dynamic-update-slice_fusion.own_ref), custom_call_target="tpu_custom_call" | custom-call | flops 132120576 | bytes 589824 | tf_op jit(solution)/shard_map/pallas_call | solution.py:156
  15.5 0.0 collective-permute-done.2
  15.5 1.9 %collective-permute-done.3 = bf16[1,96,384]{2,1,0:T(8,128)(2,1)S(1)} collective-permute-done((bf16[1,96,384]{2,1,0:T(8,128)(2,1)S(1)}, bf16[1,96,384]{2,1,0:T(8,128)(2,1)S(1)}, u32[]{:S(2)}, u32[]{:S(2)}) %collective-permute-start.3) | collective-permute-done | bytes 73760 | tf_op jit(solution)/shard_map/ppermute | solution.py:218
  17.4 0.0 collective-permute-done.4.piece_ref
  17.4 0.7 %shard_map.71.after_ref.before_ref = f32[32,768]{1,0:T(8,128)S(1)} custom-call(bf16[2,96,384]{2,1,0:T(8,128)(2,1)S(1)} %constant_dynamic-update-slice_fusion.own_ref, bf16[2,96,384]{2,1,0:T(8,128)(2,1)S(1)} %collective-permute-done.4.piece_ref, f32[32,768]{1,0:T(8,128)S(1)} %shard_map.70.before_ref), custom_call_target="tpu_custom_call" | custom-call | flops 132120576 | bytes 589824 | tf_op jit(solution)/shard_map/pallas_call | solution.py:156
  18.1 0.1 collective-permute-start.5
  18.2 0.7 %shard_map.73.before_ref = f32[32,768]{1,0:T(8,128)S(1)} custom-call(bf16[2,96,384]{2,1,0:T(8,128)(2,1)S(1)} %constant_dynamic-update-slice_fusion.own_ref, bf16[2,96,384]{2,1,0:T(8,128)(2,1)S(1)} %shard_map.72.piece_ref, f32[32,768]{1,0:T(8,128)S(1)} %shard_map.71.after_ref.before_ref), custom_call_target="tpu_custom_call" | custom-call | flops 132120576 | bytes 589824 | tf_op jit(solution)/shard_map/pallas_call | solution.py:156
  18.9 0.7 %collective-permute-done.5.piece_ref = bf16[2,96,384]{2,1,0:T(8,128)(2,1)S(1)} collective-permute-done((bf16[2,96,384]{2,1,0:T(8,128)(2,1)S(1)}, bf16[2,96,384]{2,1,0:T(8,128)(2,1)S(1)}, u32[]{:S(2)}, u32[]{:S(2)}) %collective-permute-start.5) | collective-permute-done | bytes 147488 | tf_op jit(solution)/shard_map/ppermute | solution.py:218
  19.6 0.0 copy-start.2
  19.6 0.8 %shard_map.74 = (f32[32,768]{1,0:T(8,128)S(1)}, f32[8,32]{1,0:T(8,128)S(1)}) custom-call(bf16[2,96,384]{2,1,0:T(8,128)(2,1)S(1)} %constant_dynamic-update-slice_fusion.own_ref, bf16[2,96,384]{2,1,0:T(8,128)(2,1)S(1)} %collective-permute-done.5.piece_ref, f32[32,768]{1,0:T(8,128)S(1)} %shard_map.73.before_ref, f32[32,384]{1,0:T(8,128)S(1)} %get-tuple-element.11.residual_ref, ...), custom_call_target="tpu_custom_call" | custom-call | flops 132120576 | bytes 589824 | tf_op jit(solution)/shard_map/pallas_call | solution.py:156
  20.4 0.2 collective-permute-start.6
  20.6 1.0 %collective-permute-done.6 = f32[8,32]{1,0:T(8,128)S(1)} collective-permute-done((f32[8,32]{1,0:T(8,128)S(1)}, f32[8,32]{1,0:T(8,128)S(1)}, u32[]{:S(2)}, u32[]{:S(2)}) %collective-permute-start.6) | collective-permute-done | bytes 1056 | tf_op jit(solution)/shard_map/ppermute | solution.py:218
  21.6 1.7 %collective-permute-start.7 = (f32[8,32]{1,0:T(8,128)S(1)}, f32[8,32]{1,0:T(8,128)S(1)}, u32[]{:S(2)}, u32[]{:S(2)}) collective-permute-start(f32[8,32]{1,0:T(8,128)S(1)} %add.32), channel_id=1, source_target_pairs={{0,2},{1,3},{2,0},{3,1},{4,6},{5,7},{6,4},{7,5},{8,10},{9,11},{10,... | collective-permute-start | bytes 3080 | tf_op jit(solution)/shard_map/ppermute | solution.py:218
  23.3 0.0 copy-start.1
  23.3 0.0 copy-start
  23.3 1.9 %collective-permute-done.7 = f32[8,32]{1,0:T(8,128)S(1)} collective-permute-done((f32[8,32]{1,0:T(8,128)S(1)}, f32[8,32]{1,0:T(8,128)S(1)}, u32[]{:S(2)}, u32[]{:S(2)}) %collective-permute-start.7) | collective-permute-done | bytes 1056 | tf_op jit(solution)/shard_map/ppermute | solution.py:218
  25.2 0.0 copy-done.2
  25.2 0.0 copy-done.1
  25.2 0.0 copy-done
  25.2 0.7 %multiply_add_fusion = (f32[32,192]{1,0:T(8,128)}, f32[32,192]{1,0:T(8,128)}, f32[32,192]{1,0:T(8,128)}) fusion(f32[32,192]{1,0:T(8,128)S(1)} %copy-done, f32[32]{0:T(128)S(1)} %get-tuple-element.17, f32[32,192]{1,0:T(8,128)S(1)} %copy-done.1, f32[32,64]{1,0:T(8,128)S(1)} %slice.21, f32[32,128]{1,0:T(8,128)S(1)} %slice.20, f32[32]{0:T(128)S(1)} %get-tuple-element.18, ...), kind=kLoop, calls=%fused_computation.5 | loop fusion | flops 55296 | bytes 172288 | tf_op jit(solution)/shard_map/add | solution.py:275
  (10 shorter events, 0.1 us)
Async XLA Ops:
  1.5 6.7 %collective-permute-start = (bf16[1,192,128]{2,1,0:T(8,128)(2,1)S(1)}, bf16[1,192,128]{2,1,0:T(8,128)(2,1)S(1)}, u32[]{:S(2)}, u32[]{:S(2)}) collective-permute-start(bf16[1,192,128]{2,1,0:T(8,128)(2,1)S(1)} %shard_map.67), channel_id=1, source_target_pairs={{0,8},{1,9},{2,10},{3,11},{4,12},{5,13},{6,14},{7,15},{8,0},{9,1},... | collective-permute-start | bytes 147464 | tf_op jit(solution)/shard_map/ppermute | solution.py:218
  8.2 4.7 %collective-permute-start.1 = (bf16[2,192,128]{2,1,0:T(8,128)(2,1)S(1)}, bf16[2,192,128]{2,1,0:T(8,128)(2,1)S(1)}, u32[]{:S(2)}, u32[]{:S(2)}) collective-permute-start(bf16[2,192,128]{2,1,0:T(8,128)(2,1)S(1)} %pad_maximum_fusion.1.packs_ref), channel_id=1, source_target_pairs={{0,4},{1,5},{2,6},{3,7},{4,0},{5,1},{6,2},{7,3},{8,12},{9,13},{10,... | collective-permute-start | bytes 294920 | tf_op jit(solution)/shard_map/ppermute | solution.py:218
  9.8 5.7 %collective-permute-start.2 = (bf16[1,96,384]{2,1,0:T(8,128)(2,1)S(1)}, bf16[1,96,384]{2,1,0:T(8,128)(2,1)S(1)}, u32[]{:S(2)}, u32[]{:S(2)}) collective-permute-start(bf16[1,96,384]{2,1,0:T(8,128)(2,1)S(1)} %get-tuple-element.9), channel_id=1, source_target_pairs={{0,2},{1,3},{2,0},{3,1},{4,6},{5,7},{6,4},{7,5},{8,10},{9,11},{10,... | collective-permute-start | bytes 221192 | tf_op jit(solution)/shard_map/ppermute | solution.py:218
  13.0 4.4 %collective-permute-start.3 = (bf16[1,96,384]{2,1,0:T(8,128)(2,1)S(1)}, bf16[1,96,384]{2,1,0:T(8,128)(2,1)S(1)}, u32[]{:S(2)}, u32[]{:S(2)}) collective-permute-start(bf16[1,96,384]{2,1,0:T(8,128)(2,1)S(1)} %get-tuple-element.10), channel_id=1, source_target_pairs={{0,2},{1,3},{2,0},{3,1},{4,6},{5,7},{6,4},{7,5},{8,10},{9,11},{10,... | collective-permute-start | bytes 221192 | tf_op jit(solution)/shard_map/ppermute | solution.py:218
  14.7 2.7 %collective-permute-start.4 = (bf16[2,96,384]{2,1,0:T(8,128)(2,1)S(1)}, bf16[2,96,384]{2,1,0:T(8,128)(2,1)S(1)}, u32[]{:S(2)}, u32[]{:S(2)}) collective-permute-start(bf16[2,96,384]{2,1,0:T(8,128)(2,1)S(1)} %constant_dynamic-update-slice_fusion.own_ref), channel_id=1, source_target_pairs={{0,1},{1,0},{2,3},{3,2},{4,5},{5,4},{6,7},{7,6},{8,9},{9,8},{10,11... | collective-permute-start | bytes 442376 | tf_op jit(solution)/shard_map/ppermute | solution.py:218
  18.1 1.4 %collective-permute-start.5 = (bf16[2,96,384]{2,1,0:T(8,128)(2,1)S(1)}, bf16[2,96,384]{2,1,0:T(8,128)(2,1)S(1)}, u32[]{:S(2)}, u32[]{:S(2)}) collective-permute-start(bf16[2,96,384]{2,1,0:T(8,128)(2,1)S(1)} %shard_map.72.piece_ref), channel_id=1, source_target_pairs={{0,1},{1,0},{2,3},{3,2},{4,5},{5,4},{6,7},{7,6},{8,9},{9,8},{10,11... | collective-permute-start | bytes 442376 | tf_op jit(solution)/shard_map/ppermute | solution.py:218
  19.6 5.6 %copy-start.2 = (f32[32,192]{1,0:T(8,128)S(1)}, f32[32,192]{1,0:T(8,128)}, u32[]{:S(2)}) copy-start(f32[32,192]{1,0:T(8,128)} %param.7) | copy-start | bytes 73732
  20.4 1.2 %collective-permute-start.6 = (f32[8,32]{1,0:T(8,128)S(1)}, f32[8,32]{1,0:T(8,128)S(1)}, u32[]{:S(2)}, u32[]{:S(2)}) collective-permute-start(f32[8,32]{1,0:T(8,128)S(1)} %get-tuple-element.13), channel_id=1, source_target_pairs={{0,1},{1,0},{2,3},{3,2},{4,5},{5,4},{6,7},{7,6},{8,9},{9,8},{10,11... | collective-permute-start | bytes 3080 | tf_op jit(solution)/shard_map/ppermute | solution.py:218
  21.6 3.6 %collective-permute-start.7 = (f32[8,32]{1,0:T(8,128)S(1)}, f32[8,32]{1,0:T(8,128)S(1)}, u32[]{:S(2)}, u32[]{:S(2)}) collective-permute-start(f32[8,32]{1,0:T(8,128)S(1)} %add.32), channel_id=1, source_target_pairs={{0,2},{1,3},{2,0},{3,1},{4,6},{5,7},{6,4},{7,5},{8,10},{9,11},{10,... | collective-permute-start | bytes 3080 | tf_op jit(solution)/shard_map/ppermute | solution.py:218
  23.3 1.9 %copy-start.1 = (f32[32,192]{1,0:T(8,128)S(1)}, f32[32,192]{1,0:T(8,128)}, u32[]{:S(2)}) copy-start(f32[32,192]{1,0:T(8,128)} %residual_hbm.1) | copy-start | bytes 73732
  23.3 1.9 %copy-start = (f32[32,192]{1,0:T(8,128)S(1)}, f32[32,192]{1,0:T(8,128)}, u32[]{:S(2)}) copy-start(f32[32,192]{1,0:T(8,128)} %direction_hbm.1) | copy-start | bytes 73732

commit v5 on v4

--- a/solution.py
+++ b/solution.py
@@ -115,9 +115,11 @@
     applied_ref[...] = fold(read(own_ref), read(piece_ref), before_ref[...], dim)
 
 
-def join_kernel(first_ref, after_ref, joined_ref):
+def join_kernel(first_ref, second_ref, after_ref, joined_ref):
     del after_ref
-    joined_ref[...] = first_ref[...]
+    count = first_ref.shape[0]
+    joined_ref[:count] = first_ref[...]
+    joined_ref[count:] = second_ref[...]
 
 
 def long_fold_kernel(dim, own_ref, piece_ref, before_ref, applied_ref):
@@ -233,15 +235,15 @@
         other_half, other_rest = unpack(other, dim, probes)
         own = jnp.concatenate([half, other_half], axis=0)
         beside = swapped(half, count, near)
-        other_beside = swapped(other_half, count, near)
+        other_beside = swapped(half, count, near | middle)
         crossed = swapped(own, count, cores)
         applied = call(functools.partial(first_fold_kernel, dim), full, (own,), 1)
-        applied = add_fold(own, crossed, applied, dim)
         beside = call(
             join_kernel,
             jax.ShapeDtypeStruct(own.shape, own.dtype),
-            (jnp.concatenate([beside, other_beside], axis=0), applied),
+            (beside, other_beside, applied),
         )
+        applied = add_fold(own, crossed, applied, dim)
         blocks = [own, beside]
         for stride in others:
             blocks.append(swapped(jnp.concatenate(blocks, axis=0), count, stride))

time: 26.1 us -> 24.7 us (0.946)
  starting transfers between devices: 10.8 us -> 8.79 us
  waiting for transfers between devices: 9.7 us -> 10.3 us
    ppermute x8, starting transfers between devices: 10.8 us -> 8.79 us  [swapped(): return lax.ppermute(array, AXES, [(i, i ^ stride) for i in range(count)])]
    ppermute x8, waiting for transfers between devices: 9.7 us -> 10.3 us  [swapped(): return lax.ppermute(array, AXES, [(i, i ^ stride) for i in range(count)])]
    pallas_call x7 -> x6, Pallas kernels: 3.05 us -> 2.97 us  [call(): pl.pallas_call(kernel, out_shape=outs, in_specs=[in_vmem()] * len(args),...]
  transfers between devices with their start and end apart: 8 -> 8, of which waited for: 6 -> 5; matrix products, arithmetic and copies ran while one was open for 0% -> 0% of each run, Pallas kernels for 6% -> 8%
where the time goes in v5:
time: 24.7 us; the launch traced here: 24.5 us
  waiting for transfers between devices  10.3 us (42%)
  starting transfers between devices  8.79 us (36%)
  Pallas kernels  3.86 us (16%)
  other arithmetic  0.75 us (3%)
  between operations  0.72 us (3%)
    ppermute x8, waiting for transfers between devices, swapped(): return lax.ppermute(array, AXES, [(i, i ^ stride) for i in range(count)])  10.3 us
    ppermute x8, starting transfers between devices, swapped(): return lax.ppermute(array, AXES, [(i, i ^ stride) for i in range(count)])  8.79 us
    pallas_call x6, Pallas kernels, call(): pl.pallas_call(kernel, out_shape=outs, in_specs=[in_vmem()] * len(args),...  2.97 us
    pallas_call x1, Pallas kernels, pack(): pl.pallas_call(pack_kernel, out_shape=shape, in_specs=[pl.BlockSpec(memor...  0.89 us
    add x1, other arithmetic, body(): residual_next + (new_norm / (old_norm + 1e-06))[:, None] * direction  0.71 us
  transfers between devices with their start and end apart: 8, of which 5 were waited for; matrix products, arithmetic and copies ran while one was open for 0% of the time, Pallas kernels for 8%

profile of v5, /device:TPU:0, one launch (start us, length us, event | category | flops | bytes accessed | tf_op | source)
XLA Modules:
  0.0 24.5 jit_solution(10306357256503359232)
XLA Ops:
  0.6 0.9 %shard_map.67 = bf16[1,192,128]{2,1,0:T(8,128)(2,1)S(1)} custom-call(bf16[64,192]{1,0:T(8,128)(2,1)} %points_hbm.1, f32[32,192]{1,0:T(8,128)} %direction_hbm.1, f32[32,192]{1,0:T(8,128)} %residual_hbm.1), custom_call_target="tpu_custom_call" | custom-call | tf_op jit(solution)/shard_map/pallas_call | solution.py:172
  1.5 4.1 %collective-permute-start = (bf16[1,192,128]{2,1,0:T(8,128)(2,1)S(1)}, bf16[1,192,128]{2,1,0:T(8,128)(2,1)S(1)}, u32[]{:S(2)}, u32[]{:S(2)}) collective-permute-start(bf16[1,192,128]{2,1,0:T(8,128)(2,1)S(1)} %shard_map.67), channel_id=1, source_target_pairs={{0,8},{1,9},{2,10},{3,11},{4,12},{5,13},{6,14},{7,15},{8,0},{9,1},... | collective-permute-start | bytes 147464 | tf_op jit(solution)/shard_map/ppermute | solution.py:220
  5.6 2.6 %collective-permute-done = bf16[1,192,128]{2,1,0:T(8,128)(2,1)S(1)} collective-permute-done((bf16[1,192,128]{2,1,0:T(8,128)(2,1)S(1)}, bf16[1,192,128]{2,1,0:T(8,128)(2,1)S(1)}, u32[]{:S(2)}, u32[]{:S(2)}) %collective-permute-start) | collective-permute-done | bytes 49184 | tf_op jit(solution)/shard_map/ppermute | solution.py:220
  8.2 0.1 shard_map.68
  8.3 1.4 %collective-permute-start.1 = (bf16[2,192,128]{2,1,0:T(8,128)(2,1)S(1)}, bf16[2,192,128]{2,1,0:T(8,128)(2,1)S(1)}, u32[]{:S(2)}, u32[]{:S(2)}) collective-permute-start(bf16[2,192,128]{2,1,0:T(8,128)(2,1)S(1)} %pad_maximum_fusion.packs_ref), channel_id=1, source_target_pairs={{0,4},{1,5},{2,6},{3,7},{4,0},{5,1},{6,2},{7,3},{8,12},{9,13},{10,... | collective-permute-start | bytes 294920 | tf_op jit(solution)/shard_map/ppermute | solution.py:220
  9.7 1.5 %collective-permute-start.2 = (bf16[1,96,384]{2,1,0:T(8,128)(2,1)S(1)}, bf16[1,96,384]{2,1,0:T(8,128)(2,1)S(1)}, u32[]{:S(2)}, u32[]{:S(2)}) collective-permute-start(bf16[1,96,384]{2,1,0:T(8,128)(2,1)S(1)} %get-tuple-element.9), channel_id=1, source_target_pairs={{0,2},{1,3},{2,0},{3,1},{4,6},{5,7},{6,4},{7,5},{8,10},{9,11},{10,... | collective-permute-start | bytes 221192 | tf_op jit(solution)/shard_map/ppermute | solution.py:220
  11.2 0.6 %collective-permute-start.3 = (bf16[1,96,384]{2,1,0:T(8,128)(2,1)S(1)}, bf16[1,96,384]{2,1,0:T(8,128)(2,1)S(1)}, u32[]{:S(2)}, u32[]{:S(2)}) collective-permute-start(bf16[1,96,384]{2,1,0:T(8,128)(2,1)S(1)} %get-tuple-element.9), channel_id=1, source_target_pairs={{0,6},{1,7},{2,4},{3,5},{4,2},{5,3},{6,0},{7,1},{8,14},{9,15},{10,... | collective-permute-start | bytes 221192 | tf_op jit(solution)/shard_map/ppermute | solution.py:220
  11.9 1.9 %collective-permute-done.1 = bf16[2,192,128]{2,1,0:T(8,128)(2,1)S(1)} collective-permute-done((bf16[2,192,128]{2,1,0:T(8,128)(2,1)S(1)}, bf16[2,192,128]{2,1,0:T(8,128)(2,1)S(1)}, u32[]{:S(2)}, u32[]{:S(2)}) %collective-permute-start.1) | collective-permute-done | bytes 98336 | tf_op jit(solution)/shard_map/ppermute | solution.py:220
  13.8 0.1 shard_map.74
  13.8 0.1 collective-permute-start.5
  13.9 0.7 %shard_map.69.after_ref.before_ref = f32[32,768]{1,0:T(8,128)S(1)} custom-call(bf16[2,96,384]{2,1,0:T(8,128)(2,1)S(1)} %get-tuple-element.17.own_ref), custom_call_target="tpu_custom_call" | custom-call | flops 132120576 | bytes 589824 | tf_op jit(solution)/shard_map/pallas_call | solution.py:158
  14.6 0.0 collective-permute-done.2.first_ref
  14.6 1.9 %collective-permute-done.3.second_ref = bf16[1,96,384]{2,1,0:T(8,128)(2,1)S(1)} collective-permute-done((bf16[1,96,384]{2,1,0:T(8,128)(2,1)S(1)}, bf16[1,96,384]{2,1,0:T(8,128)(2,1)S(1)}, u32[]{:S(2)}, u32[]{:S(2)}) %collective-permute-start.3) | collective-permute-done | bytes 73760 | tf_op jit(solution)/shard_map/ppermute | solution.py:220
  16.5 0.1 collective-permute-start.4
  16.6 0.0 collective-permute-done.5.piece_ref
  16.6 0.7 %shard_map.71.before_ref = f32[32,768]{1,0:T(8,128)S(1)} custom-call(bf16[2,96,384]{2,1,0:T(8,128)(2,1)S(1)} %get-tuple-element.17.own_ref, bf16[2,96,384]{2,1,0:T(8,128)(2,1)S(1)} %collective-permute-done.5.piece_ref, f32[32,768]{1,0:T(8,128)S(1)} %shard_map.69.after_ref.before_ref), custom_call_target="tpu_custom_call" | custom-call | flops 132120576 | bytes 589824 | tf_op jit(solution)/shard_map/pallas_call | solution.py:158
  17.3 0.7 %shard_map.72.before_ref = f32[32,768]{1,0:T(8,128)S(1)} custom-call(bf16[2,96,384]{2,1,0:T(8,128)(2,1)S(1)} %get-tuple-element.17.own_ref, bf16[2,96,384]{2,1,0:T(8,128)(2,1)S(1)} %shard_map.70.piece_ref, f32[32,768]{1,0:T(8,128)S(1)} %shard_map.71.before_ref), custom_call_target="tpu_custom_call" | custom-call | flops 132120576 | bytes 589824 | tf_op jit(solution)/shard_map/pallas_call | solution.py:158
  18.0 0.0 collective-permute-done.4.piece_ref
  18.0 0.0 copy-start.2
  18.0 0.8 %shard_map.73 = (f32[32,768]{1,0:T(8,128)S(1)}, f32[8,32]{1,0:T(8,128)S(1)}) custom-call(bf16[2,96,384]{2,1,0:T(8,128)(2,1)S(1)} %get-tuple-element.17.own_ref, bf16[2,96,384]{2,1,0:T(8,128)(2,1)S(1)} %collective-permute-done.4.piece_ref, f32[32,768]{1,0:T(8,128)S(1)} %shard_map.72.before_ref, f32[32,384]{1,0:T(8,128)S(1)} %get-tuple-element.11.residual_ref, ...), custom_call_target="tpu_custom_call" | custom-call | flops 132120576 | bytes 589824 | tf_op jit(solution)/shard_map/pallas_call | solution.py:158
  18.8 0.5 %collective-permute-start.6 = (f32[8,32]{1,0:T(8,128)S(1)}, f32[8,32]{1,0:T(8,128)S(1)}, u32[]{:S(2)}, u32[]{:S(2)}) collective-permute-start(f32[8,32]{1,0:T(8,128)S(1)} %get-tuple-element.13), channel_id=1, source_target_pairs={{0,1},{1,0},{2,3},{3,2},{4,5},{5,4},{6,7},{7,6},{8,9},{9,8},{10,11... | collective-permute-start | bytes 3080 | tf_op jit(solution)/shard_map/ppermute | solution.py:220
  19.3 0.8 %collective-permute-done.6 = f32[8,32]{1,0:T(8,128)S(1)} collective-permute-done((f32[8,32]{1,0:T(8,128)S(1)}, f32[8,32]{1,0:T(8,128)S(1)}, u32[]{:S(2)}, u32[]{:S(2)}) %collective-permute-start.6) | collective-permute-done | bytes 1056 | tf_op jit(solution)/shard_map/ppermute | solution.py:220
  20.1 0.5 %collective-permute-start.7 = (f32[8,32]{1,0:T(8,128)S(1)}, f32[8,32]{1,0:T(8,128)S(1)}, u32[]{:S(2)}, u32[]{:S(2)}) collective-permute-start(f32[8,32]{1,0:T(8,128)S(1)} %add.32), channel_id=1, source_target_pairs={{0,2},{1,3},{2,0},{3,1},{4,6},{5,7},{6,4},{7,5},{8,10},{9,11},{10,... | collective-permute-start | bytes 3080 | tf_op jit(solution)/shard_map/ppermute | solution.py:220
  20.7 0.0 copy-start.1
  20.7 0.0 copy-start
  20.7 3.1 %collective-permute-done.7 = f32[8,32]{1,0:T(8,128)S(1)} collective-permute-done((f32[8,32]{1,0:T(8,128)S(1)}, f32[8,32]{1,0:T(8,128)S(1)}, u32[]{:S(2)}, u32[]{:S(2)}) %collective-permute-start.7) | collective-permute-done | bytes 1056 | tf_op jit(solution)/shard_map/ppermute | solution.py:220
  23.8 0.0 copy-done.2
  23.8 0.0 copy-done.1
  23.8 0.0 copy-done
  23.8 0.7 %multiply_add_fusion = (f32[32,192]{1,0:T(8,128)}, f32[32,192]{1,0:T(8,128)}, f32[32,192]{1,0:T(8,128)}) fusion(f32[32,192]{1,0:T(8,128)S(1)} %copy-done, f32[32]{0:T(128)S(1)} %get-tuple-element.21, f32[32,192]{1,0:T(8,128)S(1)} %copy-done.1, f32[32,64]{1,0:T(8,128)S(1)} %slice.21, f32[32,128]{1,0:T(8,128)S(1)} %slice.20, f32[32]{0:T(128)S(1)} %get-tuple-element.22, ...), kind=kLoop, calls=%fused_computation.4 | loop fusion | flops 55296 | bytes 172288 | tf_op jit(solution)/shard_map/add | solution.py:277
  (8 shorter events, 0.1 us)
Async XLA Ops:
  1.5 6.7 %collective-permute-start = (bf16[1,192,128]{2,1,0:T(8,128)(2,1)S(1)}, bf16[1,192,128]{2,1,0:T(8,128)(2,1)S(1)}, u32[]{:S(2)}, u32[]{:S(2)}) collective-permute-start(bf16[1,192,128]{2,1,0:T(8,128)(2,1)S(1)} %shard_map.67), channel_id=1, source_target_pairs={{0,8},{1,9},{2,10},{3,11},{4,12},{5,13},{6,14},{7,15},{8,0},{9,1},... | collective-permute-start | bytes 147464 | tf_op jit(solution)/shard_map/ppermute | solution.py:220
  8.3 5.4 %collective-permute-start.1 = (bf16[2,192,128]{2,1,0:T(8,128)(2,1)S(1)}, bf16[2,192,128]{2,1,0:T(8,128)(2,1)S(1)}, u32[]{:S(2)}, u32[]{:S(2)}) collective-permute-start(bf16[2,192,128]{2,1,0:T(8,128)(2,1)S(1)} %pad_maximum_fusion.packs_ref), channel_id=1, source_target_pairs={{0,4},{1,5},{2,6},{3,7},{4,0},{5,1},{6,2},{7,3},{8,12},{9,13},{10,... | collective-permute-start | bytes 294920 | tf_op jit(solution)/shard_map/ppermute | solution.py:220
  9.7 4.9 %collective-permute-start.2 = (bf16[1,96,384]{2,1,0:T(8,128)(2,1)S(1)}, bf16[1,96,384]{2,1,0:T(8,128)(2,1)S(1)}, u32[]{:S(2)}, u32[]{:S(2)}) collective-permute-start(bf16[1,96,384]{2,1,0:T(8,128)(2,1)S(1)} %get-tuple-element.9), channel_id=1, source_target_pairs={{0,2},{1,3},{2,0},{3,1},{4,6},{5,7},{6,4},{7,5},{8,10},{9,11},{10,... | collective-permute-start | bytes 221192 | tf_op jit(solution)/shard_map/ppermute | solution.py:220
  11.2 5.3 %collective-permute-start.3 = (bf16[1,96,384]{2,1,0:T(8,128)(2,1)S(1)}, bf16[1,96,384]{2,1,0:T(8,128)(2,1)S(1)}, u32[]{:S(2)}, u32[]{:S(2)}) collective-permute-start(bf16[1,96,384]{2,1,0:T(8,128)(2,1)S(1)} %get-tuple-element.9), channel_id=1, source_target_pairs={{0,6},{1,7},{2,4},{3,5},{4,2},{5,3},{6,0},{7,1},{8,14},{9,15},{10,... | collective-permute-start | bytes 221192 | tf_op jit(solution)/shard_map/ppermute | solution.py:220
  13.8 2.7 %collective-permute-start.5 = (bf16[2,96,384]{2,1,0:T(8,128)(2,1)S(1)}, bf16[2,96,384]{2,1,0:T(8,128)(2,1)S(1)}, u32[]{:S(2)}, u32[]{:S(2)}) collective-permute-start(bf16[2,96,384]{2,1,0:T(8,128)(2,1)S(1)} %get-tuple-element.17.own_ref), channel_id=1, source_target_pairs={{0,1},{1,0},{2,3},{3,2},{4,5},{5,4},{6,7},{7,6},{8,9},{9,8},{10,11... | collective-permute-start | bytes 442376 | tf_op jit(solution)/shard_map/ppermute | solution.py:220
  16.5 1.5 %collective-permute-start.4 = (bf16[2,96,384]{2,1,0:T(8,128)(2,1)S(1)}, bf16[2,96,384]{2,1,0:T(8,128)(2,1)S(1)}, u32[]{:S(2)}, u32[]{:S(2)}) collective-permute-start(bf16[2,96,384]{2,1,0:T(8,128)(2,1)S(1)} %shard_map.70.piece_ref), channel_id=1, source_target_pairs={{0,1},{1,0},{2,3},{3,2},{4,5},{5,4},{6,7},{7,6},{8,9},{9,8},{10,11... | collective-permute-start | bytes 442376 | tf_op jit(solution)/shard_map/ppermute | solution.py:220
  18.0 5.8 %copy-start.2 = (f32[32,192]{1,0:T(8,128)S(1)}, f32[32,192]{1,0:T(8,128)}, u32[]{:S(2)}) copy-start(f32[32,192]{1,0:T(8,128)} %param.7) | copy-start | bytes 73732
  18.8 1.3 %collective-permute-start.6 = (f32[8,32]{1,0:T(8,128)S(1)}, f32[8,32]{1,0:T(8,128)S(1)}, u32[]{:S(2)}, u32[]{:S(2)}) collective-permute-start(f32[8,32]{1,0:T(8,128)S(1)} %get-tuple-element.13), channel_id=1, source_target_pairs={{0,1},{1,0},{2,3},{3,2},{4,5},{5,4},{6,7},{7,6},{8,9},{9,8},{10,11... | collective-permute-start | bytes 3080 | tf_op jit(solution)/shard_map/ppermute | solution.py:220
  20.1 3.6 %collective-permute-start.7 = (f32[8,32]{1,0:T(8,128)S(1)}, f32[8,32]{1,0:T(8,128)S(1)}, u32[]{:S(2)}, u32[]{:S(2)}) collective-permute-start(f32[8,32]{1,0:T(8,128)S(1)} %add.32), channel_id=1, source_target_pairs={{0,2},{1,3},{2,0},{3,1},{4,6},{5,7},{6,4},{7,5},{8,10},{9,11},{10,... | collective-permute-start | bytes 3080 | tf_op jit(solution)/shard_map/ppermute | solution.py:220
  20.7 3.1 %copy-start.1 = (f32[32,192]{1,0:T(8,128)S(1)}, f32[32,192]{1,0:T(8,128)}, u32[]{:S(2)}) copy-start(f32[32,192]{1,0:T(8,128)} %residual_hbm.1) | copy-start | bytes 73732
  20.7 3.1 %copy-start = (f32[32,192]{1,0:T(8,128)S(1)}, f32[32,192]{1,0:T(8,128)}, u32[]{:S(2)}) copy-start(f32[32,192]{1,0:T(8,128)} %direction_hbm.1) | copy-start | bytes 73732

commit v6 on v5

--- a/solution.py
+++ b/solution.py
@@ -264,8 +264,14 @@
             sums = call(
                 functools.partial(sums_kernel, dim), table, (own, rest, other_rest, applied)
             )
-        for stride in (cores, *reversed(others), near):
+        for stride in others:
             sums = sums + swapped(sums, count, stride)
+        sums = (
+            sums
+            + swapped(sums, count, near)
+            + swapped(sums, count, near | cores)
+            + swapped(sums, count, cores)
+        )
         start = 2 * LANES
         applied = jnp.concatenate([applied[:, :LANES], applied[:, start : start + width - LANES]], axis=1)
         image = applied + noise_level * direction

time: 24.7 us -> 23.4 us (0.947)
  waiting for transfers between devices: 10.3 us -> 7.86 us
  starting transfers between devices: 8.79 us -> 9.91 us
    ppermute x8 -> x9, waiting for transfers between devices: 10.3 us -> 7.86 us  [swapped(): return lax.ppermute(array, AXES, [(i, i ^ stride) for i in range(count)])]
    ppermute x8 -> x9, starting transfers between devices: 8.79 us -> 9.91 us  [swapped(): return lax.ppermute(array, AXES, [(i, i ^ stride) for i in range(count)])]
  transfers between devices with their start and end apart: 8 -> 9, of which waited for: 5 -> 4; matrix products, arithmetic and copies ran while one was open for 0% -> 0% of each run, Pallas kernels for 8% -> 9%
where the time goes in v6:
time: 23.4 us; the launch traced here: 23.2 us
  starting transfers between devices  9.91 us (42%)
  waiting for transfers between devices  7.86 us (34%)
  Pallas kernels  3.86 us (16%)
  other arithmetic  0.74 us (3%)
  between operations  0.73 us (3%)
    ppermute x9, starting transfers between devices, swapped(): return lax.ppermute(array, AXES, [(i, i ^ stride) for i in range(count)])  9.91 us
    ppermute x9, waiting for transfers between devices, swapped(): return lax.ppermute(array, AXES, [(i, i ^ stride) for i in range(count)])  7.86 us
    pallas_call x6, Pallas kernels, call(): pl.pallas_call(kernel, out_shape=outs, in_specs=[in_vmem()] * len(args),...  2.97 us
    pallas_call x1, Pallas kernels, pack(): pl.pallas_call(pack_kernel, out_shape=shape, in_specs=[pl.BlockSpec(memor...  0.89 us
    add x1, other arithmetic, body(): residual_next + (new_norm / (old_norm + 1e-06))[:, None] * direction  0.71 us
  transfers between devices with their start and end apart: 9, of which 4 were waited for; matrix products, arithmetic and copies ran while one was open for 0% of the time, Pallas kernels for 9%

profile of v6, /device:TPU:0, one launch (start us, length us, event | category | flops | bytes accessed | tf_op | source)
XLA Modules:
  0.0 23.2 jit_solution(15718730734796795837)
XLA Ops:
  0.6 0.9 %shard_map.67 = bf16[1,192,128]{2,1,0:T(8,128)(2,1)S(1)} custom-call(bf16[64,192]{1,0:T(8,128)(2,1)} %points_hbm.1, f32[32,192]{1,0:T(8,128)} %direction_hbm.1, f32[32,192]{1,0:T(8,128)} %residual_hbm.1), custom_call_target="tpu_custom_call" | custom-call | tf_op jit(solution)/shard_map/pallas_call | solution.py:172
  1.5 4.1 %collective-permute-start = (bf16[1,192,128]{2,1,0:T(8,128)(2,1)S(1)}, bf16[1,192,128]{2,1,0:T(8,128)(2,1)S(1)}, u32[]{:S(2)}, u32[]{:S(2)}) collective-permute-start(bf16[1,192,128]{2,1,0:T(8,128)(2,1)S(1)} %shard_map.67), channel_id=1, source_target_pairs={{0,8},{1,9},{2,10},{3,11},{4,12},{5,13},{6,14},{7,15},{8,0},{9,1},... | collective-permute-start | bytes 147464 | tf_op jit(solution)/shard_map/ppermute | solution.py:220
  5.6 2.6 %collective-permute-done = bf16[1,192,128]{2,1,0:T(8,128)(2,1)S(1)} collective-permute-done((bf16[1,192,128]{2,1,0:T(8,128)(2,1)S(1)}, bf16[1,192,128]{2,1,0:T(8,128)(2,1)S(1)}, u32[]{:S(2)}, u32[]{:S(2)}) %collective-permute-start) | collective-permute-done | bytes 49184 | tf_op jit(solution)/shard_map/ppermute | solution.py:220
  8.2 0.1 shard_map.68
  8.3 1.4 %collective-permute-start.1 = (bf16[2,192,128]{2,1,0:T(8,128)(2,1)S(1)}, bf16[2,192,128]{2,1,0:T(8,128)(2,1)S(1)}, u32[]{:S(2)}, u32[]{:S(2)}) collective-permute-start(bf16[2,192,128]{2,1,0:T(8,128)(2,1)S(1)} %pad_maximum_fusion.packs_ref), channel_id=1, source_target_pairs={{0,4},{1,5},{2,6},{3,7},{4,0},{5,1},{6,2},{7,3},{8,12},{9,13},{10,... | collective-permute-start | bytes 294920 | tf_op jit(solution)/shard_map/ppermute | solution.py:220
  9.7 1.5 %collective-permute-start.2 = (bf16[1,96,384]{2,1,0:T(8,128)(2,1)S(1)}, bf16[1,96,384]{2,1,0:T(8,128)(2,1)S(1)}, u32[]{:S(2)}, u32[]{:S(2)}) collective-permute-start(bf16[1,96,384]{2,1,0:T(8,128)(2,1)S(1)} %get-tuple-element.9), channel_id=1, source_target_pairs={{0,2},{1,3},{2,0},{3,1},{4,6},{5,7},{6,4},{7,5},{8,10},{9,11},{10,... | collective-permute-start | bytes 221192 | tf_op jit(solution)/shard_map/ppermute | solution.py:220
  11.2 0.6 %collective-permute-start.3 = (bf16[1,96,384]{2,1,0:T(8,128)(2,1)S(1)}, bf16[1,96,384]{2,1,0:T(8,128)(2,1)S(1)}, u32[]{:S(2)}, u32[]{:S(2)}) collective-permute-start(bf16[1,96,384]{2,1,0:T(8,128)(2,1)S(1)} %get-tuple-element.9), channel_id=1, source_target_pairs={{0,6},{1,7},{2,4},{3,5},{4,2},{5,3},{6,0},{7,1},{8,14},{9,15},{10,... | collective-permute-start | bytes 221192 | tf_op jit(solution)/shard_map/ppermute | solution.py:220
  11.9 1.9 %collective-permute-done.1 = bf16[2,192,128]{2,1,0:T(8,128)(2,1)S(1)} collective-permute-done((bf16[2,192,128]{2,1,0:T(8,128)(2,1)S(1)}, bf16[2,192,128]{2,1,0:T(8,128)(2,1)S(1)}, u32[]{:S(2)}, u32[]{:S(2)}) %collective-permute-start.1) | collective-permute-done | bytes 98336 | tf_op jit(solution)/shard_map/ppermute | solution.py:220
  13.8 0.1 shard_map.74
  13.8 0.1 collective-permute-start.5
  13.9 0.7 %shard_map.69.after_ref.before_ref = f32[32,768]{1,0:T(8,128)S(1)} custom-call(bf16[2,96,384]{2,1,0:T(8,128)(2,1)S(1)} %get-tuple-element.17.own_ref), custom_call_target="tpu_custom_call" | custom-call | flops 132120576 | bytes 589824 | tf_op jit(solution)/shard_map/pallas_call | solution.py:158
  14.6 0.0 collective-permute-done.2.first_ref
  14.6 1.9 %collective-permute-done.3.second_ref = bf16[1,96,384]{2,1,0:T(8,128)(2,1)S(1)} collective-permute-done((bf16[1,96,384]{2,1,0:T(8,128)(2,1)S(1)}, bf16[1,96,384]{2,1,0:T(8,128)(2,1)S(1)}, u32[]{:S(2)}, u32[]{:S(2)}) %collective-permute-start.3) | collective-permute-done | bytes 73760 | tf_op jit(solution)/shard_map/ppermute | solution.py:220
  16.5 0.1 collective-permute-start.4
  16.6 0.0 collective-permute-done.5.piece_ref
  16.6 0.7 %shard_map.71.before_ref = f32[32,768]{1,0:T(8,128)S(1)} custom-call(bf16[2,96,384]{2,1,0:T(8,128)(2,1)S(1)} %get-tuple-element.17.own_ref, bf16[2,96,384]{2,1,0:T(8,128)(2,1)S(1)} %collective-permute-done.5.piece_ref, f32[32,768]{1,0:T(8,128)S(1)} %shard_map.69.after_ref.before_ref), custom_call_target="tpu_custom_call" | custom-call | flops 132120576 | bytes 589824 | tf_op jit(solution)/shard_map/pallas_call | solution.py:158
  17.3 0.7 %shard_map.72.before_ref = f32[32,768]{1,0:T(8,128)S(1)} custom-call(bf16[2,96,384]{2,1,0:T(8,128)(2,1)S(1)} %get-tuple-element.17.own_ref, bf16[2,96,384]{2,1,0:T(8,128)(2,1)S(1)} %shard_map.70.piece_ref, f32[32,768]{1,0:T(8,128)S(1)} %shard_map.71.before_ref), custom_call_target="tpu_custom_call" | custom-call | flops 132120576 | bytes 589824 | tf_op jit(solution)/shard_map/pallas_call | solution.py:158
  18.0 0.0 collective-permute-done.4.piece_ref
  18.0 0.0 copy-start.2
  18.0 0.8 %shard_map.73 = (f32[32,768]{1,0:T(8,128)S(1)}, f32[8,32]{1,0:T(8,128)S(1)}) custom-call(bf16[2,96,384]{2,1,0:T(8,128)(2,1)S(1)} %get-tuple-element.17.own_ref, bf16[2,96,384]{2,1,0:T(8,128)(2,1)S(1)} %collective-permute-done.4.piece_ref, f32[32,768]{1,0:T(8,128)S(1)} %shard_map.72.before_ref, f32[32,384]{1,0:T(8,128)S(1)} %get-tuple-element.11.residual_ref, ...), custom_call_target="tpu_custom_call" | custom-call | flops 132120576 | bytes 589824 | tf_op jit(solution)/shard_map/pallas_call | solution.py:158
  18.8 0.6 %collective-permute-start.6 = (f32[8,32]{1,0:T(8,128)S(1)}, f32[8,32]{1,0:T(8,128)S(1)}, u32[]{:S(2)}, u32[]{:S(2)}) collective-permute-start(f32[8,32]{1,0:T(8,128)S(1)} %get-tuple-element.13), channel_id=1, source_target_pairs={{0,2},{1,3},{2,0},{3,1},{4,6},{5,7},{6,4},{7,5},{8,10},{9,11},{10,... | collective-permute-start | bytes 3080 | tf_op jit(solution)/shard_map/ppermute | solution.py:220
  19.4 1.3 %collective-permute-start.7 = (f32[8,32]{1,0:T(8,128)S(1)}, f32[8,32]{1,0:T(8,128)S(1)}, u32[]{:S(2)}, u32[]{:S(2)}) collective-permute-start(f32[8,32]{1,0:T(8,128)S(1)} %get-tuple-element.13), channel_id=1, source_target_pairs={{0,3},{1,2},{2,1},{3,0},{4,7},{5,6},{6,5},{7,4},{8,11},{9,10},{10,... | collective-permute-start | bytes 3080 | tf_op jit(solution)/shard_map/ppermute | solution.py:220
  20.7 0.3 %collective-permute-start.8 = (f32[8,32]{1,0:T(8,128)S(1)}, f32[8,32]{1,0:T(8,128)S(1)}, u32[]{:S(2)}, u32[]{:S(2)}) collective-permute-start(f32[8,32]{1,0:T(8,128)S(1)} %get-tuple-element.13), channel_id=1, source_target_pairs={{0,1},{1,0},{2,3},{3,2},{4,5},{5,4},{6,7},{7,6},{8,9},{9,8},{10,11... | collective-permute-start | bytes 3080 | tf_op jit(solution)/shard_map/ppermute | solution.py:220
  21.0 0.0 copy-start.1
  21.0 0.0 copy-start
  21.0 1.5 %collective-permute-done.6 = f32[8,32]{1,0:T(8,128)S(1)} collective-permute-done((f32[8,32]{1,0:T(8,128)S(1)}, f32[8,32]{1,0:T(8,128)S(1)}, u32[]{:S(2)}, u32[]{:S(2)}) %collective-permute-start.6) | collective-permute-done | bytes 1056 | tf_op jit(solution)/shard_map/ppermute | solution.py:220
  22.4 0.0 collective-permute-done.7
  22.4 0.0 collective-permute-done.8
  22.5 0.0 copy-done.2
  22.5 0.0 copy-done.1
  22.5 0.0 copy-done
  22.5 0.7 %multiply_add_fusion = (f32[32,192]{1,0:T(8,128)}, f32[32,192]{1,0:T(8,128)}, f32[32,192]{1,0:T(8,128)}) fusion(f32[32,192]{1,0:T(8,128)S(1)} %copy-done, f32[32]{0:T(128)S(1)} %get-tuple-element.21, f32[32,192]{1,0:T(8,128)S(1)} %copy-done.1, f32[32,64]{1,0:T(8,128)S(1)} %slice.21, f32[32,128]{1,0:T(8,128)S(1)} %slice.20, f32[32]{0:T(128)S(1)} %get-tuple-element.22, ...), kind=kLoop, calls=%fused_computation.4 | loop fusion | flops 55296 | bytes 172288 | tf_op jit(solution)/shard_map/add | solution.py:283
  (7 shorter events, 0.1 us)
Async XLA Ops:
  1.5 6.7 %collective-permute-start = (bf16[1,192,128]{2,1,0:T(8,128)(2,1)S(1)}, bf16[1,192,128]{2,1,0:T(8,128)(2,1)S(1)}, u32[]{:S(2)}, u32[]{:S(2)}) collective-permute-start(bf16[1,192,128]{2,1,0:T(8,128)(2,1)S(1)} %shard_map.67), channel_id=1, source_target_pairs={{0,8},{1,9},{2,10},{3,11},{4,12},{5,13},{6,14},{7,15},{8,0},{9,1},... | collective-permute-start | bytes 147464 | tf_op jit(solution)/shard_map/ppermute | solution.py:220
  8.3 5.4 %collective-permute-start.1 = (bf16[2,192,128]{2,1,0:T(8,128)(2,1)S(1)}, bf16[2,192,128]{2,1,0:T(8,128)(2,1)S(1)}, u32[]{:S(2)}, u32[]{:S(2)}) collective-permute-start(bf16[2,192,128]{2,1,0:T(8,128)(2,1)S(1)} %pad_maximum_fusion.packs_ref), channel_id=1, source_target_pairs={{0,4},{1,5},{2,6},{3,7},{4,0},{5,1},{6,2},{7,3},{8,12},{9,13},{10,... | collective-permute-start | bytes 294920 | tf_op jit(solution)/shard_map/ppermute | solution.py:220
  9.7 4.9 %collective-permute-start.2 = (bf16[1,96,384]{2,1,0:T(8,128)(2,1)S(1)}, bf16[1,96,384]{2,1,0:T(8,128)(2,1)S(1)}, u32[]{:S(2)}, u32[]{:S(2)}) collective-permute-start(bf16[1,96,384]{2,1,0:T(8,128)(2,1)S(1)} %get-tuple-element.9), channel_id=1, source_target_pairs={{0,2},{1,3},{2,0},{3,1},{4,6},{5,7},{6,4},{7,5},{8,10},{9,11},{10,... | collective-permute-start | bytes 221192 | tf_op jit(solution)/shard_map/ppermute | solution.py:220
  11.2 5.3 %collective-permute-start.3 = (bf16[1,96,384]{2,1,0:T(8,128)(2,1)S(1)}, bf16[1,96,384]{2,1,0:T(8,128)(2,1)S(1)}, u32[]{:S(2)}, u32[]{:S(2)}) collective-permute-start(bf16[1,96,384]{2,1,0:T(8,128)(2,1)S(1)} %get-tuple-element.9), channel_id=1, source_target_pairs={{0,6},{1,7},{2,4},{3,5},{4,2},{5,3},{6,0},{7,1},{8,14},{9,15},{10,... | collective-permute-start | bytes 221192 | tf_op jit(solution)/shard_map/ppermute | solution.py:220
  13.8 2.7 %collective-permute-start.5 = (bf16[2,96,384]{2,1,0:T(8,128)(2,1)S(1)}, bf16[2,96,384]{2,1,0:T(8,128)(2,1)S(1)}, u32[]{:S(2)}, u32[]{:S(2)}) collective-permute-start(bf16[2,96,384]{2,1,0:T(8,128)(2,1)S(1)} %get-tuple-element.17.own_ref), channel_id=1, source_target_pairs={{0,1},{1,0},{2,3},{3,2},{4,5},{5,4},{6,7},{7,6},{8,9},{9,8},{10,11... | collective-permute-start | bytes 442376 | tf_op jit(solution)/shard_map/ppermute | solution.py:220
  16.5 1.5 %collective-permute-start.4 = (bf16[2,96,384]{2,1,0:T(8,128)(2,1)S(1)}, bf16[2,96,384]{2,1,0:T(8,128)(2,1)S(1)}, u32[]{:S(2)}, u32[]{:S(2)}) collective-permute-start(bf16[2,96,384]{2,1,0:T(8,128)(2,1)S(1)} %shard_map.70.piece_ref), channel_id=1, source_target_pairs={{0,1},{1,0},{2,3},{3,2},{4,5},{5,4},{6,7},{7,6},{8,9},{9,8},{10,11... | collective-permute-start | bytes 442376 | tf_op jit(solution)/shard_map/ppermute | solution.py:220
  18.0 4.5 %copy-start.2 = (f32[32,192]{1,0:T(8,128)S(1)}, f32[32,192]{1,0:T(8,128)}, u32[]{:S(2)}) copy-start(f32[32,192]{1,0:T(8,128)} %param.7) | copy-start | bytes 73732
  18.8 3.6 %collective-permute-start.6 = (f32[8,32]{1,0:T(8,128)S(1)}, f32[8,32]{1,0:T(8,128)S(1)}, u32[]{:S(2)}, u32[]{:S(2)}) collective-permute-start(f32[8,32]{1,0:T(8,128)S(1)} %get-tuple-element.13), channel_id=1, source_target_pairs={{0,2},{1,3},{2,0},{3,1},{4,6},{5,7},{6,4},{7,5},{8,10},{9,11},{10,... | collective-permute-start | bytes 3080 | tf_op jit(solution)/shard_map/ppermute | solution.py:220
  19.4 3.1 %collective-permute-start.7 = (f32[8,32]{1,0:T(8,128)S(1)}, f32[8,32]{1,0:T(8,128)S(1)}, u32[]{:S(2)}, u32[]{:S(2)}) collective-permute-start(f32[8,32]{1,0:T(8,128)S(1)} %get-tuple-element.13), channel_id=1, source_target_pairs={{0,3},{1,2},{2,1},{3,0},{4,7},{5,6},{6,5},{7,4},{8,11},{9,10},{10,... | collective-permute-start | bytes 3080 | tf_op jit(solution)/shard_map/ppermute | solution.py:220
  20.7 1.8 %collective-permute-start.8 = (f32[8,32]{1,0:T(8,128)S(1)}, f32[8,32]{1,0:T(8,128)S(1)}, u32[]{:S(2)}, u32[]{:S(2)}) collective-permute-start(f32[8,32]{1,0:T(8,128)S(1)} %get-tuple-element.13), channel_id=1, source_target_pairs={{0,1},{1,0},{2,3},{3,2},{4,5},{5,4},{6,7},{7,6},{8,9},{9,8},{10,11... | collective-permute-start | bytes 3080 | tf_op jit(solution)/shard_map/ppermute | solution.py:220
  21.0 1.5 %copy-start.1 = (f32[32,192]{1,0:T(8,128)S(1)}, f32[32,192]{1,0:T(8,128)}, u32[]{:S(2)}) copy-start(f32[32,192]{1,0:T(8,128)} %residual_hbm.1) | copy-start | bytes 73732
  21.0 1.5 %copy-start = (f32[32,192]{1,0:T(8,128)S(1)}, f32[32,192]{1,0:T(8,128)}, u32[]{:S(2)}) copy-start(f32[32,192]{1,0:T(8,128)} %direction_hbm.1) | copy-start | bytes 73732

commit v7 on v6

--- a/solution.py
+++ b/solution.py
@@ -221,7 +221,7 @@
 
 
 def make_body(count):
-    far, middle, near, *others, cores = strides(count)
+    far, near, middle, *others, cores = strides(count)
 
     def body(points, direction, residual, solution):
         dim, width = points.shape
@@ -234,14 +234,14 @@
         half, rest = unpack(pair, dim, probes)
         other_half, other_rest = unpack(other, dim, probes)
         own = jnp.concatenate([half, other_half], axis=0)
+        other_beside = swapped(half, count, near | middle)
         beside = swapped(half, count, near)
-        other_beside = swapped(half, count, near | middle)
         crossed = swapped(own, count, cores)
         applied = call(functools.partial(first_fold_kernel, dim), full, (own,), 1)
         beside = call(
             join_kernel,
             jax.ShapeDtypeStruct(own.shape, own.dtype),
-            (beside, other_beside, applied),
+            (other_beside, beside, applied),
         )
         applied = add_fold(own, crossed, applied, dim)
         blocks = [own, beside]

time: 23.4 us -> 22.8 us (0.974)
  waiting for transfers between devices: 7.86 us -> 7.27 us
    ppermute x9, waiting for transfers between devices: 7.86 us -> 7.27 us  [swapped(): return lax.ppermute(array, AXES, [(i, i ^ stride) for i in range(count)])]
  transfers between devices with their start and end apart: 9 -> 9, of which waited for: 4 -> 6; matrix products, arithmetic and copies ran while one was open for 0% -> 0% of each run, Pallas kernels for 9% -> 9%
where the time goes in v7:
time: 22.8 us; the launch traced here: 22.6 us
  starting transfers between devices  9.91 us (43%)
  waiting for transfers between devices  7.27 us (32%)
  Pallas kernels  3.86 us (17%)
  other arithmetic  0.74 us (3%)
  between operations  0.73 us (3%)
    ppermute x9, starting transfers between devices, swapped(): return lax.ppermute(array, AXES, [(i, i ^ stride) for i in range(count)])  9.91 us
    ppermute x9, waiting for transfers between devices, swapped(): return lax.ppermute(array, AXES, [(i, i ^ stride) for i in range(count)])  7.27 us
    pallas_call x6, Pallas kernels, call(): pl.pallas_call(kernel, out_shape=outs, in_specs=[in_vmem()] * len(args),...  2.97 us
    pallas_call x1, Pallas kernels, pack(): pl.pallas_call(pack_kernel, out_shape=shape, in_specs=[pl.BlockSpec(memor...  0.89 us
    add x1, other arithmetic, body(): residual_next + (new_norm / (old_norm + 1e-06))[:, None] * direction  0.71 us
  transfers between devices with their start and end apart: 9, of which 6 were waited for; matrix products, arithmetic and copies ran while one was open for 0% of the time, Pallas kernels for 9%

profile of v7, /device:TPU:0, one launch (start us, length us, event | category | flops | bytes accessed | tf_op | source)
XLA Modules:
  0.0 22.6 jit_solution(10998792033342039273)
XLA Ops:
  0.6 0.9 %shard_map.67 = bf16[1,192,128]{2,1,0:T(8,128)(2,1)S(1)} custom-call(bf16[64,192]{1,0:T(8,128)(2,1)} %points_hbm.1, f32[32,192]{1,0:T(8,128)} %direction_hbm.1, f32[32,192]{1,0:T(8,128)} %residual_hbm.1), custom_call_target="tpu_custom_call" | custom-call | tf_op jit(solution)/shard_map/pallas_call | solution.py:172
  1.5 4.1 %collective-permute-start = (bf16[1,192,128]{2,1,0:T(8,128)(2,1)S(1)}, bf16[1,192,128]{2,1,0:T(8,128)(2,1)S(1)}, u32[]{:S(2)}, u32[]{:S(2)}) collective-permute-start(bf16[1,192,128]{2,1,0:T(8,128)(2,1)S(1)} %shard_map.67), channel_id=1, source_target_pairs={{0,8},{1,9},{2,10},{3,11},{4,12},{5,13},{6,14},{7,15},{8,0},{9,1},... | collective-permute-start | bytes 147464 | tf_op jit(solution)/shard_map/ppermute | solution.py:220
  5.6 2.6 %collective-permute-done = bf16[1,192,128]{2,1,0:T(8,128)(2,1)S(1)} collective-permute-done((bf16[1,192,128]{2,1,0:T(8,128)(2,1)S(1)}, bf16[1,192,128]{2,1,0:T(8,128)(2,1)S(1)}, u32[]{:S(2)}, u32[]{:S(2)}) %collective-permute-start) | collective-permute-done | bytes 49184 | tf_op jit(solution)/shard_map/ppermute | solution.py:220
  8.2 0.1 shard_map.68
  8.3 1.7 %collective-permute-start.1 = (bf16[2,192,128]{2,1,0:T(8,128)(2,1)S(1)}, bf16[2,192,128]{2,1,0:T(8,128)(2,1)S(1)}, u32[]{:S(2)}, u32[]{:S(2)}) collective-permute-start(bf16[2,192,128]{2,1,0:T(8,128)(2,1)S(1)} %pad_maximum_fusion.packs_ref), channel_id=1, source_target_pairs={{0,2},{1,3},{2,0},{3,1},{4,6},{5,7},{6,4},{7,5},{8,10},{9,11},{10,... | collective-permute-start | bytes 294920 | tf_op jit(solution)/shard_map/ppermute | solution.py:220
  10.0 1.1 %collective-permute-start.2 = (bf16[1,96,384]{2,1,0:T(8,128)(2,1)S(1)}, bf16[1,96,384]{2,1,0:T(8,128)(2,1)S(1)}, u32[]{:S(2)}, u32[]{:S(2)}) collective-permute-start(bf16[1,96,384]{2,1,0:T(8,128)(2,1)S(1)} %get-tuple-element.9), channel_id=1, source_target_pairs={{0,6},{1,7},{2,4},{3,5},{4,2},{5,3},{6,0},{7,1},{8,14},{9,15},{10,... | collective-permute-start | bytes 221192 | tf_op jit(solution)/shard_map/ppermute | solution.py:220
  11.2 0.6 %collective-permute-start.3 = (bf16[1,96,384]{2,1,0:T(8,128)(2,1)S(1)}, bf16[1,96,384]{2,1,0:T(8,128)(2,1)S(1)}, u32[]{:S(2)}, u32[]{:S(2)}) collective-permute-start(bf16[1,96,384]{2,1,0:T(8,128)(2,1)S(1)} %get-tuple-element.9), channel_id=1, source_target_pairs={{0,4},{1,5},{2,6},{3,7},{4,0},{5,1},{6,2},{7,3},{8,12},{9,13},{10,... | collective-permute-start | bytes 221192 | tf_op jit(solution)/shard_map/ppermute | solution.py:220
  11.9 1.5 %collective-permute-done.1 = bf16[2,192,128]{2,1,0:T(8,128)(2,1)S(1)} collective-permute-done((bf16[2,192,128]{2,1,0:T(8,128)(2,1)S(1)}, bf16[2,192,128]{2,1,0:T(8,128)(2,1)S(1)}, u32[]{:S(2)}, u32[]{:S(2)}) %collective-permute-start.1) | collective-permute-done | bytes 98336 | tf_op jit(solution)/shard_map/ppermute | solution.py:220
  13.4 0.1 shard_map.74
  13.5 0.1 collective-permute-start.5
  13.5 0.7 %shard_map.69.after_ref.before_ref = f32[32,768]{1,0:T(8,128)S(1)} custom-call(bf16[2,96,384]{2,1,0:T(8,128)(2,1)S(1)} %get-tuple-element.17.own_ref), custom_call_target="tpu_custom_call" | custom-call | flops 132120576 | bytes 589824 | tf_op jit(solution)/shard_map/pallas_call | solution.py:158
  14.2 1.1 %collective-permute-done.2.first_ref = bf16[1,96,384]{2,1,0:T(8,128)(2,1)S(1)} collective-permute-done((bf16[1,96,384]{2,1,0:T(8,128)(2,1)S(1)}, bf16[1,96,384]{2,1,0:T(8,128)(2,1)S(1)}, u32[]{:S(2)}, u32[]{:S(2)}) %collective-permute-start.2) | collective-permute-done | bytes 73760 | tf_op jit(solution)/shard_map/ppermute | solution.py:220
  15.3 0.2 %collective-permute-done.3.second_ref = bf16[1,96,384]{2,1,0:T(8,128)(2,1)S(1)} collective-permute-done((bf16[1,96,384]{2,1,0:T(8,128)(2,1)S(1)}, bf16[1,96,384]{2,1,0:T(8,128)(2,1)S(1)}, u32[]{:S(2)}, u32[]{:S(2)}) %collective-permute-start.3) | collective-permute-done | bytes 73760 | tf_op jit(solution)/shard_map/ppermute | solution.py:220
  15.6 0.1 collective-permute-start.4
  15.6 0.0 collective-permute-done.5.piece_ref
  15.7 0.7 %shard_map.71.before_ref = f32[32,768]{1,0:T(8,128)S(1)} custom-call(bf16[2,96,384]{2,1,0:T(8,128)(2,1)S(1)} %get-tuple-element.17.own_ref, bf16[2,96,384]{2,1,0:T(8,128)(2,1)S(1)} %collective-permute-done.5.piece_ref, f32[32,768]{1,0:T(8,128)S(1)} %shard_map.69.after_ref.before_ref), custom_call_target="tpu_custom_call" | custom-call | flops 132120576 | bytes 589824 | tf_op jit(solution)/shard_map/pallas_call | solution.py:158
  16.3 0.7 %shard_map.72.before_ref = f32[32,768]{1,0:T(8,128)S(1)} custom-call(bf16[2,96,384]{2,1,0:T(8,128)(2,1)S(1)} %get-tuple-element.17.own_ref, bf16[2,96,384]{2,1,0:T(8,128)(2,1)S(1)} %shard_map.70.piece_ref, f32[32,768]{1,0:T(8,128)S(1)} %shard_map.71.before_ref), custom_call_target="tpu_custom_call" | custom-call | flops 132120576 | bytes 589824 | tf_op jit(solution)/shard_map/pallas_call | solution.py:158
  17.0 0.0 collective-permute-done.4.piece_ref
  17.0 0.0 copy-start.2
  17.1 0.8 %shard_map.73 = (f32[32,768]{1,0:T(8,128)S(1)}, f32[8,32]{1,0:T(8,128)S(1)}) custom-call(bf16[2,96,384]{2,1,0:T(8,128)(2,1)S(1)} %get-tuple-element.17.own_ref, bf16[2,96,384]{2,1,0:T(8,128)(2,1)S(1)} %collective-permute-done.4.piece_ref, f32[32,768]{1,0:T(8,128)S(1)} %shard_map.72.before_ref, f32[32,384]{1,0:T(8,128)S(1)} %get-tuple-element.11.residual_ref, ...), custom_call_target="tpu_custom_call" | custom-call | flops 132120576 | bytes 589824 | tf_op jit(solution)/shard_map/pallas_call | solution.py:158
  17.9 0.9 %collective-permute-start.6 = (f32[8,32]{1,0:T(8,128)S(1)}, f32[8,32]{1,0:T(8,128)S(1)}, u32[]{:S(2)}, u32[]{:S(2)}) collective-permute-start(f32[8,32]{1,0:T(8,128)S(1)} %get-tuple-element.13), channel_id=1, source_target_pairs={{0,4},{1,5},{2,6},{3,7},{4,0},{5,1},{6,2},{7,3},{8,12},{9,13},{10,... | collective-permute-start | bytes 3080 | tf_op jit(solution)/shard_map/ppermute | solution.py:220
  18.8 0.9 %collective-permute-start.7 = (f32[8,32]{1,0:T(8,128)S(1)}, f32[8,32]{1,0:T(8,128)S(1)}, u32[]{:S(2)}, u32[]{:S(2)}) collective-permute-start(f32[8,32]{1,0:T(8,128)S(1)} %get-tuple-element.13), channel_id=1, source_target_pairs={{0,5},{1,4},{2,7},{3,6},{4,1},{5,0},{6,3},{7,2},{8,13},{9,12},{10,... | collective-permute-start | bytes 3080 | tf_op jit(solution)/shard_map/ppermute | solution.py:220
  19.7 0.3 %collective-permute-start.8 = (f32[8,32]{1,0:T(8,128)S(1)}, f32[8,32]{1,0:T(8,128)S(1)}, u32[]{:S(2)}, u32[]{:S(2)}) collective-permute-start(f32[8,32]{1,0:T(8,128)S(1)} %get-tuple-element.13), channel_id=1, source_target_pairs={{0,1},{1,0},{2,3},{3,2},{4,5},{5,4},{6,7},{7,6},{8,9},{9,8},{10,11... | collective-permute-start | bytes 3080 | tf_op jit(solution)/shard_map/ppermute | solution.py:220
  20.0 0.0 copy-start.1
  20.0 0.0 copy-start
  20.0 1.5 %collective-permute-done.6 = f32[8,32]{1,0:T(8,128)S(1)} collective-permute-done((f32[8,32]{1,0:T(8,128)S(1)}, f32[8,32]{1,0:T(8,128)S(1)}, u32[]{:S(2)}, u32[]{:S(2)}) %collective-permute-start.6) | collective-permute-done | bytes 1056 | tf_op jit(solution)/shard_map/ppermute | solution.py:220
  21.5 0.4 %collective-permute-done.7 = f32[8,32]{1,0:T(8,128)S(1)} collective-permute-done((f32[8,32]{1,0:T(8,128)S(1)}, f32[8,32]{1,0:T(8,128)S(1)}, u32[]{:S(2)}, u32[]{:S(2)}) %collective-permute-start.7) | collective-permute-done | bytes 1056 | tf_op jit(solution)/shard_map/ppermute | solution.py:220
  21.9 0.0 collective-permute-done.8
  21.9 0.0 copy-done.2
  21.9 0.0 copy-done.1
  21.9 0.0 copy-done
  21.9 0.7 %multiply_add_fusion = (f32[32,192]{1,0:T(8,128)}, f32[32,192]{1,0:T(8,128)}, f32[32,192]{1,0:T(8,128)}) fusion(f32[32,192]{1,0:T(8,128)S(1)} %copy-done, f32[32]{0:T(128)S(1)} %get-tuple-element.21, f32[32,192]{1,0:T(8,128)S(1)} %copy-done.1, f32[32,64]{1,0:T(8,128)S(1)} %slice.21, f32[32,128]{1,0:T(8,128)S(1)} %slice.20, f32[32]{0:T(128)S(1)} %get-tuple-element.22, ...), kind=kLoop, calls=%fused_computation.4 | loop fusion | flops 55296 | bytes 172288 | tf_op jit(solution)/shard_map/add | solution.py:283
  (7 shorter events, 0.1 us)
Async XLA Ops:
  1.5 6.7 %collective-permute-start = (bf16[1,192,128]{2,1,0:T(8,128)(2,1)S(1)}, bf16[1,192,128]{2,1,0:T(8,128)(2,1)S(1)}, u32[]{:S(2)}, u32[]{:S(2)}) collective-permute-start(bf16[1,192,128]{2,1,0:T(8,128)(2,1)S(1)} %shard_map.67), channel_id=1, source_target_pairs={{0,8},{1,9},{2,10},{3,11},{4,12},{5,13},{6,14},{7,15},{8,0},{9,1},... | collective-permute-start | bytes 147464 | tf_op jit(solution)/shard_map/ppermute | solution.py:220
  8.3 5.1 %collective-permute-start.1 = (bf16[2,192,128]{2,1,0:T(8,128)(2,1)S(1)}, bf16[2,192,128]{2,1,0:T(8,128)(2,1)S(1)}, u32[]{:S(2)}, u32[]{:S(2)}) collective-permute-start(bf16[2,192,128]{2,1,0:T(8,128)(2,1)S(1)} %pad_maximum_fusion.packs_ref), channel_id=1, source_target_pairs={{0,2},{1,3},{2,0},{3,1},{4,6},{5,7},{6,4},{7,5},{8,10},{9,11},{10,... | collective-permute-start | bytes 294920 | tf_op jit(solution)/shard_map/ppermute | solution.py:220
  10.0 5.3 %collective-permute-start.2 = (bf16[1,96,384]{2,1,0:T(8,128)(2,1)S(1)}, bf16[1,96,384]{2,1,0:T(8,128)(2,1)S(1)}, u32[]{:S(2)}, u32[]{:S(2)}) collective-permute-start(bf16[1,96,384]{2,1,0:T(8,128)(2,1)S(1)} %get-tuple-element.9), channel_id=1, source_target_pairs={{0,6},{1,7},{2,4},{3,5},{4,2},{5,3},{6,0},{7,1},{8,14},{9,15},{10,... | collective-permute-start | bytes 221192 | tf_op jit(solution)/shard_map/ppermute | solution.py:220
  11.2 4.4 %collective-permute-start.3 = (bf16[1,96,384]{2,1,0:T(8,128)(2,1)S(1)}, bf16[1,96,384]{2,1,0:T(8,128)(2,1)S(1)}, u32[]{:S(2)}, u32[]{:S(2)}) collective-permute-start(bf16[1,96,384]{2,1,0:T(8,128)(2,1)S(1)} %get-tuple-element.9), channel_id=1, source_target_pairs={{0,4},{1,5},{2,6},{3,7},{4,0},{5,1},{6,2},{7,3},{8,12},{9,13},{10,... | collective-permute-start | bytes 221192 | tf_op jit(solution)/shard_map/ppermute | solution.py:220
  13.5 2.2 %collective-permute-start.5 = (bf16[2,96,384]{2,1,0:T(8,128)(2,1)S(1)}, bf16[2,96,384]{2,1,0:T(8,128)(2,1)S(1)}, u32[]{:S(2)}, u32[]{:S(2)}) collective-permute-start(bf16[2,96,384]{2,1,0:T(8,128)(2,1)S(1)} %get-tuple-element.17.own_ref), channel_id=1, source_target_pairs={{0,1},{1,0},{2,3},{3,2},{4,5},{5,4},{6,7},{7,6},{8,9},{9,8},{10,11... | collective-permute-start | bytes 442376 | tf_op jit(solution)/shard_map/ppermute | solution.py:220
  15.6 1.5 %collective-permute-start.4 = (bf16[2,96,384]{2,1,0:T(8,128)(2,1)S(1)}, bf16[2,96,384]{2,1,0:T(8,128)(2,1)S(1)}, u32[]{:S(2)}, u32[]{:S(2)}) collective-permute-start(bf16[2,96,384]{2,1,0:T(8,128)(2,1)S(1)} %shard_map.70.piece_ref), channel_id=1, source_target_pairs={{0,1},{1,0},{2,3},{3,2},{4,5},{5,4},{6,7},{7,6},{8,9},{9,8},{10,11... | collective-permute-start | bytes 442376 | tf_op jit(solution)/shard_map/ppermute | solution.py:220
  17.0 4.9 %copy-start.2 = (f32[32,192]{1,0:T(8,128)S(1)}, f32[32,192]{1,0:T(8,128)}, u32[]{:S(2)}) copy-start(f32[32,192]{1,0:T(8,128)} %param.7) | copy-start | bytes 73732
  17.9 3.6 %collective-permute-start.6 = (f32[8,32]{1,0:T(8,128)S(1)}, f32[8,32]{1,0:T(8,128)S(1)}, u32[]{:S(2)}, u32[]{:S(2)}) collective-permute-start(f32[8,32]{1,0:T(8,128)S(1)} %get-tuple-element.13), channel_id=1, source_target_pairs={{0,4},{1,5},{2,6},{3,7},{4,0},{5,1},{6,2},{7,3},{8,12},{9,13},{10,... | collective-permute-start | bytes 3080 | tf_op jit(solution)/shard_map/ppermute | solution.py:220
  18.8 3.0 %collective-permute-start.7 = (f32[8,32]{1,0:T(8,128)S(1)}, f32[8,32]{1,0:T(8,128)S(1)}, u32[]{:S(2)}, u32[]{:S(2)}) collective-permute-start(f32[8,32]{1,0:T(8,128)S(1)} %get-tuple-element.13), channel_id=1, source_target_pairs={{0,5},{1,4},{2,7},{3,6},{4,1},{5,0},{6,3},{7,2},{8,13},{9,12},{10,... | collective-permute-start | bytes 3080 | tf_op jit(solution)/shard_map/ppermute | solution.py:220
  19.7 2.1 %collective-permute-start.8 = (f32[8,32]{1,0:T(8,128)S(1)}, f32[8,32]{1,0:T(8,128)S(1)}, u32[]{:S(2)}, u32[]{:S(2)}) collective-permute-start(f32[8,32]{1,0:T(8,128)S(1)} %get-tuple-element.13), channel_id=1, source_target_pairs={{0,1},{1,0},{2,3},{3,2},{4,5},{5,4},{6,7},{7,6},{8,9},{9,8},{10,11... | collective-permute-start | bytes 3080 | tf_op jit(solution)/shard_map/ppermute | solution.py:220
  20.0 1.9 %copy-start.1 = (f32[32,192]{1,0:T(8,128)S(1)}, f32[32,192]{1,0:T(8,128)}, u32[]{:S(2)}) copy-start(f32[32,192]{1,0:T(8,128)} %residual_hbm.1) | copy-start | bytes 73732
  20.0 1.9 %copy-start = (f32[32,192]{1,0:T(8,128)S(1)}, f32[32,192]{1,0:T(8,128)}, u32[]{:S(2)}) copy-start(f32[32,192]{1,0:T(8,128)} %direction_hbm.1) | copy-start | bytes 73732

commit v8 on v7

--- a/solution.py
+++ b/solution.py
@@ -113,6 +113,12 @@
 
 def fold_kernel(dim, own_ref, piece_ref, before_ref, applied_ref):
     applied_ref[...] = fold(read(own_ref), read(piece_ref), before_ref[...], dim)
+
+
+def two_folds_kernel(dim, own_ref, first_ref, second_ref, before_ref, applied_ref):
+    own = read(own_ref)
+    applied = fold(own, read(first_ref), before_ref[...], dim)
+    applied_ref[...] = fold(own, read(second_ref), applied, dim)
 
 
 def join_kernel(first_ref, second_ref, after_ref, joined_ref):
@@ -243,13 +249,16 @@
             jax.ShapeDtypeStruct(own.shape, own.dtype),
             (other_beside, beside, applied),
         )
-        applied = add_fold(own, crossed, applied, dim)
+        applied = call(
+            functools.partial(two_folds_kernel, dim), full, (own, crossed, beside, applied), 2
+        )
         blocks = [own, beside]
         for stride in others:
             blocks.append(swapped(jnp.concatenate(blocks, axis=0), count, stride))
         for block in blocks[1:]:
             crossed = swapped(block, count, cores)
-            applied = add_fold(own, block, applied, dim)
+            if block is not beside:
+                applied = add_fold(own, block, applied, dim)
             if block is not blocks[-1]:
                 applied = add_fold(own, crossed, applied, dim)
         if crossed.shape[0] == 2:

time: 22.8 us -> 22.8 us (level)
    pallas_call x6 -> x5, Pallas kernels: 2.97 us -> 2.86 us  [call(): pl.pallas_call(kernel, out_shape=outs, in_specs=[in_vmem()] * len(args),...]
  transfers between devices with their start and end apart: 9 -> 9, of which waited for: 6 -> 7; matrix products, arithmetic and copies ran while one was open for 0% -> 0% of each run, Pallas kernels for 9% -> 9%
where the time goes in v8:
time: 22.8 us; the launch traced here: 22.6 us
  starting transfers between devices  9.91 us (43%)
  waiting for transfers between devices  7.35 us (32%)
  Pallas kernels  3.75 us (16%)
  other arithmetic  0.74 us (3%)
  between operations  0.72 us (3%)
    ppermute x9, starting transfers between devices, swapped(): return lax.ppermute(array, AXES, [(i, i ^ stride) for i in range(count)])  9.91 us
    ppermute x9, waiting for transfers between devices, swapped(): return lax.ppermute(array, AXES, [(i, i ^ stride) for i in range(count)])  7.35 us
    pallas_call x5, Pallas kernels, call(): pl.pallas_call(kernel, out_shape=outs, in_specs=[in_vmem()] * len(args),...  2.86 us
    pallas_call x1, Pallas kernels, pack(): pl.pallas_call(pack_kernel, out_shape=shape, in_specs=[pl.BlockSpec(memor...  0.89 us
    add x1, other arithmetic, body(): residual_next + (new_norm / (old_norm + 1e-06))[:, None] * direction  0.71 us
  transfers between devices with their start and end apart: 9, of which 7 were waited for; matrix products, arithmetic and copies ran while one was open for 0% of the time, Pallas kernels for 9%

profile of v8, /device:TPU:0, one launch (start us, length us, event | category | flops | bytes accessed | tf_op | source)
XLA Modules:
  0.0 22.6 jit_solution(13337181767568155501)
XLA Ops:
  0.6 0.9 %shard_map.67 = bf16[1,192,128]{2,1,0:T(8,128)(2,1)S(1)} custom-call(bf16[64,192]{1,0:T(8,128)(2,1)} %points_hbm.1, f32[32,192]{1,0:T(8,128)} %direction_hbm.1, f32[32,192]{1,0:T(8,128)} %residual_hbm.1), custom_call_target="tpu_custom_call" | custom-call | tf_op jit(solution)/shard_map/pallas_call | solution.py:178
  1.5 4.1 %collective-permute-start = (bf16[1,192,128]{2,1,0:T(8,128)(2,1)S(1)}, bf16[1,192,128]{2,1,0:T(8,128)(2,1)S(1)}, u32[]{:S(2)}, u32[]{:S(2)}) collective-permute-start(bf16[1,192,128]{2,1,0:T(8,128)(2,1)S(1)} %shard_map.67), channel_id=1, source_target_pairs={{0,8},{1,9},{2,10},{3,11},{4,12},{5,13},{6,14},{7,15},{8,0},{9,1},... | collective-permute-start | bytes 147464 | tf_op jit(solution)/shard_map/ppermute | solution.py:226
  5.6 2.6 %collective-permute-done = bf16[1,192,128]{2,1,0:T(8,128)(2,1)S(1)} collective-permute-done((bf16[1,192,128]{2,1,0:T(8,128)(2,1)S(1)}, bf16[1,192,128]{2,1,0:T(8,128)(2,1)S(1)}, u32[]{:S(2)}, u32[]{:S(2)}) %collective-permute-start) | collective-permute-done | bytes 49184 | tf_op jit(solution)/shard_map/ppermute | solution.py:226
  8.2 0.1 shard_map.68
  8.3 1.7 %collective-permute-start.1 = (bf16[2,192,128]{2,1,0:T(8,128)(2,1)S(1)}, bf16[2,192,128]{2,1,0:T(8,128)(2,1)S(1)}, u32[]{:S(2)}, u32[]{:S(2)}) collective-permute-start(bf16[2,192,128]{2,1,0:T(8,128)(2,1)S(1)} %pad_maximum_fusion.packs_ref), channel_id=1, source_target_pairs={{0,2},{1,3},{2,0},{3,1},{4,6},{5,7},{6,4},{7,5},{8,10},{9,11},{10,... | collective-permute-start | bytes 294920 | tf_op jit(solution)/shard_map/ppermute | solution.py:226
  10.0 1.1 %collective-permute-start.2 = (bf16[1,96,384]{2,1,0:T(8,128)(2,1)S(1)}, bf16[1,96,384]{2,1,0:T(8,128)(2,1)S(1)}, u32[]{:S(2)}, u32[]{:S(2)}) collective-permute-start(bf16[1,96,384]{2,1,0:T(8,128)(2,1)S(1)} %get-tuple-element.9), channel_id=1, source_target_pairs={{0,6},{1,7},{2,4},{3,5},{4,2},{5,3},{6,0},{7,1},{8,14},{9,15},{10,... | collective-permute-start | bytes 221192 | tf_op jit(solution)/shard_map/ppermute | solution.py:226
  11.2 0.6 %collective-permute-start.3 = (bf16[1,96,384]{2,1,0:T(8,128)(2,1)S(1)}, bf16[1,96,384]{2,1,0:T(8,128)(2,1)S(1)}, u32[]{:S(2)}, u32[]{:S(2)}) collective-permute-start(bf16[1,96,384]{2,1,0:T(8,128)(2,1)S(1)} %get-tuple-element.9), channel_id=1, source_target_pairs={{0,4},{1,5},{2,6},{3,7},{4,0},{5,1},{6,2},{7,3},{8,12},{9,13},{10,... | collective-permute-start | bytes 221192 | tf_op jit(solution)/shard_map/ppermute | solution.py:226
  11.9 1.5 %collective-permute-done.1 = bf16[2,192,128]{2,1,0:T(8,128)(2,1)S(1)} collective-permute-done((bf16[2,192,128]{2,1,0:T(8,128)(2,1)S(1)}, bf16[2,192,128]{2,1,0:T(8,128)(2,1)S(1)}, u32[]{:S(2)}, u32[]{:S(2)}) %collective-permute-start.1) | collective-permute-done | bytes 98336 | tf_op jit(solution)/shard_map/ppermute | solution.py:226
  13.4 0.1 shard_map.73
  13.5 0.1 collective-permute-start.5
  13.5 0.7 %shard_map.69.after_ref.before_ref = f32[32,768]{1,0:T(8,128)S(1)} custom-call(bf16[2,96,384]{2,1,0:T(8,128)(2,1)S(1)} %get-tuple-element.17.own_ref), custom_call_target="tpu_custom_call" | custom-call | flops 132120576 | bytes 589824 | tf_op jit(solution)/shard_map/pallas_call | solution.py:164
  14.2 1.1 %collective-permute-done.2.first_ref = bf16[1,96,384]{2,1,0:T(8,128)(2,1)S(1)} collective-permute-done((bf16[1,96,384]{2,1,0:T(8,128)(2,1)S(1)}, bf16[1,96,384]{2,1,0:T(8,128)(2,1)S(1)}, u32[]{:S(2)}, u32[]{:S(2)}) %collective-permute-start.2) | collective-permute-done | bytes 73760 | tf_op jit(solution)/shard_map/ppermute | solution.py:226
  15.3 0.2 %collective-permute-done.3.second_ref = bf16[1,96,384]{2,1,0:T(8,128)(2,1)S(1)} collective-permute-done((bf16[1,96,384]{2,1,0:T(8,128)(2,1)S(1)}, bf16[1,96,384]{2,1,0:T(8,128)(2,1)S(1)}, u32[]{:S(2)}, u32[]{:S(2)}) %collective-permute-start.3) | collective-permute-done | bytes 73760 | tf_op jit(solution)/shard_map/ppermute | solution.py:226
  15.6 0.1 collective-permute-start.4
  15.6 0.0 collective-permute-done.5.first_ref
  15.7 1.3 %shard_map.71.before_ref = f32[32,768]{1,0:T(8,128)S(1)} custom-call(bf16[2,96,384]{2,1,0:T(8,128)(2,1)S(1)} %get-tuple-element.17.own_ref, bf16[2,96,384]{2,1,0:T(8,128)(2,1)S(1)} %collective-permute-done.5.first_ref, bf16[2,96,384]{2,1,0:T(8,128)(2,1)S(1)} %shard_map.70.second_ref, f32[32,768]{1,0:T(8,128)S(1)} %shard_map.69.after_ref.before_ref), custom_call_target="tpu_custom_call" | custom-call | flops 264241152 | bytes 1179648 | tf_op jit(solution)/shard_map/pallas_call | solution.py:164
  16.9 0.1 collective-permute-done.4.piece_ref
  17.0 0.0 copy-start.2
  17.0 0.8 %shard_map.72 = (f32[32,768]{1,0:T(8,128)S(1)}, f32[8,32]{1,0:T(8,128)S(1)}) custom-call(bf16[2,96,384]{2,1,0:T(8,128)(2,1)S(1)} %get-tuple-element.17.own_ref, bf16[2,96,384]{2,1,0:T(8,128)(2,1)S(1)} %collective-permute-done.4.piece_ref, f32[32,768]{1,0:T(8,128)S(1)} %shard_map.71.before_ref, f32[32,384]{1,0:T(8,128)S(1)} %get-tuple-element.11.residual_ref, ...), custom_call_target="tpu_custom_call" | custom-call | flops 132120576 | bytes 589824 | tf_op jit(solution)/shard_map/pallas_call | solution.py:164
  17.8 0.9 %collective-permute-start.6 = (f32[8,32]{1,0:T(8,128)S(1)}, f32[8,32]{1,0:T(8,128)S(1)}, u32[]{:S(2)}, u32[]{:S(2)}) collective-permute-start(f32[8,32]{1,0:T(8,128)S(1)} %get-tuple-element.13), channel_id=1, source_target_pairs={{0,4},{1,5},{2,6},{3,7},{4,0},{5,1},{6,2},{7,3},{8,12},{9,13},{10,... | collective-permute-start | bytes 3080 | tf_op jit(solution)/shard_map/ppermute | solution.py:226
  18.8 0.9 %collective-permute-start.7 = (f32[8,32]{1,0:T(8,128)S(1)}, f32[8,32]{1,0:T(8,128)S(1)}, u32[]{:S(2)}, u32[]{:S(2)}) collective-permute-start(f32[8,32]{1,0:T(8,128)S(1)} %get-tuple-element.13), channel_id=1, source_target_pairs={{0,5},{1,4},{2,7},{3,6},{4,1},{5,0},{6,3},{7,2},{8,13},{9,12},{10,... | collective-permute-start | bytes 3080 | tf_op jit(solution)/shard_map/ppermute | solution.py:226
  19.6 0.4 %collective-permute-start.8 = (f32[8,32]{1,0:T(8,128)S(1)}, f32[8,32]{1,0:T(8,128)S(1)}, u32[]{:S(2)}, u32[]{:S(2)}) collective-permute-start(f32[8,32]{1,0:T(8,128)S(1)} %get-tuple-element.13), channel_id=1, source_target_pairs={{0,1},{1,0},{2,3},{3,2},{4,5},{5,4},{6,7},{7,6},{8,9},{9,8},{10,11... | collective-permute-start | bytes 3080 | tf_op jit(solution)/shard_map/ppermute | solution.py:226
  20.0 0.0 copy-start.1
  20.0 0.0 copy-start
  20.0 1.5 %collective-permute-done.6 = f32[8,32]{1,0:T(8,128)S(1)} collective-permute-done((f32[8,32]{1,0:T(8,128)S(1)}, f32[8,32]{1,0:T(8,128)S(1)}, u32[]{:S(2)}, u32[]{:S(2)}) %collective-permute-start.6) | collective-permute-done | bytes 1056 | tf_op jit(solution)/shard_map/ppermute | solution.py:226
  21.5 0.4 %collective-permute-done.7 = f32[8,32]{1,0:T(8,128)S(1)} collective-permute-done((f32[8,32]{1,0:T(8,128)S(1)}, f32[8,32]{1,0:T(8,128)S(1)}, u32[]{:S(2)}, u32[]{:S(2)}) %collective-permute-start.7) | collective-permute-done | bytes 1056 | tf_op jit(solution)/shard_map/ppermute | solution.py:226
  21.8 0.0 collective-permute-done.8
  21.8 0.0 copy-done.2
  21.8 0.0 copy-done.1
  21.9 0.0 copy-done
  21.9 0.7 %multiply_add_fusion = (f32[32,192]{1,0:T(8,128)}, f32[32,192]{1,0:T(8,128)}, f32[32,192]{1,0:T(8,128)}) fusion(f32[32,192]{1,0:T(8,128)S(1)} %copy-done, f32[32]{0:T(128)S(1)} %get-tuple-element.21, f32[32,192]{1,0:T(8,128)S(1)} %copy-done.1, f32[32,64]{1,0:T(8,128)S(1)} %slice.21, f32[32,128]{1,0:T(8,128)S(1)} %slice.20, f32[32]{0:T(128)S(1)} %get-tuple-element.22, ...), kind=kLoop, calls=%fused_computation.4 | loop fusion | flops 55296 | bytes 172288 | tf_op jit(solution)/shard_map/add | solution.py:292
  (7 shorter events, 0.1 us)
Async XLA Ops:
  1.5 6.7 %collective-permute-start = (bf16[1,192,128]{2,1,0:T(8,128)(2,1)S(1)}, bf16[1,192,128]{2,1,0:T(8,128)(2,1)S(1)}, u32[]{:S(2)}, u32[]{:S(2)}) collective-permute-start(bf16[1,192,128]{2,1,0:T(8,128)(2,1)S(1)} %shard_map.67), channel_id=1, source_target_pairs={{0,8},{1,9},{2,10},{3,11},{4,12},{5,13},{6,14},{7,15},{8,0},{9,1},... | collective-permute-start | bytes 147464 | tf_op jit(solution)/shard_map/ppermute | solution.py:226
  8.3 5.1 %collective-permute-start.1 = (bf16[2,192,128]{2,1,0:T(8,128)(2,1)S(1)}, bf16[2,192,128]{2,1,0:T(8,128)(2,1)S(1)}, u32[]{:S(2)}, u32[]{:S(2)}) collective-permute-start(bf16[2,192,128]{2,1,0:T(8,128)(2,1)S(1)} %pad_maximum_fusion.packs_ref), channel_id=1, source_target_pairs={{0,2},{1,3},{2,0},{3,1},{4,6},{5,7},{6,4},{7,5},{8,10},{9,11},{10,... | collective-permute-start | bytes 294920 | tf_op jit(solution)/shard_map/ppermute | solution.py:226
  10.0 5.3 %collective-permute-start.2 = (bf16[1,96,384]{2,1,0:T(8,128)(2,1)S(1)}, bf16[1,96,384]{2,1,0:T(8,128)(2,1)S(1)}, u32[]{:S(2)}, u32[]{:S(2)}) collective-permute-start(bf16[1,96,384]{2,1,0:T(8,128)(2,1)S(1)} %get-tuple-element.9), channel_id=1, source_target_pairs={{0,6},{1,7},{2,4},{3,5},{4,2},{5,3},{6,0},{7,1},{8,14},{9,15},{10,... | collective-permute-start | bytes 221192 | tf_op jit(solution)/shard_map/ppermute | solution.py:226
  11.2 4.4 %collective-permute-start.3 = (bf16[1,96,384]{2,1,0:T(8,128)(2,1)S(1)}, bf16[1,96,384]{2,1,0:T(8,128)(2,1)S(1)}, u32[]{:S(2)}, u32[]{:S(2)}) collective-permute-start(bf16[1,96,384]{2,1,0:T(8,128)(2,1)S(1)} %get-tuple-element.9), channel_id=1, source_target_pairs={{0,4},{1,5},{2,6},{3,7},{4,0},{5,1},{6,2},{7,3},{8,12},{9,13},{10,... | collective-permute-start | bytes 221192 | tf_op jit(solution)/shard_map/ppermute | solution.py:226
  13.5 2.2 %collective-permute-start.5 = (bf16[2,96,384]{2,1,0:T(8,128)(2,1)S(1)}, bf16[2,96,384]{2,1,0:T(8,128)(2,1)S(1)}, u32[]{:S(2)}, u32[]{:S(2)}) collective-permute-start(bf16[2,96,384]{2,1,0:T(8,128)(2,1)S(1)} %get-tuple-element.17.own_ref), channel_id=1, source_target_pairs={{0,1},{1,0},{2,3},{3,2},{4,5},{5,4},{6,7},{7,6},{8,9},{9,8},{10,11... | collective-permute-start | bytes 442376 | tf_op jit(solution)/shard_map/ppermute | solution.py:226
  15.6 1.4 %collective-permute-start.4 = (bf16[2,96,384]{2,1,0:T(8,128)(2,1)S(1)}, bf16[2,96,384]{2,1,0:T(8,128)(2,1)S(1)}, u32[]{:S(2)}, u32[]{:S(2)}) collective-permute-start(bf16[2,96,384]{2,1,0:T(8,128)(2,1)S(1)} %shard_map.70.second_ref), channel_id=1, source_target_pairs={{0,1},{1,0},{2,3},{3,2},{4,5},{5,4},{6,7},{7,6},{8,9},{9,8},{10,11... | collective-permute-start | bytes 442376 | tf_op jit(solution)/shard_map/ppermute | solution.py:226
  17.0 4.8 %copy-start.2 = (f32[32,192]{1,0:T(8,128)S(1)}, f32[32,192]{1,0:T(8,128)}, u32[]{:S(2)}) copy-start(f32[32,192]{1,0:T(8,128)} %param.7) | copy-start | bytes 73732
  17.8 3.6 %collective-permute-start.6 = (f32[8,32]{1,0:T(8,128)S(1)}, f32[8,32]{1,0:T(8,128)S(1)}, u32[]{:S(2)}, u32[]{:S(2)}) collective-permute-start(f32[8,32]{1,0:T(8,128)S(1)} %get-tuple-element.13), channel_id=1, source_target_pairs={{0,4},{1,5},{2,6},{3,7},{4,0},{5,1},{6,2},{7,3},{8,12},{9,13},{10,... | collective-permute-start | bytes 3080 | tf_op jit(solution)/shard_map/ppermute | solution.py:226
  18.8 3.0 %collective-permute-start.7 = (f32[8,32]{1,0:T(8,128)S(1)}, f32[8,32]{1,0:T(8,128)S(1)}, u32[]{:S(2)}, u32[]{:S(2)}) collective-permute-start(f32[8,32]{1,0:T(8,128)S(1)} %get-tuple-element.13), channel_id=1, source_target_pairs={{0,5},{1,4},{2,7},{3,6},{4,1},{5,0},{6,3},{7,2},{8,13},{9,12},{10,... | collective-permute-start | bytes 3080 | tf_op jit(solution)/shard_map/ppermute | solution.py:226
  19.6 2.2 %collective-permute-start.8 = (f32[8,32]{1,0:T(8,128)S(1)}, f32[8,32]{1,0:T(8,128)S(1)}, u32[]{:S(2)}, u32[]{:S(2)}) collective-permute-start(f32[8,32]{1,0:T(8,128)S(1)} %get-tuple-element.13), channel_id=1, source_target_pairs={{0,1},{1,0},{2,3},{3,2},{4,5},{5,4},{6,7},{7,6},{8,9},{9,8},{10,11... | collective-permute-start | bytes 3080 | tf_op jit(solution)/shard_map/ppermute | solution.py:226
  20.0 1.9 %copy-start.1 = (f32[32,192]{1,0:T(8,128)S(1)}, f32[32,192]{1,0:T(8,128)}, u32[]{:S(2)}) copy-start(f32[32,192]{1,0:T(8,128)} %residual_hbm.1) | copy-start | bytes 73732
  20.0 1.9 %copy-start = (f32[32,192]{1,0:T(8,128)S(1)}, f32[32,192]{1,0:T(8,128)}, u32[]{:S(2)}) copy-start(f32[32,192]{1,0:T(8,128)} %direction_hbm.1) | copy-start | bytes 73732
